TPU v7x, 512 devices: a whole 4x4x16 slice. The times are simulated.
512 devices in a mesh: wide: 64 (over y, z), narrow: 8 (over x, core).
Axes of the slice: x: 4, y: 4, z: 16, core: 2. Of those that a mesh axis runs over, the one named last changes fastest.
Arguments:
- right_side: float32 [16, 512, 1024], P(None, 'wide', 'narrow'), may hold values from -8 to 8
- capacity: float32 [16, 512, 1024], P(None, 'wide', 'narrow'), may hold values from 0.1 to 2
- phase: int32 [16, 512, 1024], P(None, 'wide', 'narrow'), may hold values from 0 to 2
- mold_flags: int32 [16, 512, 1024], P(None, 'wide', 'narrow'), may hold values 0 or 1
Outputs:
- adjoint_field: float32 [16, 512, 1024], P(None, 'wide', 'narrow')
- residual: float32 [16, 512, 1024], P(None, 'wide', 'narrow')
All inputs are finite; a program needn't handle non-finite values. No bound on the sum of `mold_flags` on one device may be relied on, other than what follows from the above.
Results may differ from a plain program's by a relative error of at most 0.0003.
Values sent between devices are 32-bit elements; how exact they have to be, the bound alone decides.
No kernel may reach another device: no remote copies, remote signals or barrier semaphores. Data moves between devices by JAX's collectives and lax.ppermute only.
A program may use at most 64 MiB of HBM per device.

v0:
```python
import jax
import jax.numpy as jnp
from jax import lax
from jax.sharding import PartitionSpec as P

LEVELS = 4
COARSE_SWEEPS = 4
ITERS = 2


OMEGA = 0.8


def with_halo(array, sides, width):
    for axis, dim in sides:
        peers, length = (lax.axis_size(axis), array.shape[dim])
        up = [(i, (i + 1) % peers) for i in range(peers - 1)]
        down = [(j, i) for i, j in up]
        last = lax.slice_in_dim(array, length - width, length, axis=dim)
        first = lax.slice_in_dim(array, 0, width, axis=dim)
        before = lax.ppermute(last, axis, up)
        after = lax.ppermute(first, axis, down)
        array = jnp.concatenate([before, array, after], axis=dim)
    return array


def restrict(field):
    zc, xc, yc = field.shape
    return field.reshape(zc // 2, 2, xc // 2, 2, yc // 2, 2).mean(axis=(1, 3, 5))


def prolong(field):
    return jnp.repeat(jnp.repeat(jnp.repeat(field, 2, 0), 2, 1), 2, 2)


def operate(field, extra, scale, spread):
    if spread:
        padded = with_halo(field, (("wide", 1), ("narrow", 2)), 1)
        padded = jnp.pad(padded, ((1, 1), (0, 0), (0, 0)))
    else:
        padded = with_halo(field, (("narrow", 2),), 1)
        padded = jnp.pad(padded, ((1, 1), (1, 1), (0, 0)))
    beside = padded[2:, 1:-1, 1:-1] + padded[:-2, 1:-1, 1:-1]
    beside = beside + padded[1:-1, 2:, 1:-1] + padded[1:-1, :-2, 1:-1]
    beside = beside + padded[1:-1, 1:-1, 2:] + padded[1:-1, 1:-1, :-2]
    return scale * (6.0 * field - beside) + extra * field


def vcycle(level, source, diags, collect):
    scale = 0.25**level
    spread = level < collect
    inverse = OMEGA / (6.0 * scale + diags[level])
    correct = inverse * source
    if level == LEVELS - 1:
        for sweep in range(COARSE_SWEEPS - 1):
            correct = correct + inverse * (source - operate(correct, diags[level], scale, spread))
        line_total = jnp.sum(source, axis=1, keepdims=True)
        line_weight = jnp.sum(diags[level], axis=1, keepdims=True)
        return correct + line_total / line_weight
    left = restrict(source - operate(correct, diags[level], scale, spread))
    if level + 1 == collect:
        width = left.shape[1]
        whole = lax.all_gather(left, "wide", axis=1, tiled=True)
        coarse = vcycle(level + 1, whole, diags, collect)
        coarse = lax.dynamic_slice_in_dim(coarse, lax.axis_index("wide") * width, width, 1)
    else:
        coarse = vcycle(level + 1, left, diags, collect)
    correct = correct + prolong(coarse)
    return correct + inverse * (source - operate(correct, diags[level], scale, spread))


def inner_sum(first, second):
    return lax.psum(jnp.sum(first * second), ("wide", "narrow"))


def on_device(right_side, capacity, phase, mold_flags):
    collect = 2
    weight = jnp.where(phase == 1, jnp.float32(4.0), jnp.float32(1.0))
    base = 0.05 * capacity * weight + 0.5 * mold_flags.astype(jnp.float32)
    diags = [base]
    for level in range(1, LEVELS):
        lower = restrict(diags[-1])
        if level == collect:
            lower = lax.all_gather(lower, "wide", axis=1, tiled=True)
        diags.append(lower)
    adjoint_field = jnp.zeros_like(right_side)
    residual = right_side
    precond = vcycle(0, residual, diags, collect)
    rho = inner_sum(residual, precond)
    direction = precond
    for step in range(ITERS):
        image = operate(direction, base, 1.0, True)
        alpha = rho / lax.psum(jnp.sum(direction * image), ("wide", "narrow"))
        adjoint_field = adjoint_field + alpha * direction
        residual = residual - alpha * image
        if step + 1 < ITERS:
            precond = vcycle(0, residual, diags, collect)
            rho_next = inner_sum(residual, precond)
            direction = precond + rho_next / rho * direction
            rho = rho_next
    return (adjoint_field, residual)


def solution(mesh):
    in_specs = (
        P(None, "wide", "narrow"),
        P(None, "wide", "narrow"),
        P(None, "wide", "narrow"),
        P(None, "wide", "narrow"),
    )
    out_specs = (P(None, "wide", "narrow"), P(None, "wide", "narrow"))
    return jax.shard_map(
        on_device, mesh=mesh, in_specs=in_specs, out_specs=out_specs, check_vma=False
    )
```

profile of v0, /device:TPU:1, one launch (start us, length us, event | category | flops | bytes accessed | tf_op | source)
XLA Modules:
  0.0 856.9 jit_solution(18248448103635427115)
XLA Ops:
  1.6 4.4 collective-permute-start
  10.7 4.9 collective-permute-start.2
  18.7 5.6 reshape.98
  27.3 5.6 reshape.99
  43.7 4.8 collective-permute-start.6
  50.4 68.8 %all_gather.9 = f32[4,128,32]{2,0,1:T(4,128)S(1)} all-gather(f32[4,2,32]{2,0,1:T(4,128)S(1)} %broadcast_multiply_fusion.5), channel_id=1, replica_groups=mesh['wide'=64,'narrow'=8] {'wide'}, dimensions={1}, use_global_device_ids=true | all-gather | bytes 66560 | tf_op jit(solution)/shard_map/all_gather | solution.py:84
  120.3 61.5 %all_gather.10 = f32[4,128,32]{2,0,1:T(4,128)S(1)} all-gather(f32[4,2,32]{2,0,1:T(4,128)S(1)} %broadcast_multiply_fusion.4), channel_id=1, replica_groups=mesh['wide'=64,'narrow'=8] {'wide'}, dimensions={1}, use_global_device_ids=true | all-gather | bytes 66560 | tf_op jit(solution)/shard_map/all_gather | solution.py:63
  182.0 36.3 %collective-permute-start.9 = (f32[4,128,1]{1,2,0:T(1,128)S(1)}, f32[4,128,1]{1,2,0:T(1,128)S(1)}, u32[]{:S(2)}, u32[]{:S(2)}) collective-permute-start(f32[4,128,1]{1,2,0:T(1,128)S(1)} %get-tuple-element.69), channel_id=1, source_target_pairs={{1,0},{2,1},{3,2},{4,3},{5,4},{6,5},{7,6},{9,8},{10,9},{11,10},{12... | collective-permute-start | bytes 6152 | tf_op jit(solution)/shard_map/ppermute | solution.py:22
  218.3 6.7 collective-permute-start.8
  225.0 5.6 reshape.101
  233.4 5.6 reshape.102
  250.0 4.2 collective-permute-start.12
  257.0 4.2 collective-permute-start.14
  264.4 4.4 collective-permute-start.16
  277.1 5.6 collective-permute-start.20
  321.9 105.4 %all-reduce.20 = (f32[]{:T(128)}, f32[]{:T(128)}) all-reduce(f32[]{:T(128)} %get-tuple-element.11, f32[]{:T(128)} %get-tuple-element.10), channel_id=1, replica_groups=mesh['wide'=64,'narrow'=8] {'wide','narrow'}, use_global_device_ids=true, to_apply=%region_9.10 | all-reduce | flops 2 | bytes 16 | tf_op jit(solution)/shard_map/psum | solution.py:73
  444.9 5.6 reshape.112
  468.6 68.0 %all_gather.11 = f32[4,128,32]{2,0,1:T(4,128)S(1)} all-gather(f32[4,2,32]{2,0,1:T(4,128)S(1)} %broadcast_multiply_fusion.3), channel_id=1, replica_groups=mesh['wide'=64,'narrow'=8] {'wide'}, dimensions={1}, use_global_device_ids=true | all-gather | bytes 66560 | tf_op jit(solution)/shard_map/all_gather | solution.py:63
  536.7 18.5 %collective-permute-start.39 = (f32[4,128,1]{1,2,0:T(1,128)S(1)}, f32[4,128,1]{1,2,0:T(1,128)S(1)}, u32[]{:S(2)}, u32[]{:S(2)}) collective-permute-start(f32[4,128,1]{1,2,0:T(1,128)S(1)} %get-tuple-element.57), channel_id=1, source_target_pairs={{1,0},{2,1},{3,2},{4,3},{5,4},{6,5},{7,6},{9,8},{10,9},{11,10},{12... | collective-permute-start | bytes 6152 | tf_op jit(solution)/shard_map/ppermute | solution.py:22
  560.3 5.6 reshape.114
  570.3 4.2 collective-permute-start.40
  603.2 5.3 collective-permute-start.50
  630.4 104.1 %psum.30 = f32[]{:T(128)} all-reduce(f32[]{:T(128)} %get-tuple-element.16), channel_id=1, replica_groups=mesh['wide'=64,'narrow'=8] {'wide','narrow'}, use_global_device_ids=true, to_apply=%region_17.18 | all-reduce | flops 1 | bytes 8 | tf_op jit(solution)/shard_map/psum | solution.py:73
  751.3 103.6 %psum.31 = f32[]{:T(128)} all-reduce(f32[]{:T(128)} %get-tuple-element.14), channel_id=1, replica_groups=mesh['wide'=64,'narrow'=8] {'wide','narrow'}, use_global_device_ids=true, to_apply=%region_19.20 | all-reduce | flops 1 | bytes 8 | tf_op jit(solution)/shard_map/psum | solution.py:93
  (295 shorter events, 202.3 us)
Async XLA Ops:
  1.6 5.7 collective-permute-start
  10.7 16.1 %collective-permute-start.2 = (f32[16,10,1]{2,0,1:T(8,128)S(1)}, f32[16,10,1]{2,0,1:T(8,128)S(1)}, u32[]{:S(2)}, u32[]{:S(2)}) collective-permute-start(f32[16,10,1]{2,0,1:T(8,128)S(1)} %get-tuple-element.49), channel_id=1, source_target_pairs={{0,1},{1,2},{2,3},{3,4},{4,5},{5,6},{6,7},{8,9},{9,10},{10,11},{11... | collective-permute-start | bytes 1928 | tf_op jit(solution)/shard_map/ppermute | solution.py:21
  15.6 11.2 %collective-permute-start.3 = (f32[16,10,1]{2,0,1:T(8,128)S(1)}, f32[16,10,1]{2,0,1:T(8,128)S(1)}, u32[]{:S(2)}, u32[]{:S(2)}) collective-permute-start(f32[16,10,1]{2,0,1:T(8,128)S(1)} %get-tuple-element.50), channel_id=1, source_target_pairs={{1,0},{2,1},{3,2},{4,3},{5,4},{6,5},{7,6},{9,8},{10,9},{11,10},{12... | collective-permute-start | bytes 1928 | tf_op jit(solution)/shard_map/ppermute | solution.py:22
  37.9 5.7 collective-permute-start.5
  43.7 75.6 %collective-permute-start.6 = (f32[8,6,1]{2,0,1:T(8,128)S(1)}, f32[8,6,1]{2,0,1:T(8,128)S(1)}, u32[]{:S(2)}, u32[]{:S(2)}) collective-permute-start(f32[8,6,1]{2,0,1:T(8,128)S(1)} %get-tuple-element.87), channel_id=1, source_target_pairs={{0,1},{1,2},{2,3},{3,4},{4,5},{5,6},{6,7},{8,9},{9,10},{10,11},{11... | collective-permute-start | bytes 584 | tf_op jit(solution)/shard_map/ppermute | solution.py:21
  48.5 70.8 %collective-permute-start.7 = (f32[8,6,1]{2,0,1:T(8,128)S(1)}, f32[8,6,1]{2,0,1:T(8,128)S(1)}, u32[]{:S(2)}, u32[]{:S(2)}) collective-permute-start(f32[8,6,1]{2,0,1:T(8,128)S(1)} %get-tuple-element.88), channel_id=1, source_target_pairs={{1,0},{2,1},{3,2},{4,3},{5,4},{6,5},{7,6},{9,8},{10,9},{11,10},{12... | collective-permute-start | bytes 584 | tf_op jit(solution)/shard_map/ppermute | solution.py:22
  182.0 51.1 %collective-permute-start.9 = (f32[4,128,1]{1,2,0:T(1,128)S(1)}, f32[4,128,1]{1,2,0:T(1,128)S(1)}, u32[]{:S(2)}, u32[]{:S(2)}) collective-permute-start(f32[4,128,1]{1,2,0:T(1,128)S(1)} %get-tuple-element.69), channel_id=1, source_target_pairs={{1,0},{2,1},{3,2},{4,3},{5,4},{6,5},{7,6},{9,8},{10,9},{11,10},{12... | collective-permute-start | bytes 6152 | tf_op jit(solution)/shard_map/ppermute | solution.py:22
  218.3 14.8 %collective-permute-start.8 = (f32[4,128,1]{1,2,0:T(1,128)S(1)}, f32[4,128,1]{1,2,0:T(1,128)S(1)}, u32[]{:S(2)}, u32[]{:S(2)}) collective-permute-start(f32[4,128,1]{1,2,0:T(1,128)S(1)} %get-tuple-element.70), channel_id=1, source_target_pairs={{0,1},{1,2},{2,3},{3,4},{4,5},{5,6},{6,7},{8,9},{9,10},{10,11},{11... | collective-permute-start | bytes 6152 | tf_op jit(solution)/shard_map/ppermute | solution.py:21
  248.0 6.1 collective-permute-start.13
  255.1 6.1 collective-permute-start.15
  262.4 6.3 collective-permute-start.17
  277.1 7.5 collective-permute-start.20
  298.6 5.8 collective-permute-start.25
  313.7 5.8 collective-permute-start.29
  434.9 5.7 collective-permute-start.32
  438.7 5.8 collective-permute-start.33
  536.7 22.6 %collective-permute-start.39 = (f32[4,128,1]{1,2,0:T(1,128)S(1)}, f32[4,128,1]{1,2,0:T(1,128)S(1)}, u32[]{:S(2)}, u32[]{:S(2)}) collective-permute-start(f32[4,128,1]{1,2,0:T(1,128)S(1)} %get-tuple-element.57), channel_id=1, source_target_pairs={{1,0},{2,1},{3,2},{4,3},{5,4},{6,5},{7,6},{9,8},{10,9},{11,10},{12... | collective-permute-start | bytes 6152 | tf_op jit(solution)/shard_map/ppermute | solution.py:22
  568.4 6.1 collective-permute-start.41
  575.4 6.1 collective-permute-start.43
  582.5 6.1 collective-permute-start.45
  589.8 6.1 collective-permute-start.47
  603.2 7.3 collective-permute-start.50
  622.1 5.8 collective-permute-start.55
  742.5 6.4 collective-permute-start.59
  (37 other events, 170.9 us)
where the time goes:
time: 859 us; the launch traced here: 857 us
  blocking collectives  511 us (59%)
  starting transfers between devices  215 us (25%)
  waiting for transfers between devices  59.7 us (7%)
  local copies, waits for them, and re-layouts  39.2 us (5%)
  other arithmetic  25.1 us (3%)
    psum x2, blocking collectives, inner_sum(): return lax.psum(jnp.sum(first * second), ('wide', 'narrow'))  210 us
    all_gather x2, blocking collectives, vcycle(): whole = lax.all_gather(left, 'wide', axis=1, tiled=True)  129 us
    ppermute x30, starting transfers between devices, with_halo(): before = lax.ppermute(last, axis, up)  109 us
    ppermute x30, starting transfers between devices, with_halo(): after = lax.ppermute(first, axis, down)  106 us
    psum x1, blocking collectives, on_device(): alpha = rho / lax.psum(jnp.sum(direction * image), ('wide', 'narrow'))  104 us
    all_gather x1, blocking collectives, on_device(): lower = lax.all_gather(lower, 'wide', axis=1, tiled=True)  68.8 us
    ppermute x30, waiting for transfers between devices, with_halo(): after = lax.ppermute(first, axis, down)  49.6 us
    reshape x8, local copies, waits for them, and re-layouts, restrict(): field.reshape(zc // 2, 2, xc // 2, 2, yc // 2, 2).mean(axis=(1, 3, 5))  34.5 us
  transfers between devices with their start and end apart: 60, of which 29 were waited for; matrix products, arithmetic and copies ran while one was open for 2% of the time, Pallas kernels for 0%

commit v1 on v0

--- a/solution.py
+++ b/solution.py
@@ -9,6 +9,18 @@
 
 
 OMEGA = 0.8
+
+
+def gathered(array, axis):
+    peers = lax.axis_size(axis)
+    slots = jnp.broadcast_to(array[None], (peers,) + array.shape)
+    return lax.all_to_all(slots, axis, 0, 0)
+
+
+def gather_rows(array):
+    parts = gathered(array, "wide")
+    peers, zc, xc, yc = parts.shape
+    return jnp.transpose(parts, (1, 0, 2, 3)).reshape(zc, peers * xc, yc)
 
 
 def with_halo(array, sides, width):
@@ -60,7 +72,7 @@
     left = restrict(source - operate(correct, diags[level], scale, spread))
     if level + 1 == collect:
         width = left.shape[1]
-        whole = lax.all_gather(left, "wide", axis=1, tiled=True)
+        whole = gather_rows(left)
         coarse = vcycle(level + 1, whole, diags, collect)
         coarse = lax.dynamic_slice_in_dim(coarse, lax.axis_index("wide") * width, width, 1)
     else:
@@ -70,7 +82,9 @@
 
 
 def inner_sum(first, second):
-    return lax.psum(jnp.sum(first * second), ("wide", "narrow"))
+    part = jnp.sum(first * second).reshape(1)
+    part = jnp.sum(gathered(part, "narrow"), axis=0)
+    return jnp.sum(gathered(part, "wide"))
 
 
 def on_device(right_side, capacity, phase, mold_flags):
@@ -81,7 +95,7 @@
     for level in range(1, LEVELS):
         lower = restrict(diags[-1])
         if level == collect:
-            lower = lax.all_gather(lower, "wide", axis=1, tiled=True)
+            lower = gather_rows(lower)
         diags.append(lower)
     adjoint_field = jnp.zeros_like(right_side)
     residual = right_side
@@ -90,7 +104,7 @@
     direction = precond
     for step in range(ITERS):
         image = operate(direction, base, 1.0, True)
-        alpha = rho / lax.psum(jnp.sum(direction * image), ("wide", "narrow"))
+        alpha = rho / inner_sum(direction, image)
         adjoint_field = adjoint_field + alpha * direction
         residual = residual - alpha * image
         if step + 1 < ITERS:

time: 859 us -> 515 us (0.60)
  blocking collectives: 511 us -> 96.3 us
  waiting for transfers between devices: 59.7 us -> 122 us
    psum x3 -> x0, blocking collectives: 313 us -> none  [the longest x2 210 us: inner_sum(): return lax.psum(jnp.sum(first * second), ('wide', 'narrow'))]
    all_gather x3 -> x0, blocking collectives: 198 us -> none  [the longest x2 129 us: vcycle(): whole = lax.all_gather(left, 'wide', axis=1, tiled=True)]
    all_to_all x0 -> x6, blocking collectives: none -> 96.3 us  [gathered(): return lax.all_to_all(slots, axis, 0, 0)]
    all_to_all x0 -> x5, waiting for transfers between devices: none -> 52.6 us  [gathered(): return lax.all_to_all(slots, axis, 0, 0)]
    ppermute x30, starting transfers between devices: 106 us -> 56.2 us  [with_halo(): after = lax.ppermute(first, axis, down)]
    all_to_all x0 -> x5, starting transfers between devices: none -> 41 us  [gathered(): return lax.all_to_all(slots, axis, 0, 0)]
    reshape x8 -> x7, local copies, waits for them, and re-layouts: 34.5 us -> 28.7 us  [restrict(): field.reshape(zc // 2, 2, xc // 2, 2, yc // 2, 2).mean(axis=(1, 3, 5))]
  transfers between devices with their start and end apart: 60 -> 65, of which waited for: 29 -> 40; matrix products, arithmetic and copies ran while one was open for 2% -> 3% of each run, Pallas kernels for 0% -> 0%
where the time goes in v1:
time: 515 us; the launch traced here: 512 us
  starting transfers between devices  210 us (41%)
  waiting for transfers between devices  122 us (24%)
  blocking collectives  96.3 us (19%)
  local copies, waits for them, and re-layouts  44.7 us (9%)
  other arithmetic  32.4 us (6%)
  between operations  6.52 us (1%)
    ppermute x30, starting transfers between devices, with_halo(): before = lax.ppermute(last, axis, up)  113 us
    all_to_all x6, blocking collectives, gathered(): return lax.all_to_all(slots, axis, 0, 0)  96.3 us
    ppermute x30, waiting for transfers between devices, with_halo(): after = lax.ppermute(first, axis, down)  57 us
    ppermute x30, starting transfers between devices, with_halo(): after = lax.ppermute(first, axis, down)  56.2 us
    all_to_all x5, waiting for transfers between devices, gathered(): return lax.all_to_all(slots, axis, 0, 0)  52.6 us
    all_to_all x5, starting transfers between devices, gathered(): return lax.all_to_all(slots, axis, 0, 0)  41 us
    reshape x7, local copies, waits for them, and re-layouts, restrict(): field.reshape(zc // 2, 2, xc // 2, 2, yc // 2, 2).mean(axis=(1, 3, 5))  28.7 us
    reduce_sum x10, other arithmetic, restrict(): field.reshape(zc // 2, 2, xc // 2, 2, yc // 2, 2).mean(axis=(1, 3, 5))  13.5 us
  transfers between devices with their start and end apart: 65, of which 40 were waited for; matrix products, arithmetic and copies ran while one was open for 3% of the time, Pallas kernels for 0%

profile of v1, /device:TPU:1, one launch (start us, length us, event | category | flops | bytes accessed | tf_op | source)
XLA Modules:
  0.0 512.4 jit_solution(17522952714345467542)
XLA Ops:
  10.7 4.9 collective-permute-start.2
  18.7 5.5 %reshape.166 = f32[8,2,4,2,64,2]{5,4,3,2,1,0:T(8,128)} reshape(f32[16,8,128]{2,1,0:T(8,128)S(1)} %get-tuple-element.26) | data formatting | bytes 131072 | tf_op jit(solution)/shard_map/reshape | solution.py:41
  27.3 5.5 %reshape.167 = f32[8,2,4,2,64,2]{5,4,3,2,1,0:T(8,128)} reshape(f32[16,8,128]{2,1,0:T(8,128)S(1)} %fusion.26) | data formatting | bytes 131072 | tf_op jit(solution)/shard_map/reshape | solution.py:41
  43.6 4.8 collective-permute-start.6
  51.3 16.6 %all-to-all-start = ((f32[64,1,256]{2,1,0:T(1,128)}), f32[64,1,256]{2,1,0:T(1,128)S(1)}, u32[]{:S(2)}, u32[]{:S(2)}) async-start(f32[64,1,256]{2,1,0:T(1,128)} %reshape.196), calls=%async_computation | async-start | bytes 131072 | tf_op jit(solution)/shard_map/all_to_all | solution.py:17
  69.9 11.6 %all-to-all-done = f32[64,1,256]{2,1,0:T(1,128)S(1)} async-done(((f32[64,1,256]{2,1,0:T(1,128)}), f32[64,1,256]{2,1,0:T(1,128)S(1)}, u32[]{:S(2)}, u32[]{:S(2)}) %all-to-all-start) | async-done | bytes 65568 | tf_op jit(solution)/shard_map/all_to_all | solution.py:17
  87.7 12.0 %all-to-all-done.1 = f32[64,1,256]{2,1,0:T(1,128)S(1)} async-done(((f32[64,1,256]{2,1,0:T(1,128)}), f32[64,1,256]{2,1,0:T(1,128)S(1)}, u32[]{:S(2)}, u32[]{:S(2)}) %all-to-all-start.1) | async-done | bytes 65568 | tf_op jit(solution)/shard_map/all_to_all | solution.py:17
  103.0 6.2 %collective-permute-start.8 = (f32[4,128,1]{2,1,0:T(8,128)S(1)}, f32[4,128,1]{2,1,0:T(8,128)S(1)}, u32[]{:S(2)}, u32[]{:S(2)}) collective-permute-start(f32[4,128,1]{2,1,0:T(8,128)S(1)} %get-tuple-element.36), channel_id=1, source_target_pairs={{0,1},{1,2},{2,3},{3,4},{4,5},{5,6},{6,7},{8,9},{9,10},{10,11},{11... | collective-permute-start | bytes 6152 | tf_op jit(solution)/shard_map/ppermute | solution.py:33
  113.3 5.5 %reshape.171 = f32[2,2,64,2,16,2]{3,2,5,4,1,0:T(8,128)} reshape(f32[4,128,32]{1,2,0:T(8,128)S(1)} %copy.782) | data formatting | bytes 131072 | tf_op jit(solution)/shard_map/reshape | solution.py:41
  160.5 5.8 %collective-permute-start.20 = (f32[8,6,1]{2,0,1:T(8,128)S(1)}, f32[8,6,1]{2,0,1:T(8,128)S(1)}, u32[]{:S(2)}, u32[]{:S(2)}) collective-permute-start(f32[8,6,1]{2,0,1:T(8,128)S(1)} %get-tuple-element.83), channel_id=1, source_target_pairs={{0,1},{1,2},{2,3},{3,4},{4,5},{5,6},{6,7},{8,9},{9,10},{10,11},{11... | collective-permute-start | bytes 584 | tf_op jit(solution)/shard_map/ppermute | solution.py:33
  204.5 10.0 %all_to_all.63 = f32[8,1,1]{2,1,0:T(1,128)S(1)} all-to-all(f32[8,1,1]{2,1,0:T(1,128)S(1)} %broadcast_in_dim.143), channel_id=1, replica_groups=mesh['wide'=64,'narrow'=8] {'narrow'}, dimensions={0} | all-to-all | bytes 64 | tf_op jit(solution)/shard_map/all_to_all | solution.py:17
  225.3 11.3 %all-to-all-start.5 = ((f32[64,1,1]{2,1,0:T(1,128)}), f32[64,1,1]{2,1,0:T(1,128)S(1)}, u32[]{:S(2)}, u32[]{:S(2)}) async-start(f32[64,1,1]{2,1,0:T(1,128)} %broadcast_in_dim.144), calls=%async_computation.5 | async-start | bytes 65536 | tf_op jit(solution)/shard_map/all_to_all | solution.py:17
  237.2 12.6 %all-to-all-done.5 = f32[64,1,1]{2,1,0:T(1,128)S(1)} async-done(((f32[64,1,1]{2,1,0:T(1,128)}), f32[64,1,1]{2,1,0:T(1,128)S(1)}, u32[]{:S(2)}, u32[]{:S(2)}) %all-to-all-start.5) | async-done | bytes 288 | tf_op jit(solution)/shard_map/all_to_all | solution.py:17
  256.4 12.5 %all-to-all-done.3 = f32[64,1,1]{2,1,0:T(1,128)S(1)} async-done(((f32[64,1,1]{2,1,0:T(1,128)}), f32[64,1,1]{2,1,0:T(1,128)S(1)}, u32[]{:S(2)}, u32[]{:S(2)}) %all-to-all-start.3) | async-done | bytes 288 | tf_op jit(solution)/shard_map/all_to_all | solution.py:17
  277.5 6.8 %collective-permute-start.32 = (f32[16,10,1]{2,0,1:T(8,128)S(1)}, f32[16,10,1]{2,0,1:T(8,128)S(1)}, u32[]{:S(2)}, u32[]{:S(2)}) collective-permute-start(f32[16,10,1]{2,0,1:T(8,128)S(1)} %get-tuple-element.47), channel_id=1, source_target_pairs={{0,1},{1,2},{2,3},{3,4},{4,5},{5,6},{6,7},{8,9},{9,10},{10,11},{11... | collective-permute-start | bytes 1928 | tf_op jit(solution)/shard_map/ppermute | solution.py:33
  290.5 5.5 %reshape.181 = f32[8,2,4,2,64,2]{5,4,3,2,1,0:T(8,128)} reshape(f32[16,8,128]{2,1,0:T(8,128)S(1)} %fusion.51) | data formatting | bytes 131072 | tf_op jit(solution)/shard_map/reshape | solution.py:41
  315.2 23.3 %all_to_all.64 = f32[64,1,256]{2,1,0:T(1,128)S(1)} all-to-all(f32[64,1,256]{2,1,0:T(1,128)S(1)} %reshape.198), channel_id=1, replica_groups=mesh['wide'=64,'narrow'=8] {'wide'}, dimensions={0} | all-to-all | bytes 131072 | tf_op jit(solution)/shard_map/all_to_all | solution.py:17
  349.8 5.5 %reshape.184 = f32[2,2,64,2,16,2]{3,2,5,4,1,0:T(8,128)} reshape(f32[4,128,32]{1,2,0:T(8,128)S(1)} %copy.829) | data formatting | bytes 131072 | tf_op jit(solution)/shard_map/reshape | solution.py:41
  397.1 5.8 %collective-permute-start.50 = (f32[8,6,1]{2,0,1:T(8,128)S(1)}, f32[8,6,1]{2,0,1:T(8,128)S(1)}, u32[]{:S(2)}, u32[]{:S(2)}) collective-permute-start(f32[8,6,1]{2,0,1:T(8,128)S(1)} %get-tuple-element.75), channel_id=1, source_target_pairs={{0,1},{1,2},{2,3},{3,4},{4,5},{5,6},{6,7},{8,9},{9,10},{10,11},{11... | collective-permute-start | bytes 584 | tf_op jit(solution)/shard_map/ppermute | solution.py:33
  424.6 9.6 %all_to_all.65 = f32[8,1,1]{2,1,0:T(1,128)S(1)} all-to-all(f32[8,1,1]{2,1,0:T(1,128)S(1)} %broadcast_in_dim.155), channel_id=1, replica_groups=mesh['wide'=64,'narrow'=8] {'narrow'}, dimensions={0} | all-to-all | bytes 64 | tf_op jit(solution)/shard_map/all_to_all | solution.py:17
  435.5 23.2 %all_to_all.66 = f32[64,1,1]{2,1,0:T(1,128)S(1)} all-to-all(f32[64,1,1]{2,1,0:T(1,128)S(1)} %broadcast_in_dim.156), channel_id=1, replica_groups=mesh['wide'=64,'narrow'=8] {'wide'}, dimensions={0} | all-to-all | bytes 512 | tf_op jit(solution)/shard_map/all_to_all | solution.py:17
  467.3 5.6 %collective-permute-start.59 = (f32[16,10,1]{2,0,1:T(8,128)S(1)}, f32[16,10,1]{2,0,1:T(8,128)S(1)}, u32[]{:S(2)}, u32[]{:S(2)}) collective-permute-start(f32[16,10,1]{2,0,1:T(8,128)S(1)} %get-tuple-element.39), channel_id=1, source_target_pairs={{1,0},{2,1},{3,2},{4,3},{5,4},{6,5},{7,6},{9,8},{10,9},{11,10},{12... | collective-permute-start | bytes 1928 | tf_op jit(solution)/shard_map/ppermute | solution.py:34
  478.2 9.0 %all_to_all.67 = f32[8,1,1]{2,1,0:T(1,128)S(1)} all-to-all(f32[8,1,1]{2,1,0:T(1,128)S(1)} %broadcast_in_dim.157), channel_id=1, replica_groups=mesh['wide'=64,'narrow'=8] {'narrow'}, dimensions={0} | all-to-all | bytes 64 | tf_op jit(solution)/shard_map/all_to_all | solution.py:17
  488.5 21.3 %all_to_all.68 = f32[64,1,1]{2,1,0:T(1,128)S(1)} all-to-all(f32[64,1,1]{2,1,0:T(1,128)S(1)} %broadcast_in_dim.158), channel_id=1, replica_groups=mesh['wide'=64,'narrow'=8] {'wide'}, dimensions={0} | all-to-all | bytes 512 | tf_op jit(solution)/shard_map/all_to_all | solution.py:17
  (342 shorter events, 265.4 us)
Async XLA Ops:
  10.7 16.1 %collective-permute-start.2 = (f32[16,10,1]{2,0,1:T(8,128)S(1)}, f32[16,10,1]{2,0,1:T(8,128)S(1)}, u32[]{:S(2)}, u32[]{:S(2)}) collective-permute-start(f32[16,10,1]{2,0,1:T(8,128)S(1)} %get-tuple-element.59), channel_id=1, source_target_pairs={{0,1},{1,2},{2,3},{3,4},{4,5},{5,6},{6,7},{8,9},{9,10},{10,11},{11... | collective-permute-start | bytes 1928 | tf_op jit(solution)/shard_map/ppermute | solution.py:33
  15.6 11.2 %collective-permute-start.3 = (f32[16,10,1]{2,0,1:T(8,128)S(1)}, f32[16,10,1]{2,0,1:T(8,128)S(1)}, u32[]{:S(2)}, u32[]{:S(2)}) collective-permute-start(f32[16,10,1]{2,0,1:T(8,128)S(1)} %get-tuple-element.60), channel_id=1, source_target_pairs={{1,0},{2,1},{3,2},{4,3},{5,4},{6,5},{7,6},{9,8},{10,9},{11,10},{12... | collective-permute-start | bytes 1928 | tf_op jit(solution)/shard_map/ppermute | solution.py:34
  43.6 24.3 %collective-permute-start.6 = (f32[8,6,1]{2,0,1:T(8,128)S(1)}, f32[8,6,1]{2,0,1:T(8,128)S(1)}, u32[]{:S(2)}, u32[]{:S(2)}) collective-permute-start(f32[8,6,1]{2,0,1:T(8,128)S(1)} %get-tuple-element.87), channel_id=1, source_target_pairs={{0,1},{1,2},{2,3},{3,4},{4,5},{5,6},{6,7},{8,9},{9,10},{10,11},{11... | collective-permute-start | bytes 584 | tf_op jit(solution)/shard_map/ppermute | solution.py:33
  48.4 19.5 %collective-permute-start.7 = (f32[8,6,1]{2,0,1:T(8,128)S(1)}, f32[8,6,1]{2,0,1:T(8,128)S(1)}, u32[]{:S(2)}, u32[]{:S(2)}) collective-permute-start(f32[8,6,1]{2,0,1:T(8,128)S(1)} %get-tuple-element.88), channel_id=1, source_target_pairs={{1,0},{2,1},{3,2},{4,3},{5,4},{6,5},{7,6},{9,8},{10,9},{11,10},{12... | collective-permute-start | bytes 584 | tf_op jit(solution)/shard_map/ppermute | solution.py:34
  51.3 30.2 %all-to-all-start = ((f32[64,1,256]{2,1,0:T(1,128)}), f32[64,1,256]{2,1,0:T(1,128)S(1)}, u32[]{:S(2)}, u32[]{:S(2)}) async-start(f32[64,1,256]{2,1,0:T(1,128)} %reshape.196), calls=%async_computation | async-start | bytes 131072 | tf_op jit(solution)/shard_map/all_to_all | solution.py:17
  81.4 18.3 %all-to-all-start.1 = ((f32[64,1,256]{2,1,0:T(1,128)}), f32[64,1,256]{2,1,0:T(1,128)S(1)}, u32[]{:S(2)}, u32[]{:S(2)}) async-start(f32[64,1,256]{2,1,0:T(1,128)} %reshape.194), calls=%async_computation.1 | async-start | bytes 131072 | tf_op jit(solution)/shard_map/all_to_all | solution.py:17
  101.1 10.1 %collective-permute-start.9 = (f32[4,128,1]{2,1,0:T(8,128)S(1)}, f32[4,128,1]{2,1,0:T(8,128)S(1)}, u32[]{:S(2)}, u32[]{:S(2)}) collective-permute-start(f32[4,128,1]{2,1,0:T(8,128)S(1)} %get-tuple-element.35), channel_id=1, source_target_pairs={{1,0},{2,1},{3,2},{4,3},{5,4},{6,5},{7,6},{9,8},{10,9},{11,10},{12... | collective-permute-start | bytes 6152 | tf_op jit(solution)/shard_map/ppermute | solution.py:34
  103.0 9.4 %collective-permute-start.8 = (f32[4,128,1]{2,1,0:T(8,128)S(1)}, f32[4,128,1]{2,1,0:T(8,128)S(1)}, u32[]{:S(2)}, u32[]{:S(2)}) collective-permute-start(f32[4,128,1]{2,1,0:T(8,128)S(1)} %get-tuple-element.36), channel_id=1, source_target_pairs={{0,1},{1,2},{2,3},{3,4},{4,5},{5,6},{6,7},{8,9},{9,10},{10,11},{11... | collective-permute-start | bytes 6152 | tf_op jit(solution)/shard_map/ppermute | solution.py:33
  121.4 6.3 %collective-permute-start.11 = (f32[2,64,1]{1,2,0:T(1,128)S(1)}, f32[2,64,1]{1,2,0:T(1,128)S(1)}, u32[]{:S(2)}, u32[]{:S(2)}) collective-permute-start(f32[2,64,1]{1,2,0:T(1,128)S(1)} %get-tuple-element.110), channel_id=1, source_target_pairs={{1,0},{2,1},{3,2},{4,3},{5,4},{6,5},{7,6},{9,8},{10,9},{11,10},{12... | collective-permute-start | bytes 1544 | tf_op jit(solution)/shard_map/ppermute | solution.py:34
  135.6 6.1 %collective-permute-start.15 = (f32[2,64,1]{1,2,0:T(1,128)S(1)}, f32[2,64,1]{1,2,0:T(1,128)S(1)}, u32[]{:S(2)}, u32[]{:S(2)}) collective-permute-start(f32[2,64,1]{1,2,0:T(1,128)S(1)} %get-tuple-element.106), channel_id=1, source_target_pairs={{1,0},{2,1},{3,2},{4,3},{5,4},{6,5},{7,6},{9,8},{10,9},{11,10},{12... | collective-permute-start | bytes 1544 | tf_op jit(solution)/shard_map/ppermute | solution.py:34
  143.3 8.2 %collective-permute-start.17 = (f32[4,128,1]{2,1,0:T(8,128)S(1)}, f32[4,128,1]{2,1,0:T(8,128)S(1)}, u32[]{:S(2)}, u32[]{:S(2)}) collective-permute-start(f32[4,128,1]{2,1,0:T(8,128)S(1)} %get-tuple-element.33), channel_id=1, source_target_pairs={{1,0},{2,1},{3,2},{4,3},{5,4},{6,5},{7,6},{9,8},{10,9},{11,10},{12... | collective-permute-start | bytes 6152 | tf_op jit(solution)/shard_map/ppermute | solution.py:34
  145.2 7.5 %collective-permute-start.16 = (f32[4,128,1]{2,1,0:T(8,128)S(1)}, f32[4,128,1]{2,1,0:T(8,128)S(1)}, u32[]{:S(2)}, u32[]{:S(2)}) collective-permute-start(f32[4,128,1]{2,1,0:T(8,128)S(1)} %get-tuple-element.34), channel_id=1, source_target_pairs={{0,1},{1,2},{2,3},{3,4},{4,5},{5,6},{6,7},{8,9},{9,10},{10,11},{11... | collective-permute-start | bytes 6152 | tf_op jit(solution)/shard_map/ppermute | solution.py:33
  160.5 7.7 %collective-permute-start.20 = (f32[8,6,1]{2,0,1:T(8,128)S(1)}, f32[8,6,1]{2,0,1:T(8,128)S(1)}, u32[]{:S(2)}, u32[]{:S(2)}) collective-permute-start(f32[8,6,1]{2,0,1:T(8,128)S(1)} %get-tuple-element.83), channel_id=1, source_target_pairs={{0,1},{1,2},{2,3},{3,4},{4,5},{5,6},{6,7},{8,9},{9,10},{10,11},{11... | collective-permute-start | bytes 584 | tf_op jit(solution)/shard_map/ppermute | solution.py:33
  215.7 8.4 %all-to-all-start.2 = ((f32[8,1,1]{2,1,0:T(1,128)}), f32[8,1,1]{2,1,0:T(1,128)S(1)}, u32[]{:S(2)}, u32[]{:S(2)}) async-start(f32[8,1,1]{2,1,0:T(1,128)} %broadcast_in_dim.141), calls=%async_computation.2 | async-start | bytes 8192 | tf_op jit(solution)/shard_map/all_to_all | solution.py:17
  225.3 24.5 %all-to-all-start.5 = ((f32[64,1,1]{2,1,0:T(1,128)}), f32[64,1,1]{2,1,0:T(1,128)S(1)}, u32[]{:S(2)}, u32[]{:S(2)}) async-start(f32[64,1,1]{2,1,0:T(1,128)} %broadcast_in_dim.144), calls=%async_computation.5 | async-start | bytes 65536 | tf_op jit(solution)/shard_map/all_to_all | solution.py:17
  251.1 17.8 %all-to-all-start.3 = ((f32[64,1,1]{2,1,0:T(1,128)}), f32[64,1,1]{2,1,0:T(1,128)S(1)}, u32[]{:S(2)}, u32[]{:S(2)}) async-start(f32[64,1,1]{2,1,0:T(1,128)} %broadcast_in_dim.142), calls=%async_computation.3 | async-start | bytes 65536 | tf_op jit(solution)/shard_map/all_to_all | solution.py:17
  277.5 8.7 %collective-permute-start.32 = (f32[16,10,1]{2,0,1:T(8,128)S(1)}, f32[16,10,1]{2,0,1:T(8,128)S(1)}, u32[]{:S(2)}, u32[]{:S(2)}) collective-permute-start(f32[16,10,1]{2,0,1:T(8,128)S(1)} %get-tuple-element.47), channel_id=1, source_target_pairs={{0,1},{1,2},{2,3},{3,4},{4,5},{5,6},{6,7},{8,9},{9,10},{10,11},{11... | collective-permute-start | bytes 1928 | tf_op jit(solution)/shard_map/ppermute | solution.py:33
  339.8 7.9 %collective-permute-start.39 = (f32[4,128,1]{2,1,0:T(8,128)S(1)}, f32[4,128,1]{2,1,0:T(8,128)S(1)}, u32[]{:S(2)}, u32[]{:S(2)}) collective-permute-start(f32[4,128,1]{2,1,0:T(8,128)S(1)} %get-tuple-element.29), channel_id=1, source_target_pairs={{1,0},{2,1},{3,2},{4,3},{5,4},{6,5},{7,6},{9,8},{10,9},{11,10},{12... | collective-permute-start | bytes 6152 | tf_op jit(solution)/shard_map/ppermute | solution.py:34
  341.8 7.2 %collective-permute-start.38 = (f32[4,128,1]{2,1,0:T(8,128)S(1)}, f32[4,128,1]{2,1,0:T(8,128)S(1)}, u32[]{:S(2)}, u32[]{:S(2)}) collective-permute-start(f32[4,128,1]{2,1,0:T(8,128)S(1)} %get-tuple-element.30), channel_id=1, source_target_pairs={{0,1},{1,2},{2,3},{3,4},{4,5},{5,6},{6,7},{8,9},{9,10},{10,11},{11... | collective-permute-start | bytes 6152 | tf_op jit(solution)/shard_map/ppermute | solution.py:33
  357.9 6.3 %collective-permute-start.41 = (f32[2,64,1]{1,2,0:T(1,128)S(1)}, f32[2,64,1]{1,2,0:T(1,128)S(1)}, u32[]{:S(2)}, u32[]{:S(2)}) collective-permute-start(f32[2,64,1]{1,2,0:T(1,128)S(1)} %get-tuple-element.97), channel_id=1, source_target_pairs={{1,0},{2,1},{3,2},{4,3},{5,4},{6,5},{7,6},{9,8},{10,9},{11,10},{12... | collective-permute-start | bytes 1544 | tf_op jit(solution)/shard_map/ppermute | solution.py:34
  379.8 8.2 %collective-permute-start.47 = (f32[4,128,1]{2,1,0:T(8,128)S(1)}, f32[4,128,1]{2,1,0:T(8,128)S(1)}, u32[]{:S(2)}, u32[]{:S(2)}) collective-permute-start(f32[4,128,1]{2,1,0:T(8,128)S(1)} %get-tuple-element.27), channel_id=1, source_target_pairs={{1,0},{2,1},{3,2},{4,3},{5,4},{6,5},{7,6},{9,8},{10,9},{11,10},{12... | collective-permute-start | bytes 6152 | tf_op jit(solution)/shard_map/ppermute | solution.py:34
  381.7 7.5 %collective-permute-start.46 = (f32[4,128,1]{2,1,0:T(8,128)S(1)}, f32[4,128,1]{2,1,0:T(8,128)S(1)}, u32[]{:S(2)}, u32[]{:S(2)}) collective-permute-start(f32[4,128,1]{2,1,0:T(8,128)S(1)} %get-tuple-element.28), channel_id=1, source_target_pairs={{0,1},{1,2},{2,3},{3,4},{4,5},{5,6},{6,7},{8,9},{9,10},{10,11},{11... | collective-permute-start | bytes 6152 | tf_op jit(solution)/shard_map/ppermute | solution.py:33
  397.1 7.7 %collective-permute-start.50 = (f32[8,6,1]{2,0,1:T(8,128)S(1)}, f32[8,6,1]{2,0,1:T(8,128)S(1)}, u32[]{:S(2)}, u32[]{:S(2)}) collective-permute-start(f32[8,6,1]{2,0,1:T(8,128)S(1)} %get-tuple-element.75), channel_id=1, source_target_pairs={{0,1},{1,2},{2,3},{3,4},{4,5},{5,6},{6,7},{8,9},{9,10},{10,11},{11... | collective-permute-start | bytes 584 | tf_op jit(solution)/shard_map/ppermute | solution.py:33
  467.3 7.9 %collective-permute-start.59 = (f32[16,10,1]{2,0,1:T(8,128)S(1)}, f32[16,10,1]{2,0,1:T(8,128)S(1)}, u32[]{:S(2)}, u32[]{:S(2)}) collective-permute-start(f32[16,10,1]{2,0,1:T(8,128)S(1)} %get-tuple-element.39), channel_id=1, source_target_pairs={{1,0},{2,1},{3,2},{4,3},{5,4},{6,5},{7,6},{9,8},{10,9},{11,10},{12... | collective-permute-start | bytes 1928 | tf_op jit(solution)/shard_map/ppermute | solution.py:34
  (42 other events, 203.8 us)

commit v2 on v0

v2 whole, which is shorter than its diff:
```python
import functools

import jax
import jax.numpy as jnp
from jax import lax
from jax.experimental import pallas as pl
from jax.experimental.pallas import tpu as pltpu
from jax.sharding import PartitionSpec as P

OMEGA = 0.8
HALO = 5
OWN = 8
EXT = OWN + 2 * HALO
LANES = 256
F32 = jnp.float32


def iota(shape, dim):
    return lax.broadcasted_iota(jnp.int32, shape, dim)


def roll(value, shift, axis):
    return pltpu.roll(value, shift % value.shape[axis], axis)


def swap(value, width, axis):
    at = iota(value.shape, axis)
    lower = (at // width) % 2 == 0
    return jnp.where(lower, roll(value, -width, axis), roll(value, width, axis))


def along_y(value, width):
    axis = value.ndim - 1
    return roll(value, width, axis) + roll(value, -width, axis)


def apply_fine(even, odd, extra_even, extra_odd):
    e, o = even[1:-1], odd[1:-1]
    k = iota(e.shape, 1)
    by_e = o + jnp.where(k > 0, roll(o, 1, 1), 0.0) + even[2:] + even[:-2] + along_y(e, 1)
    by_o = e + jnp.where(k < 7, roll(e, -1, 1), 0.0) + odd[2:] + odd[:-2] + along_y(o, 1)
    return 6.0 * e - by_e + extra_even * e, 6.0 * o - by_o + extra_odd * o


def restrict_fine(even, odd):
    both = even + odd
    both = jnp.sum(both.reshape((both.shape[0] // 2, 2) + both.shape[1:]), axis=1)
    return 0.125 * (both + swap(both, 1, 2))


def double_rows(value):
    wide = jnp.broadcast_to(value[:, None], (value.shape[0], 2) + value.shape[1:])
    return wide.reshape((2 * value.shape[0],) + value.shape[1:])


def apply_one(value, extra):
    v = value[1:-1]
    k = iota(v.shape, 1)
    beside = jnp.where(k > 0, roll(v, 1, 1), 0.0) + jnp.where(k < 7, roll(v, -1, 1), 0.0)
    beside = beside + value[2:] + value[:-2] + along_y(v, 2)
    return 0.25 * (6.0 * v - beside) + extra * v


def pack_two(value, first_lane):
    pairs = jnp.sum(value.reshape((2, 2) + value.shape[1:]), axis=1)
    pairs = pairs + swap(pairs, 1, 1)
    rows = jnp.where(iota(pairs.shape[1:], 0) % 2 == 0, pairs[0], pairs[1])
    shape = (LANES, 128)
    matrix = jnp.where(iota(shape, 0) // 4 + first_lane == iota(shape, 1), 0.0625, 0.0)
    return jnp.dot(rows, matrix.astype(F32), precision=lax.Precision.HIGHEST)


def split_two(ref, wide):
    return [[ref[pl.ds(2 * z + x, wide, stride=8), :] for z in range(4)] for x in range(2)]


def add(terms):
    return functools.reduce(lambda a, b: a + b, terms)


def before(value):
    return jnp.where(iota(value.shape, 0) > 0, roll(value, 1, 0), 0.0)


def after(value):
    last = value.shape[0] - 1
    return jnp.where(iota(value.shape, 0) < last, roll(value, -1, 0), 0.0)


def each(function, *lists):
    return [[function(*(a[x][z] for a in lists)) for z in range(4)] for x in range(2)]


def apply_two(v, d):
    out = [[], []]
    for x in range(2):
        for z in range(4):
            terms = [along_y(v[x][z], 1), v[1 - x][z]]
            terms += [before(v[1][z])] if x == 0 else [after(v[0][z])]
            terms += [v[x][k] for k in (z - 1, z + 1) if 0 <= k < 4]
            out[x].append(0.0625 * (6.0 * v[x][z] - add(terms)) + d[x][z] * v[x][z])
    return out


def restrict_two(v):
    out = []
    for z in range(2):
        total = v[0][2 * z] + v[0][2 * z + 1] + v[1][2 * z] + v[1][2 * z + 1]
        out.append(0.125 * (total + swap(total, 1, 1)))
    return out


def apply_three(v, d):
    out = []
    for z in range(2):
        beside = before(v[z]) + after(v[z]) + v[1 - z] + along_y(v[z], 2)
        out.append(0.015625 * (6.0 * v[z] - beside) + d[z] * v[z])
    return out


def solve_coarse(r2, d2, mine, narrow):
    shape = r2[0][0].shape
    lane = iota(shape, 1) % 64
    column = 32 * mine + jnp.where(lane < 48, lane, lane - 64)
    inside = (column >= 0) & (column < 32 * narrow)
    i2 = each(lambda d: jnp.where(inside, OMEGA / (0.375 + d), 0.0), d2)
    c2 = each(lambda i, r: i * r, i2, r2)
    left = each(lambda r, a: r - a, r2, apply_two(c2, d2))
    r3, d3 = restrict_two(left), restrict_two(d2)
    i3 = [jnp.where(inside, OMEGA / (0.09375 + d), 0.0) for d in d3]
    e3 = [i * r for i, r in zip(i3, r3)]
    for _ in range(3):
        a3 = apply_three(e3, d3)
        e3 = [e + i * (r - a) for e, i, r, a in zip(e3, i3, r3, a3)]
    one = inside[:1]
    for z in range(2):
        weight = jnp.where(one, jnp.sum(d3[z], axis=0, keepdims=True), 1.0)
        line = jnp.where(one, jnp.sum(r3[z], axis=0, keepdims=True) / weight, 0.0)
        e3[z] = e3[z] + line
    e2 = [[c2[x][z] + e3[z // 2] for z in range(4)] for x in range(2)]
    return each(lambda e, i, r, a: e + i * (r - a), e2, i2, r2, apply_two(e2, d2))


def rise(e2, scratch, at, r1, d1, i1):
    wide = e2[0][0].shape[0]
    blank = jnp.zeros((8, 128), F32)
    for x in range(2):
        for z in range(4):
            scratch[2 * z + x, 0:8, :] = blank
            scratch[2 * z + x, 8 + wide : 16 + wide, :] = blank
            scratch[2 * z + x, 8 : 8 + wide, :] = e2[x][z]
    pair = iota((8, 128), 0) // 2
    rows = []
    for x, step in ((1, -1), (0, 0), (1, 0), (0, 1)):
        tile = blank
        for z in range(4):
            line = scratch[2 * z + x, pl.ds(at + (8 + step), 1), :]
            tile = jnp.where(pair == z, jnp.broadcast_to(line, (8, 128)), tile)
        rows.append(tile)
    shape = (128, LANES)
    matrix = jnp.where(iota(shape, 0) == iota(shape, 1) // 4, 1.0, 0.0).astype(F32)
    spread = jnp.dot(jnp.concatenate(rows, 0), matrix, precision=lax.Precision.HIGHEST)
    e1 = i1 * r1 + double_rows(spread.reshape(4, 8, LANES))
    return e1[1:-1] + i1[1:-1] * (r1[1:-1] - apply_one(e1, d1[1:-1]))


def finish(e1, source, extra, inverse):
    up = double_rows(e1)
    e = [inverse[p, 3:15] * source[p, 3:15] + up for p in range(2)]
    a = apply_fine(e[0], e[1], extra[0, 4:14], extra[1, 4:14])
    z = [e[p][1:-1] + inverse[p, 4:14] * (source[p, 4:14] - a[p]) for p in range(2)]
    q = apply_fine(z[0], z[1], extra[0, 5:13], extra[1, 5:13])
    return [v[1:-1] for v in z], q


def descend(source, extra, inverse):
    c = [i * s for i, s in zip(inverse, source)]
    a = apply_fine(c[0], c[1], extra[0][1:-1], extra[1][1:-1])
    left = [source[p][1:-1] - a[p] for p in range(2)]
    return restrict_fine(left[0], left[1])


def leave_one(r1, d1, i1):
    c1 = (i1 * r1)[1:7]
    return r1[2:6] - apply_one(c1, d1[2:6])


def total(a, b):
    return jnp.sum(jnp.sum(a[0] * b[0] + a[1] * b[1], axis=0), keepdims=True)


def place(values, shape, first):
    lane = iota(shape, len(shape) - 1)
    out = jnp.zeros(shape, F32)
    for i, v in enumerate(values):
        out = jnp.where(lane == first + i, v, out)
    return out


def prepare_kernel(right, capacity, phase, flags, own, low, high):
    half = iota((8, 128), 1) < 64
    for p in range(2):
        for x in range(OWN):
            rows = pl.ds(x + 8 * p, 8, stride=16)
            r = right[rows, :]
            weight = jnp.where(phase[rows, :] == 1, 4.0, 1.0)
            d = 0.05 * capacity[rows, :] * weight + 0.5 * flags[rows, :].astype(F32)
            first = jnp.where(half, r, roll(d, 64, 1))
            second = jnp.where(half, roll(r, 64, 1), d)
            for side, value in ((0, first), (1, second)):
                own[side, p, x] = value
                if x < HALO:
                    low[side, p, x] = value
                if x >= OWN - HALO:
                    high[side, p, x - (OWN - HALO)] = value


def down_kernel(wide, narrow, a, b, from_left, from_right, r0, d0, i0, r1, d1, i1, send):
    me_w, me_n = lax.axis_index("wide"), lax.axis_index("narrow")
    shape = (EXT, 8, 128)
    half = iota(shape, 2) < 64
    fine = (EXT, 8, LANES)
    lane, row = iota(fine, 2), iota(fine, 0)
    column = 128 * me_n + jnp.where(lane < 192, lane, lane - 256)
    line = 8 * me_w - HALO + row
    inside = (column >= 0) & (column < 128 * narrow) & (line >= 0) & (line < 8 * wide)
    source, extra, inverse = [], [], []
    for p in range(2):
        fa, fb, fl, fr = a[p], b[p], from_left[p], from_right[p]
        own_r = jnp.where(half, fa, roll(fb, 64, 2))
        own_d = jnp.where(half, roll(fa, 64, 2), fb)
        far_r = jnp.where(half, fr, roll(fl, 64, 2))
        far_d = jnp.where(half, roll(fr, 64, 2), fl)
        source.append(jnp.concatenate([own_r, far_r], axis=2))
        extra.append(jnp.concatenate([own_d, far_d], axis=2))
        inverse.append(jnp.where(inside, OMEGA / (6.0 + extra[p]), 0.0))
        r0[p] = source[p]
        d0[p] = extra[p]
        i0[p] = inverse[p]
    vr1 = descend(source, extra, inverse)
    vd1 = restrict_fine(extra[0][1:-1], extra[1][1:-1])
    line = 4 * me_w - 2 + iota(vd1.shape, 0)
    inside = (column[:8] >= 0) & (column[:8] < 128 * narrow) & (line >= 0) & (line < 4 * wide)
    vi1 = jnp.where(inside, OMEGA / (1.5 + vd1), 0.0)
    r1[...] = vr1
    d1[...] = vd1
    i1[...] = vi1
    send[...] = pack_two(leave_one(vr1, vd1, vi1), 0) + pack_two(vd1[2:6], 64)


def both_halves(tile):
    half = iota(tile.shape, 1) < 64
    other = roll(tile, 64, 1)
    return jnp.where(half, tile, other), jnp.where(half, other, tile)


def up_kernel(wide, narrow, got, r0, d0, i0, r1, d1, i1, z, q, low, high, sums, scratch):
    me_w, me_n = lax.axis_index("wide"), lax.axis_index("narrow")
    tiles = split_two(got, wide)
    r2 = each(lambda t: both_halves(t)[0], tiles)
    d2 = each(lambda t: both_halves(t)[1], tiles)
    e2 = solve_coarse(r2, d2, me_n, narrow)
    e1 = rise(e2, scratch, me_w, r1[...], d1[...], i1[...])
    vz, vq = finish(e1, r0, d0, i0)
    for p in range(2):
        z[p] = vz[p][:, :, :128]
        q[p] = vq[p]
        low[p] = vq[p][:HALO]
        high[p] = vq[p][OWN - HALO :]
    mine = [v[:, :, :128] for v in vz]
    image = [v[:, :, :128] for v in vq]
    residual = [r0[p, HALO : HALO + OWN, :, :128] for p in range(2)]
    sums[...] = place([total(residual, mine), total(mine, image)], (8, 128), 64)


def down_again_kernel(q, low, high, d0, i0, d1, i1, sums, source, r1, send):
    full, extra, inverse = [], [], []
    for p in range(2):
        full.append(jnp.concatenate([low[p], q[p], high[p]], axis=0))
        extra.append(d0[p])
        inverse.append(i0[p])
        source[p] = full[p]
    vr1 = descend(full, extra, inverse)
    r1[...] = vr1
    send[...] = pack_two(leave_one(vr1, d1[...], i1[...]), 0) + sums[...]


def window_kernel(narrow, got, send):
    me = lax.axis_index("narrow")
    lane = iota((8, 128), 1)
    right = got[jnp.minimum(me + 1, narrow - 1)]
    left = got[jnp.maximum(me - 1, 0)]
    tile = jnp.where(lane < 32, got[me], jnp.where(lane < 48, roll(right, 32, 1), roll(left, 32, 1)))
    scalars = jnp.sum(got[...], axis=0)
    send[...] = jnp.where(lane < 64, tile, scalars)


def up_again_kernel(wide, narrow, got, first, source, r0, d0, i0, r1, d1, i1, z0, z1, image1, res1, sums, known, scratch):
    me_w, me_n = lax.axis_index("wide"), lax.axis_index("narrow")
    r2 = each(lambda t: both_halves(t)[0], split_two(got, wide))
    d2 = each(lambda t: both_halves(t)[1], split_two(first, wide))
    e2 = solve_coarse(r2, d2, me_n, narrow)
    e1 = rise(e2, scratch, me_w, r1[...], d1[...], i1[...])
    vw, vy = finish(e1, source, d0, i0)
    scalars = jnp.sum(got[pl.ds(0, wide, stride=8), :], axis=0, keepdims=True)
    lane = iota((1, 128), 1)
    rho = jnp.sum(jnp.where(lane == 64, scalars, 0.0), keepdims=True)
    curve = jnp.sum(jnp.where(lane == 65, scalars, 0.0), keepdims=True)
    alpha = (rho / curve).reshape(1, 1, 1)
    own = slice(HALO, HALO + OWN)
    vz0 = [z0[p] for p in range(2)]
    vq0 = [source[p, own, :, :128] for p in range(2)]
    vz1 = [vz0[p] - alpha * vw[p][:, :, :128] for p in range(2)]
    vi1 = [vq0[p] - alpha * vy[p][:, :, :128] for p in range(2)]
    vr1 = [r0[p, own, :, :128] - alpha * vq0[p] for p in range(2)]
    for p in range(2):
        z1[p] = vz1[p]
        image1[p] = vi1[p]
        res1[p] = vr1[p]
    cross = total(vz1, vq0) + total(vz0, vi1)
    sums[...] = place([total(vr1, vz1), total(vz1, vi1), cross], (1, 128), 0)
    known[...] = place([rho, curve], (1, 128), 0)


def last_kernel(got, known, z0, source, z1, image1, res1, field, residual):
    scalars = jnp.sum(got[...], axis=0, keepdims=True)
    lane = iota((1, 128), 1)

    def pick(vector, at):
        return jnp.sum(jnp.where(lane == at, vector, 0.0), keepdims=True)

    rho, curve = pick(known[...], 0), pick(known[...], 1)
    rho_next, square, cross = (pick(scalars, i) for i in range(3))
    alpha = rho / curve
    beta = rho_next / rho
    alpha_next = rho_next / (square + beta * cross + beta * beta * curve)
    for p in range(2):
        for x in range(OWN):
            rows = pl.ds(x + 8 * p, 8, stride=16)
            z, q = z0[p, x], source[p, HALO + x, :, :128]
            field[rows, :] = alpha * z + alpha_next * (z1[p, x] + beta * z)
            residual[rows, :] = res1[p, x] - alpha_next * (image1[p, x] + beta * q)


def call(kernel, outs, *args, scratch=()):
    return pl.pallas_call(
        kernel,
        out_shape=tuple(jax.ShapeDtypeStruct(s, F32) for s in outs),
        in_specs=[pl.BlockSpec(memory_space=pltpu.VMEM)] * len(args),
        out_specs=tuple(pl.BlockSpec(memory_space=pltpu.VMEM) for _ in outs),
        scratch_shapes=scratch,
        compiler_params=pltpu.CompilerParams(vmem_limit_bytes=40 * 1024 * 1024),
    )(*args)


def gathered(array, axis):
    peers = lax.axis_size(axis)
    slots = jnp.broadcast_to(array[None], (peers,) + array.shape)
    return lax.all_to_all(slots, axis, 0, 0)


def to_next(array, axis):
    n = lax.axis_size(axis)
    return lax.ppermute(array, axis, [(i, i + 1) for i in range(n - 1)])


def to_previous(array, axis):
    n = lax.axis_size(axis)
    return lax.ppermute(array, axis, [(i + 1, i) for i in range(n - 1)])


def on_device(right_side, capacity, phase, mold_flags):
    wide, narrow = lax.axis_size("wide"), lax.axis_size("narrow")
    flat = [v.reshape(128, 128) for v in (right_side, capacity, phase, mold_flags)]
    edge = (2, 2, HALO, 8, 128)
    own, low, high = call(prepare_kernel, [(2, 2, OWN, 8, 128), edge, edge], *flat)
    below, above = to_next(high, "wide"), to_previous(low, "wide")
    a = jnp.concatenate([below[0], own[0], above[0]], axis=1)
    b = jnp.concatenate([below[1], own[1], above[1]], axis=1)
    from_left, from_right = to_next(b, "narrow"), to_previous(a, "narrow")
    fine, coarse = (2, EXT, 8, LANES), (8, 8, LANES)
    r0, d0, i0, r1, d1, i1, send = call(
        functools.partial(down_kernel, wide, narrow),
        [fine, fine, fine, coarse, coarse, coarse, (8, 128)],
        a, b, from_left, from_right,
    )
    first = gathered(send, "wide").reshape(8 * wide, 128)
    block = (2, OWN, 8, 128)
    band = (2, HALO, 8, LANES)
    scratch = [pltpu.VMEM((8, wide + 16, 128), F32)]
    z0, q0, low, high, sums = call(
        functools.partial(up_kernel, wide, narrow),
        [block, (2, OWN, 8, LANES), band, band, (8, 128)],
        first, r0, d0, i0, r1, d1, i1,
        scratch=scratch,
    )
    below, above = to_next(high, "wide"), to_previous(low, "wide")
    source, r1, send = call(
        down_again_kernel, [fine, coarse, (8, 128)], q0, below, above, d0, i0, d1, i1, sums
    )
    (send,) = call(functools.partial(window_kernel, narrow), [(8, 128)], gathered(send, "narrow"))
    second = gathered(send, "wide").reshape(8 * wide, 128)
    z1, image1, res1, sums, known = call(
        functools.partial(up_again_kernel, wide, narrow),
        [block, block, block, (1, 128), (1, 128)],
        second, first, source, r0, d0, i0, r1, d1, i1, z0,
        scratch=scratch,
    )
    sums = jnp.sum(gathered(sums, "narrow"), axis=0)
    third = gathered(sums, "wide").reshape(wide, 128)
    field, residual = call(
        last_kernel, [(128, 128), (128, 128)], third, known, z0, source, z1, image1, res1
    )
    return field.reshape(right_side.shape), residual.reshape(right_side.shape)


def solution(mesh):
    spec = P(None, "wide", "narrow")
    return jax.shard_map(
        on_device, mesh=mesh, in_specs=(spec,) * 4, out_specs=(spec, spec), check_vma=False
    )
```

time: 859 us -> 144 us (0.17)
  blocking collectives: 511 us -> 106 us
  starting transfers between devices: 215 us -> 18 us
  waiting for transfers between devices: 59.7 us -> 10.4 us
  local copies, waits for them, and re-layouts: 39.2 us -> 3.45 us
  other arithmetic: 25.1 us -> 0.04 us
    psum x3 -> x0, blocking collectives: 313 us -> none  [the longest x2 210 us: inner_sum(): return lax.psum(jnp.sum(first * second), ('wide', 'narrow'))]
    all_gather x3 -> x0, blocking collectives: 198 us -> none  [the longest x2 129 us: vcycle(): whole = lax.all_gather(left, 'wide', axis=1, tiled=True)]
    ppermute x60 -> x6, starting transfers between devices: 215 us -> 18 us  [the longest x3 9.26 us: to_previous(): return lax.ppermute(array, axis, [(i + 1, i) for i in range(n - 1)])]
    all_to_all x0 -> x5, blocking collectives: none -> 106 us  [gathered(): return lax.all_to_all(slots, axis, 0, 0)]
    ppermute x60 -> x6, waiting for transfers between devices: 59.7 us -> 10.4 us  [the longest x3 7.7 us: to_previous(): return lax.ppermute(array, axis, [(i + 1, i) for i in range(n - 1)])]
    reshape x18 -> x0, local copies, waits for them, and re-layouts: 35.6 us -> none  [the longest x8 34.5 us: restrict(): field.reshape(zc // 2, 2, xc // 2, 2, yc // 2, 2).mean(axis=(1, 3, 5))]
    reduce_sum x14 -> x1, other arithmetic: 18.1 us -> 0.02 us  [on_device(): sums = jnp.sum(gathered(sums, 'narrow'), axis=0)]
  transfers between devices with their start and end apart: 60 -> 6, of which waited for: 29 -> 5; matrix products, arithmetic and copies ran while one was open for 2% -> 0% of each run, Pallas kernels for 0% -> 0%
where the time goes in v2:
time: 144 us; the launch traced here: 143 us
  blocking collectives  106 us (74%)
  starting transfers between devices  18 us (12%)
  waiting for transfers between devices  10.4 us (7%)
  Pallas kernels  5.25 us (4%)
  local copies, waits for them, and re-layouts  3.45 us (2%)
    all_to_all x5, blocking collectives, gathered(): return lax.all_to_all(slots, axis, 0, 0)  106 us
    ppermute x3, starting transfers between devices, to_previous(): return lax.ppermute(array, axis, [(i + 1, i) for i in range(n - 1)])  9.26 us
    ppermute x3, starting transfers between devices, to_next(): return lax.ppermute(array, axis, [(i, i + 1) for i in range(n - 1)])  8.71 us
    ppermute x3, waiting for transfers between devices, to_previous(): return lax.ppermute(array, axis, [(i + 1, i) for i in range(n - 1)])  7.7 us
    pallas_call x7, Pallas kernels, call(): pl.pallas_call(kernel, out_shape=tuple((jax.ShapeDtypeStruct(s, F32) for...  5.25 us
    unnamed x8, local copies, waits for them, and re-layouts  3.35 us
  transfers between devices with their start and end apart: 6, of which 5 were waited for; matrix products, arithmetic and copies ran while one was open for 0% of the time, Pallas kernels for 0%

profile of v2, /device:TPU:1, one launch (start us, length us, event | category | flops | bytes accessed | tf_op | source)
XLA Modules:
  0.0 143.4 jit_solution(6037775998834071742)
XLA Ops:
  0.6 0.8 copy-done
  1.5 0.8 copy-done.1
  2.3 0.8 copy-done.2
  3.2 0.8 copy-done.3
  4.2 4.4 %collective-permute-start = (f32[2,2,5,8,128]{4,3,2,1,0:T(8,128)S(1)}, f32[2,2,5,8,128]{4,3,2,1,0:T(8,128)S(1)}, u32[]{:S(2)}, u32[]{:S(2)}) collective-permute-start(f32[2,2,5,8,128]{4,3,2,1,0:T(8,128)S(1)} %get-tuple-element.27), channel_id=1, source_target_pairs={{0,8},{8,16},{16,24},{24,32},{32,40},{40,48},{48,56},{56,64},{64,7... | collective-permute-start | bytes 245768 | tf_op jit(solution)/shard_map/ppermute | solution.py:364
  8.5 1.3 collective-permute-start.1
  10.0 3.9 %collective-permute-done.1 = f32[2,2,5,8,128]{4,3,2,1,0:T(8,128)S(1)} collective-permute-done((f32[2,2,5,8,128]{4,3,2,1,0:T(8,128)S(1)}, f32[2,2,5,8,128]{4,3,2,1,0:T(8,128)S(1)}, u32[]{:S(2)}, u32[]{:S(2)}) %collective-permute-start.1) | collective-permute-done | bytes 81952 | tf_op jit(solution)/shard_map/ppermute | solution.py:369
  13.9 6.7 %collective-permute-start.3 = (f32[2,18,8,128]{3,2,1,0:T(8,128)S(1)}, f32[2,18,8,128]{3,2,1,0:T(8,128)S(1)}, u32[]{:S(2)}, u32[]{:S(2)}) collective-permute-start(f32[2,18,8,128]{3,2,1,0:T(8,128)S(1)} %pad_maximum_fusion.a), channel_id=1, source_target_pairs={{1,0},{2,1},{3,2},{4,3},{5,4},{6,5},{7,6},{9,8},{10,9},{11,10},{12... | collective-permute-start | bytes 442376 | tf_op jit(solution)/shard_map/ppermute | solution.py:369
  20.6 1.9 %collective-permute-start.2 = (f32[2,18,8,128]{3,2,1,0:T(8,128)S(1)}, f32[2,18,8,128]{3,2,1,0:T(8,128)S(1)}, u32[]{:S(2)}, u32[]{:S(2)}) collective-permute-start(f32[2,18,8,128]{3,2,1,0:T(8,128)S(1)} %pad_maximum_fusion.1.b), channel_id=1, source_target_pairs={{0,1},{1,2},{2,3},{3,4},{4,5},{5,6},{6,7},{8,9},{9,10},{10,11},{11... | collective-permute-start | bytes 442376 | tf_op jit(solution)/shard_map/ppermute | solution.py:364
  22.6 2.1 %collective-permute-done.2.from_left = f32[2,18,8,128]{3,2,1,0:T(8,128)S(1)} collective-permute-done((f32[2,18,8,128]{3,2,1,0:T(8,128)S(1)}, f32[2,18,8,128]{3,2,1,0:T(8,128)S(1)}, u32[]{:S(2)}, u32[]{:S(2)}) %collective-permute-start.2) | collective-permute-done | bytes 147488 | tf_op jit(solution)/shard_map/ppermute | solution.py:364
  24.6 0.7 shard_map.60
  25.3 36.6 %all_to_all.25 = f32[64,8,128]{2,1,0:T(8,128)S(1)} all-to-all(f32[64,8,128]{2,1,0:T(8,128)S(1)} %broadcast_in_dim.12), channel_id=1, replica_groups=mesh['wide'=64,'narrow'=8] {'wide'}, dimensions={0} | all-to-all | bytes 524288 | tf_op jit(solution)/shard_map/all_to_all | solution.py:359
  62.0 1.5 %shard_map.61 = (f32[2,8,8,128]{3,2,1,0:T(8,128)S(1)}, f32[2,8,8,256]{3,2,1,0:T(8,128)S(1)}, f32[2,5,8,256]{3,2,1,0:T(8,128)S(1)}, f32[2,5,8,256]{3,2,1,0:T(8,128)S(1)}, f32[8,128]{1,0:T(8,128)S(1)}) custom-call(f32[512,128]{1,0:T(8,128)S(1)} %bitcast.23, f32[2,18,8,256]{3,2,1,0:T(8,128)S(1)} %get-tuple-element.31.r0, ...), custom_call_target="tpu_custom_call" | custom-call | tf_op jit(solution)/shard_map/pallas_call | solution.py:346
  63.5 2.4 %collective-permute-start.4 = (f32[2,5,8,256]{3,2,1,0:T(8,128)S(1)}, f32[2,5,8,256]{3,2,1,0:T(8,128)S(1)}, u32[]{:S(2)}, u32[]{:S(2)}) collective-permute-start(f32[2,5,8,256]{3,2,1,0:T(8,128)S(1)} %get-tuple-element.38), channel_id=1, source_target_pairs={{0,8},{8,16},{16,24},{24,32},{32,40},{40,48},{48,56},{56,64},{64,7... | collective-permute-start | bytes 245768 | tf_op jit(solution)/shard_map/ppermute | solution.py:364
  65.9 1.3 collective-permute-start.5
  67.2 0.5 collective-permute-done.4.low
  67.7 3.8 %collective-permute-done.5.high = f32[2,5,8,256]{3,2,1,0:T(8,128)S(1)} collective-permute-done((f32[2,5,8,256]{3,2,1,0:T(8,128)S(1)}, f32[2,5,8,256]{3,2,1,0:T(8,128)S(1)}, u32[]{:S(2)}, u32[]{:S(2)}) %collective-permute-start.5) | collective-permute-done | bytes 81952 | tf_op jit(solution)/shard_map/ppermute | solution.py:369
  71.5 0.5 shard_map.62
  72.0 11.3 %all_to_all.26.got = f32[8,8,128]{2,1,0:T(8,128)S(1)} all-to-all(f32[8,8,128]{2,1,0:T(8,128)S(1)} %broadcast_in_dim.13), channel_id=1, replica_groups=mesh['wide'=64,'narrow'=8] {'narrow'}, dimensions={0} | all-to-all | bytes 65536 | tf_op jit(solution)/shard_map/all_to_all | solution.py:359
  83.4 28.4 %all_to_all.27 = f32[64,8,128]{2,1,0:T(8,128)S(1)} all-to-all(f32[64,8,128]{2,1,0:T(8,128)S(1)} %broadcast_in_dim.14), channel_id=1, replica_groups=mesh['wide'=64,'narrow'=8] {'wide'}, dimensions={0} | all-to-all | bytes 524288 | tf_op jit(solution)/shard_map/all_to_all | solution.py:359
  111.8 1.6 %shard_map.64 = (f32[2,8,8,128]{3,2,1,0:T(8,128)S(1)}, f32[2,8,8,128]{3,2,1,0:T(8,128)S(1)}, f32[2,8,8,128]{3,2,1,0:T(8,128)S(1)}, f32[1,128]{1,0:T(1,128)S(1)}, f32[1,128]{1,0:T(1,128)S(1)}) custom-call(f32[512,128]{1,0:T(8,128)S(1)} %bitcast.25, f32[512,128]{1,0:T(8,128)S(1)} %bitcast.24, f32[2,18,8,256]{3,2,1,0:T(8,128)S(1)} %get-tuple-element.42.source, ...), custom_call_target="tpu_custom_call" | custom-call | tf_op jit(solution)/shard_map/pallas_call | solution.py:346
  113.4 9.9 %all_to_all.28 = f32[8,1,128]{2,1,0:T(1,128)S(1)} all-to-all(f32[8,1,128]{2,1,0:T(1,128)S(1)} %broadcast_in_dim.16), channel_id=1, replica_groups=mesh['wide'=64,'narrow'=8] {'narrow'}, dimensions={0} | all-to-all | bytes 8192 | tf_op jit(solution)/shard_map/all_to_all | solution.py:359
  123.4 19.2 %all_to_all.29 = f32[64,1,128]{2,1,0:T(1,128)S(1)} all-to-all(f32[64,1,128]{2,1,0:T(1,128)S(1)} %broadcast_in_dim.17), channel_id=1, replica_groups=mesh['wide'=64,'narrow'=8] {'wide'}, dimensions={0} | all-to-all | bytes 65536 | tf_op jit(solution)/shard_map/all_to_all | solution.py:359
  142.6 0.8 shard_map.65
  (19 shorter events, 0.5 us)
Async XLA Ops:
  0.6 0.8 copy-start
  1.5 0.8 copy-start.1
  2.3 0.8 copy-start.2
  3.2 0.8 copy-start.3
  4.2 5.8 %collective-permute-start = (f32[2,2,5,8,128]{4,3,2,1,0:T(8,128)S(1)}, f32[2,2,5,8,128]{4,3,2,1,0:T(8,128)S(1)}, u32[]{:S(2)}, u32[]{:S(2)}) collective-permute-start(f32[2,2,5,8,128]{4,3,2,1,0:T(8,128)S(1)} %get-tuple-element.27), channel_id=1, source_target_pairs={{0,8},{8,16},{16,24},{24,32},{32,40},{40,48},{48,56},{56,64},{64,7... | collective-permute-start | bytes 245768 | tf_op jit(solution)/shard_map/ppermute | solution.py:364
  8.5 5.4 %collective-permute-start.1 = (f32[2,2,5,8,128]{4,3,2,1,0:T(8,128)S(1)}, f32[2,2,5,8,128]{4,3,2,1,0:T(8,128)S(1)}, u32[]{:S(2)}, u32[]{:S(2)}) collective-permute-start(f32[2,2,5,8,128]{4,3,2,1,0:T(8,128)S(1)} %get-tuple-element.29), channel_id=1, source_target_pairs={{8,0},{16,8},{24,16},{32,24},{40,32},{48,40},{56,48},{64,56},{72,6... | collective-permute-start | bytes 245768 | tf_op jit(solution)/shard_map/ppermute | solution.py:369
  13.9 8.6 %collective-permute-start.3 = (f32[2,18,8,128]{3,2,1,0:T(8,128)S(1)}, f32[2,18,8,128]{3,2,1,0:T(8,128)S(1)}, u32[]{:S(2)}, u32[]{:S(2)}) collective-permute-start(f32[2,18,8,128]{3,2,1,0:T(8,128)S(1)} %pad_maximum_fusion.a), channel_id=1, source_target_pairs={{1,0},{2,1},{3,2},{4,3},{5,4},{6,5},{7,6},{9,8},{10,9},{11,10},{12... | collective-permute-start | bytes 442376 | tf_op jit(solution)/shard_map/ppermute | solution.py:369
  20.6 4.0 %collective-permute-start.2 = (f32[2,18,8,128]{3,2,1,0:T(8,128)S(1)}, f32[2,18,8,128]{3,2,1,0:T(8,128)S(1)}, u32[]{:S(2)}, u32[]{:S(2)}) collective-permute-start(f32[2,18,8,128]{3,2,1,0:T(8,128)S(1)} %pad_maximum_fusion.1.b), channel_id=1, source_target_pairs={{0,1},{1,2},{2,3},{3,4},{4,5},{5,6},{6,7},{8,9},{9,10},{10,11},{11... | collective-permute-start | bytes 442376 | tf_op jit(solution)/shard_map/ppermute | solution.py:364
  63.5 4.2 %collective-permute-start.4 = (f32[2,5,8,256]{3,2,1,0:T(8,128)S(1)}, f32[2,5,8,256]{3,2,1,0:T(8,128)S(1)}, u32[]{:S(2)}, u32[]{:S(2)}) collective-permute-start(f32[2,5,8,256]{3,2,1,0:T(8,128)S(1)} %get-tuple-element.38), channel_id=1, source_target_pairs={{0,8},{8,16},{16,24},{24,32},{32,40},{40,48},{48,56},{56,64},{64,7... | collective-permute-start | bytes 245768 | tf_op jit(solution)/shard_map/ppermute | solution.py:364
  65.9 5.6 %collective-permute-start.5 = (f32[2,5,8,256]{3,2,1,0:T(8,128)S(1)}, f32[2,5,8,256]{3,2,1,0:T(8,128)S(1)}, u32[]{:S(2)}, u32[]{:S(2)}) collective-permute-start(f32[2,5,8,256]{3,2,1,0:T(8,128)S(1)} %get-tuple-element.39), channel_id=1, source_target_pairs={{8,0},{16,8},{24,16},{32,24},{40,32},{48,40},{56,48},{64,56},{72,6... | collective-permute-start | bytes 245768 | tf_op jit(solution)/shard_map/ppermute | solution.py:369

commit v3 on v2

--- a/solution.py
+++ b/solution.py
@@ -13,6 +13,8 @@
 EXT = OWN + 2 * HALO
 LANES = 256
 F32 = jnp.float32
+DEEP = 16
+SUMS = 44
 
 
 def iota(shape, dim):
@@ -68,6 +70,18 @@
     shape = (LANES, 128)
     matrix = jnp.where(iota(shape, 0) // 4 + first_lane == iota(shape, 1), 0.0625, 0.0)
     return jnp.dot(rows, matrix.astype(F32), precision=lax.Precision.HIGHEST)
+
+
+def pack_rows(value, scratch):
+    pairs = jnp.sum(value.reshape((2, 2) + value.shape[1:]), axis=1)
+    pairs = pairs + swap(pairs, 1, 1)
+    shape = (LANES, 128)
+    out = jnp.zeros((8, 128), F32)
+    for x in range(2):
+        matrix = jnp.where(iota(shape, 0) // 4 + 64 * x == iota(shape, 1), 0.0625, 0.0)
+        out = out + jnp.dot(pairs[x], matrix.astype(F32), precision=lax.Precision.HIGHEST)
+    scratch[...] = out
+    return scratch[pl.ds(0, 4, stride=2), :]
 
 
 def split_two(ref, wide):
@@ -197,7 +211,13 @@
     return out
 
 
-def prepare_kernel(right, capacity, phase, flags, own, low, high):
+def prepare_kernel(right_in, capacity_in, phase_in, flags_in, own, low, high, right, capacity, phase, flags, done):
+    pairs = ((right_in, right), (capacity_in, capacity), (phase_in, phase), (flags_in, flags))
+    copies = [pltpu.make_async_copy(a, b, done.at[i]) for i, (a, b) in enumerate(pairs)]
+    for copy in copies:
+        copy.start()
+    for copy in copies:
+        copy.wait()
     half = iota((8, 128), 1) < 64
     for p in range(2):
         for x in range(OWN):
@@ -270,10 +290,10 @@
     mine = [v[:, :, :128] for v in vz]
     image = [v[:, :, :128] for v in vq]
     residual = [r0[p, HALO : HALO + OWN, :, :128] for p in range(2)]
-    sums[...] = place([total(residual, mine), total(mine, image)], (8, 128), 64)
-
-
-def down_again_kernel(q, low, high, d0, i0, d1, i1, sums, source, r1, send):
+    sums[...] = place([total(residual, mine), total(mine, image)], (8, 128), SUMS)
+
+
+def down_again_kernel(q, low, high, d0, i0, d1, i1, sums, source, r1, send, scratch):
     full, extra, inverse = [], [], []
     for p in range(2):
         full.append(jnp.concatenate([low[p], q[p], high[p]], axis=0))
@@ -282,30 +302,48 @@
         source[p] = full[p]
     vr1 = descend(full, extra, inverse)
     r1[...] = vr1
-    send[...] = pack_two(leave_one(vr1, d1[...], i1[...]), 0) + sums[...]
-
-
-def window_kernel(narrow, got, send):
+    rows = pack_rows(leave_one(vr1, d1[...], i1[...]), scratch)
+    lane = iota(rows.shape, 1)
+    send[...] = jnp.where((lane == SUMS) | (lane == SUMS + 1), sums[0:4, :], rows)
+
+
+def window_kernel(narrow, got, send, own, right, left):
     me = lax.axis_index("narrow")
-    lane = iota((8, 128), 1)
-    right = got[jnp.minimum(me + 1, narrow - 1)]
-    left = got[jnp.maximum(me - 1, 0)]
-    tile = jnp.where(lane < 32, got[me], jnp.where(lane < 48, roll(right, 32, 1), roll(left, 32, 1)))
-    scalars = jnp.sum(got[...], axis=0)
-    send[...] = jnp.where(lane < 64, tile, scalars)
+    for y in range(got.shape[0] // narrow):
+        rows = slice(4 * y, 4 * y + 4)
+        own[rows, :] = got[y * narrow + me]
+        right[rows, :] = got[y * narrow + jnp.minimum(me + 1, narrow - 1)]
+        left[rows, :] = got[y * narrow + jnp.maximum(me - 1, 0)]
+    lane = iota(own.shape, 1)
+    cell = lane % 64
+    halo = jnp.where(cell < 48, roll(right[...], 32, 1), roll(left[...], 32, 1))
+    tile = jnp.where(cell < 32, own[...], halo)
+    scalars = jnp.sum(jnp.sum(got[...], axis=0), axis=0, keepdims=True) * 0.25
+    send[...] = jnp.where((lane == SUMS) | (lane == SUMS + 1), scalars, tile)
+
+
+def split_deep(ref, wide):
+    sides = [[], []]
+    across = wide // DEEP
+    for z in range(4):
+        rows = [ref[pl.ds(4 * y + z, DEEP, stride=4 * across), :] for y in range(across)]
+        for side, value in zip(sides, both_halves(jnp.concatenate(rows, 0))):
+            side.append(value)
+    return sides
 
 
 def up_again_kernel(wide, narrow, got, first, source, r0, d0, i0, r1, d1, i1, z0, z1, image1, res1, sums, known, scratch):
     me_w, me_n = lax.axis_index("wide"), lax.axis_index("narrow")
-    r2 = each(lambda t: both_halves(t)[0], split_two(got, wide))
+    r2 = split_deep(got, wide)
     d2 = each(lambda t: both_halves(t)[1], split_two(first, wide))
     e2 = solve_coarse(r2, d2, me_n, narrow)
     e1 = rise(e2, scratch, me_w, r1[...], d1[...], i1[...])
     vw, vy = finish(e1, source, d0, i0)
-    scalars = jnp.sum(got[pl.ds(0, wide, stride=8), :], axis=0, keepdims=True)
+    stride = 4 * (wide // DEEP)
+    scalars = jnp.sum(got[pl.ds(0, DEEP, stride=stride), :], axis=0, keepdims=True)
     lane = iota((1, 128), 1)
-    rho = jnp.sum(jnp.where(lane == 64, scalars, 0.0), keepdims=True)
-    curve = jnp.sum(jnp.where(lane == 65, scalars, 0.0), keepdims=True)
+    rho = jnp.sum(jnp.where(lane == SUMS, scalars, 0.0), keepdims=True)
+    curve = jnp.sum(jnp.where(lane == SUMS + 1, scalars, 0.0), keepdims=True)
     alpha = (rho / curve).reshape(1, 1, 1)
     own = slice(HALO, HALO + OWN)
     vz0 = [z0[p] for p in range(2)]
@@ -342,21 +380,21 @@
             residual[rows, :] = res1[p, x] - alpha_next * (image1[p, x] + beta * q)
 
 
-def call(kernel, outs, *args, scratch=()):
+def call(kernel, outs, *args, scratch=(), space=pltpu.VMEM):
     return pl.pallas_call(
         kernel,
         out_shape=tuple(jax.ShapeDtypeStruct(s, F32) for s in outs),
-        in_specs=[pl.BlockSpec(memory_space=pltpu.VMEM)] * len(args),
+        in_specs=[pl.BlockSpec(memory_space=space)] * len(args),
         out_specs=tuple(pl.BlockSpec(memory_space=pltpu.VMEM) for _ in outs),
         scratch_shapes=scratch,
         compiler_params=pltpu.CompilerParams(vmem_limit_bytes=40 * 1024 * 1024),
     )(*args)
 
 
-def gathered(array, axis):
-    peers = lax.axis_size(axis)
+def gathered(array, axis, groups=None):
+    peers = lax.axis_size(axis) if groups is None else len(groups[0])
     slots = jnp.broadcast_to(array[None], (peers,) + array.shape)
-    return lax.all_to_all(slots, axis, 0, 0)
+    return lax.all_to_all(slots, axis, 0, 0, axis_index_groups=groups)
 
 
 def to_next(array, axis):
@@ -373,7 +411,14 @@
     wide, narrow = lax.axis_size("wide"), lax.axis_size("narrow")
     flat = [v.reshape(128, 128) for v in (right_side, capacity, phase, mold_flags)]
     edge = (2, 2, HALO, 8, 128)
-    own, low, high = call(prepare_kernel, [(2, 2, OWN, 8, 128), edge, edge], *flat)
+    staged = [pltpu.VMEM((128, 128), v.dtype) for v in flat]
+    own, low, high = call(
+        prepare_kernel,
+        [(2, 2, OWN, 8, 128), edge, edge],
+        *flat,
+        scratch=staged + [pltpu.SemaphoreType.DMA((4,))],
+        space=pl.ANY,
+    )
     below, above = to_next(high, "wide"), to_previous(low, "wide")
     a = jnp.concatenate([below[0], own[0], above[0]], axis=1)
     b = jnp.concatenate([below[1], own[1], above[1]], axis=1)
@@ -396,10 +441,25 @@
     )
     below, above = to_next(high, "wide"), to_previous(low, "wide")
     source, r1, send = call(
-        down_again_kernel, [fine, coarse, (8, 128)], q0, below, above, d0, i0, d1, i1, sums
-    )
-    (send,) = call(functools.partial(window_kernel, narrow), [(8, 128)], gathered(send, "narrow"))
-    second = gathered(send, "wide").reshape(8 * wide, 128)
+        down_again_kernel,
+        [fine, coarse, (4, 128)],
+        q0, below, above, d0, i0, d1, i1, sums,
+        scratch=[pltpu.VMEM((8, 128), F32)],
+    )
+    across = wide // DEEP
+    near = [
+        [(DEEP * y + z) * narrow + n for y in range(across) for n in range(narrow)]
+        for z in range(DEEP)
+    ]
+    far = [[DEEP * y + z for z in range(DEEP)] for y in range(across)]
+    rows = (4 * across, 128)
+    (send,) = call(
+        functools.partial(window_kernel, narrow),
+        [rows],
+        gathered(send, ("wide", "narrow"), near),
+        scratch=[pltpu.VMEM(rows, F32)] * 3,
+    )
+    second = gathered(send, "wide", far).reshape(DEEP * 4 * across, 128)
     z1, image1, res1, sums, known = call(
         functools.partial(up_again_kernel, wide, narrow),
         [block, block, block, (1, 128), (1, 128)],

time: 144 us -> 139 us (0.965)
  blocking collectives: 106 us -> 100 us
    all_to_all x5, blocking collectives: 106 us -> 100 us  [gathered(): return lax.all_to_all(slots, axis, 0, 0, axis_index_groups=groups)]
where the time goes in v3:
time: 139 us; the launch traced here: 138 us
  blocking collectives  100 us (72%)
  starting transfers between devices  18 us (13%)
  waiting for transfers between devices  10.4 us (7%)
  Pallas kernels  5.62 us (4%)
  local copies, waits for them, and re-layouts  3.46 us (2%)
    all_to_all x5, blocking collectives, gathered(): return lax.all_to_all(slots, axis, 0, 0, axis_index_groups=groups)  100 us
    ppermute x3, starting transfers between devices, to_previous(): return lax.ppermute(array, axis, [(i + 1, i) for i in range(n - 1)])  9.26 us
    ppermute x3, starting transfers between devices, to_next(): return lax.ppermute(array, axis, [(i, i + 1) for i in range(n - 1)])  8.72 us
    ppermute x3, waiting for transfers between devices, to_previous(): return lax.ppermute(array, axis, [(i + 1, i) for i in range(n - 1)])  7.7 us
    pallas_call x7, Pallas kernels, call(): pl.pallas_call(kernel, out_shape=tuple((jax.ShapeDtypeStruct(s, F32) for...  5.62 us
    unnamed x8, local copies, waits for them, and re-layouts  3.35 us
  transfers between devices with their start and end apart: 6, of which 5 were waited for; matrix products, arithmetic and copies ran while one was open for 0% of the time, Pallas kernels for 0%

profile of v3, /device:TPU:1, one launch (start us, length us, event | category | flops | bytes accessed | tf_op | source)
XLA Modules:
  0.0 138.4 jit_solution(3176016920867246615)
XLA Ops:
  0.6 0.8 copy-done
  1.5 0.8 copy-done.1
  2.3 0.8 copy-done.2
  3.2 0.8 copy-done.3
  4.0 0.5 shard_map.59
  4.5 4.4 %collective-permute-start = (f32[2,2,5,8,128]{4,3,2,1,0:T(8,128)S(1)}, f32[2,2,5,8,128]{4,3,2,1,0:T(8,128)S(1)}, u32[]{:S(2)}, u32[]{:S(2)}) collective-permute-start(f32[2,2,5,8,128]{4,3,2,1,0:T(8,128)S(1)} %get-tuple-element.27), channel_id=1, source_target_pairs={{0,8},{8,16},{16,24},{24,32},{32,40},{40,48},{48,56},{56,64},{64,7... | collective-permute-start | bytes 245768 | tf_op jit(solution)/shard_map/ppermute | solution.py:402
  8.9 1.3 collective-permute-start.1
  10.4 3.9 %collective-permute-done.1 = f32[2,2,5,8,128]{4,3,2,1,0:T(8,128)S(1)} collective-permute-done((f32[2,2,5,8,128]{4,3,2,1,0:T(8,128)S(1)}, f32[2,2,5,8,128]{4,3,2,1,0:T(8,128)S(1)}, u32[]{:S(2)}, u32[]{:S(2)}) %collective-permute-start.1) | collective-permute-done | bytes 81952 | tf_op jit(solution)/shard_map/ppermute | solution.py:407
  14.3 6.7 %collective-permute-start.3 = (f32[2,18,8,128]{3,2,1,0:T(8,128)S(1)}, f32[2,18,8,128]{3,2,1,0:T(8,128)S(1)}, u32[]{:S(2)}, u32[]{:S(2)}) collective-permute-start(f32[2,18,8,128]{3,2,1,0:T(8,128)S(1)} %pad_maximum_fusion.a), channel_id=1, source_target_pairs={{1,0},{2,1},{3,2},{4,3},{5,4},{6,5},{7,6},{9,8},{10,9},{11,10},{12... | collective-permute-start | bytes 442376 | tf_op jit(solution)/shard_map/ppermute | solution.py:407
  21.0 1.9 %collective-permute-start.2 = (f32[2,18,8,128]{3,2,1,0:T(8,128)S(1)}, f32[2,18,8,128]{3,2,1,0:T(8,128)S(1)}, u32[]{:S(2)}, u32[]{:S(2)}) collective-permute-start(f32[2,18,8,128]{3,2,1,0:T(8,128)S(1)} %pad_maximum_fusion.1.b), channel_id=1, source_target_pairs={{0,1},{1,2},{2,3},{3,4},{4,5},{5,6},{6,7},{8,9},{9,10},{10,11},{11... | collective-permute-start | bytes 442376 | tf_op jit(solution)/shard_map/ppermute | solution.py:402
  22.9 2.1 %collective-permute-done.2.from_left = f32[2,18,8,128]{3,2,1,0:T(8,128)S(1)} collective-permute-done((f32[2,18,8,128]{3,2,1,0:T(8,128)S(1)}, f32[2,18,8,128]{3,2,1,0:T(8,128)S(1)}, u32[]{:S(2)}, u32[]{:S(2)}) %collective-permute-start.2) | collective-permute-done | bytes 147488 | tf_op jit(solution)/shard_map/ppermute | solution.py:402
  25.0 0.7 shard_map.60
  25.7 36.6 %all_to_all.25 = f32[64,8,128]{2,1,0:T(8,128)S(1)} all-to-all(f32[64,8,128]{2,1,0:T(8,128)S(1)} %broadcast_in_dim.12), channel_id=1, replica_groups=mesh['wide'=64,'narrow'=8] {'wide'}, dimensions={0} | all-to-all | bytes 524288 | tf_op jit(solution)/shard_map/all_to_all | solution.py:397
  62.3 1.5 %shard_map.61 = (f32[2,8,8,128]{3,2,1,0:T(8,128)S(1)}, f32[2,8,8,256]{3,2,1,0:T(8,128)S(1)}, f32[2,5,8,256]{3,2,1,0:T(8,128)S(1)}, f32[2,5,8,256]{3,2,1,0:T(8,128)S(1)}, f32[8,128]{1,0:T(8,128)S(1)}) custom-call(f32[512,128]{1,0:T(8,128)S(1)} %bitcast.23, f32[2,18,8,256]{3,2,1,0:T(8,128)S(1)} %get-tuple-element.31.r0, ...), custom_call_target="tpu_custom_call" | custom-call | tf_op jit(solution)/shard_map/pallas_call | solution.py:384
  63.8 2.4 %collective-permute-start.4 = (f32[2,5,8,256]{3,2,1,0:T(8,128)S(1)}, f32[2,5,8,256]{3,2,1,0:T(8,128)S(1)}, u32[]{:S(2)}, u32[]{:S(2)}) collective-permute-start(f32[2,5,8,256]{3,2,1,0:T(8,128)S(1)} %get-tuple-element.38), channel_id=1, source_target_pairs={{0,8},{8,16},{16,24},{24,32},{32,40},{40,48},{48,56},{56,64},{64,7... | collective-permute-start | bytes 245768 | tf_op jit(solution)/shard_map/ppermute | solution.py:402
  66.3 1.3 collective-permute-start.5
  68.0 3.8 %collective-permute-done.5.high = f32[2,5,8,256]{3,2,1,0:T(8,128)S(1)} collective-permute-done((f32[2,5,8,256]{3,2,1,0:T(8,128)S(1)}, f32[2,5,8,256]{3,2,1,0:T(8,128)S(1)}, u32[]{:S(2)}, u32[]{:S(2)}) %collective-permute-start.5) | collective-permute-done | bytes 81952 | tf_op jit(solution)/shard_map/ppermute | solution.py:407
  71.8 0.5 shard_map.62
  72.4 17.4 %all_to_all.26.got = f32[32,4,128]{2,1,0:T(4,128)S(1)} all-to-all(f32[32,4,128]{2,1,0:T(4,128)S(1)} %broadcast_in_dim.13), channel_id=1, replica_groups={{0,1,2,3,4,5,6,7,128,129,130,131,132,133,134,135,256,257,258,259,260,26..., dimensions={0} | all-to-all | bytes 131072 | tf_op jit(solution)/shard_map/all_to_all | solution.py:397
  89.9 17.3 %all_to_all.27 = f32[16,16,128]{2,1,0:T(8,128)S(1)} all-to-all(f32[16,16,128]{2,1,0:T(8,128)S(1)} %broadcast_in_dim.14), channel_id=1, replica_groups={{0,8,16,24,32,40,48,56,64,72,80,88,96,104,112,120},{128,136,144,152,160..., dimensions={0} | all-to-all | bytes 262144 | tf_op jit(solution)/shard_map/all_to_all | solution.py:397
  107.3 1.5 %shard_map.64 = (f32[2,8,8,128]{3,2,1,0:T(8,128)S(1)}, f32[2,8,8,128]{3,2,1,0:T(8,128)S(1)}, f32[2,8,8,128]{3,2,1,0:T(8,128)S(1)}, f32[1,128]{1,0:T(1,128)S(1)}, f32[1,128]{1,0:T(1,128)S(1)}) custom-call(f32[256,128]{1,0:T(8,128)S(1)} %bitcast.25, f32[512,128]{1,0:T(8,128)S(1)} %bitcast.24, f32[2,18,8,256]{3,2,1,0:T(8,128)S(1)} %get-tuple-element.42.source, ...), custom_call_target="tpu_custom_call" | custom-call | tf_op jit(solution)/shard_map/pallas_call | solution.py:384
  108.8 10.2 %all_to_all.28 = f32[8,1,128]{2,1,0:T(1,128)S(1)} all-to-all(f32[8,1,128]{2,1,0:T(1,128)S(1)} %broadcast_in_dim.16), channel_id=1, replica_groups=mesh['wide'=64,'narrow'=8] {'narrow'}, dimensions={0} | all-to-all | bytes 8192 | tf_op jit(solution)/shard_map/all_to_all | solution.py:397
  119.0 18.5 %all_to_all.29 = f32[64,1,128]{2,1,0:T(1,128)S(1)} all-to-all(f32[64,1,128]{2,1,0:T(1,128)S(1)} %broadcast_in_dim.17), channel_id=1, replica_groups=mesh['wide'=64,'narrow'=8] {'wide'}, dimensions={0} | all-to-all | bytes 65536 | tf_op jit(solution)/shard_map/all_to_all | solution.py:397
  137.5 0.8 shard_map.65
  (19 shorter events, 0.9 us)
Async XLA Ops:
  0.6 0.8 copy-start
  1.5 0.8 copy-start.1
  2.3 0.8 copy-start.2
  3.2 0.8 copy-start.3
  4.5 5.8 %collective-permute-start = (f32[2,2,5,8,128]{4,3,2,1,0:T(8,128)S(1)}, f32[2,2,5,8,128]{4,3,2,1,0:T(8,128)S(1)}, u32[]{:S(2)}, u32[]{:S(2)}) collective-permute-start(f32[2,2,5,8,128]{4,3,2,1,0:T(8,128)S(1)} %get-tuple-element.27), channel_id=1, source_target_pairs={{0,8},{8,16},{16,24},{24,32},{32,40},{40,48},{48,56},{56,64},{64,7... | collective-permute-start | bytes 245768 | tf_op jit(solution)/shard_map/ppermute | solution.py:402
  8.9 5.4 %collective-permute-start.1 = (f32[2,2,5,8,128]{4,3,2,1,0:T(8,128)S(1)}, f32[2,2,5,8,128]{4,3,2,1,0:T(8,128)S(1)}, u32[]{:S(2)}, u32[]{:S(2)}) collective-permute-start(f32[2,2,5,8,128]{4,3,2,1,0:T(8,128)S(1)} %get-tuple-element.29), channel_id=1, source_target_pairs={{8,0},{16,8},{24,16},{32,24},{40,32},{48,40},{56,48},{64,56},{72,6... | collective-permute-start | bytes 245768 | tf_op jit(solution)/shard_map/ppermute | solution.py:407
  14.3 8.6 %collective-permute-start.3 = (f32[2,18,8,128]{3,2,1,0:T(8,128)S(1)}, f32[2,18,8,128]{3,2,1,0:T(8,128)S(1)}, u32[]{:S(2)}, u32[]{:S(2)}) collective-permute-start(f32[2,18,8,128]{3,2,1,0:T(8,128)S(1)} %pad_maximum_fusion.a), channel_id=1, source_target_pairs={{1,0},{2,1},{3,2},{4,3},{5,4},{6,5},{7,6},{9,8},{10,9},{11,10},{12... | collective-permute-start | bytes 442376 | tf_op jit(solution)/shard_map/ppermute | solution.py:407
  21.0 4.0 %collective-permute-start.2 = (f32[2,18,8,128]{3,2,1,0:T(8,128)S(1)}, f32[2,18,8,128]{3,2,1,0:T(8,128)S(1)}, u32[]{:S(2)}, u32[]{:S(2)}) collective-permute-start(f32[2,18,8,128]{3,2,1,0:T(8,128)S(1)} %pad_maximum_fusion.1.b), channel_id=1, source_target_pairs={{0,1},{1,2},{2,3},{3,4},{4,5},{5,6},{6,7},{8,9},{9,10},{10,11},{11... | collective-permute-start | bytes 442376 | tf_op jit(solution)/shard_map/ppermute | solution.py:402
  63.8 4.2 %collective-permute-start.4 = (f32[2,5,8,256]{3,2,1,0:T(8,128)S(1)}, f32[2,5,8,256]{3,2,1,0:T(8,128)S(1)}, u32[]{:S(2)}, u32[]{:S(2)}) collective-permute-start(f32[2,5,8,256]{3,2,1,0:T(8,128)S(1)} %get-tuple-element.38), channel_id=1, source_target_pairs={{0,8},{8,16},{16,24},{24,32},{32,40},{40,48},{48,56},{56,64},{64,7... | collective-permute-start | bytes 245768 | tf_op jit(solution)/shard_map/ppermute | solution.py:402
  66.3 5.6 %collective-permute-start.5 = (f32[2,5,8,256]{3,2,1,0:T(8,128)S(1)}, f32[2,5,8,256]{3,2,1,0:T(8,128)S(1)}, u32[]{:S(2)}, u32[]{:S(2)}) collective-permute-start(f32[2,5,8,256]{3,2,1,0:T(8,128)S(1)} %get-tuple-element.39), channel_id=1, source_target_pairs={{8,0},{16,8},{24,16},{32,24},{40,32},{48,40},{56,48},{64,56},{72,6... | collective-permute-start | bytes 245768 | tf_op jit(solution)/shard_map/ppermute | solution.py:407

commit v4 on v3

--- a/solution.py
+++ b/solution.py
@@ -155,7 +155,7 @@
     return each(lambda e, i, r, a: e + i * (r - a), e2, i2, r2, apply_two(e2, d2))
 
 
-def rise(e2, scratch, at, r1, d1, i1):
+def rise(e2, scratch, at, reach, r1, d1, i1):
     wide = e2[0][0].shape[0]
     blank = jnp.zeros((8, 128), F32)
     for x in range(2):
@@ -165,7 +165,8 @@
             scratch[2 * z + x, 8 : 8 + wide, :] = e2[x][z]
     pair = iota((8, 128), 0) // 2
     rows = []
-    for x, step in ((1, -1), (0, 0), (1, 0), (0, 1)):
+    for row in range(-reach, 2 + reach):
+        x, step = row % 2, row // 2
         tile = blank
         for z in range(4):
             line = scratch[2 * z + x, pl.ds(at + (8 + step), 1), :]
@@ -174,17 +175,20 @@
     shape = (128, LANES)
     matrix = jnp.where(iota(shape, 0) == iota(shape, 1) // 4, 1.0, 0.0).astype(F32)
     spread = jnp.dot(jnp.concatenate(rows, 0), matrix, precision=lax.Precision.HIGHEST)
-    e1 = i1 * r1 + double_rows(spread.reshape(4, 8, LANES))
+    e1 = i1 * r1 + double_rows(spread.reshape(len(rows), 8, LANES))
     return e1[1:-1] + i1[1:-1] * (r1[1:-1] - apply_one(e1, d1[1:-1]))
 
 
-def finish(e1, source, extra, inverse):
-    up = double_rows(e1)
-    e = [inverse[p, 3:15] * source[p, 3:15] + up for p in range(2)]
-    a = apply_fine(e[0], e[1], extra[0, 4:14], extra[1, 4:14])
-    z = [e[p][1:-1] + inverse[p, 4:14] * (source[p, 4:14] - a[p]) for p in range(2)]
-    q = apply_fine(z[0], z[1], extra[0, 5:13], extra[1, 5:13])
-    return [v[1:-1] for v in z], q
+def rows_of(pair, first, stop):
+    return [pair[p][first:stop] for p in range(2)]
+
+
+def finish(up, source, extra, inverse):
+    e = [inverse[p] * source[p] + up for p in range(2)]
+    a = apply_fine(e[0], e[1], extra[0][1:-1], extra[1][1:-1])
+    z = [e[p][1:-1] + inverse[p][1:-1] * (source[p][1:-1] - a[p]) for p in range(2)]
+    q = apply_fine(z[0], z[1], extra[0][2:-2], extra[1][2:-2])
+    return z, q
 
 
 def descend(source, extra, inverse):
@@ -195,8 +199,15 @@
 
 
 def leave_one(r1, d1, i1):
-    c1 = (i1 * r1)[1:7]
-    return r1[2:6] - apply_one(c1, d1[2:6])
+    return r1[1:-1] - apply_one(i1 * r1, d1[1:-1])
+
+
+def invert_one(d1, first, me_w, me_n, wide, narrow):
+    lane = iota(d1.shape, 2)
+    column = 128 * me_n + jnp.where(lane < 192, lane, lane - 256)
+    line = 4 * me_w + first + iota(d1.shape, 0)
+    inside = (column >= 0) & (column < 128 * narrow) & (line >= 0) & (line < 4 * wide)
+    return jnp.where(inside, OMEGA / (1.5 + d1), 0.0)
 
 
 def total(a, b):
@@ -235,7 +246,7 @@
                     high[side, p, x - (OWN - HALO)] = value
 
 
-def down_kernel(wide, narrow, a, b, from_left, from_right, r0, d0, i0, r1, d1, i1, send):
+def down_kernel(wide, narrow, a, b, from_left, from_right, r0, d0, i0, one, send):
     me_w, me_n = lax.axis_index("wide"), lax.axis_index("narrow")
     shape = (EXT, 8, 128)
     half = iota(shape, 2) < 64
@@ -257,15 +268,12 @@
         r0[p] = source[p]
         d0[p] = extra[p]
         i0[p] = inverse[p]
-    vr1 = descend(source, extra, inverse)
-    vd1 = restrict_fine(extra[0][1:-1], extra[1][1:-1])
-    line = 4 * me_w - 2 + iota(vd1.shape, 0)
-    inside = (column[:8] >= 0) & (column[:8] < 128 * narrow) & (line >= 0) & (line < 4 * wide)
-    vi1 = jnp.where(inside, OMEGA / (1.5 + vd1), 0.0)
-    r1[...] = vr1
-    d1[...] = vd1
-    i1[...] = vi1
-    send[...] = pack_two(leave_one(vr1, vd1, vi1), 0) + pack_two(vd1[2:6], 64)
+    vr1 = descend(source, extra, inverse)[1:7]
+    vd1 = restrict_fine(extra[0][3:15], extra[1][3:15])
+    vi1 = invert_one(vd1, -1, me_w, me_n, wide, narrow)
+    one[0] = vr1[1:5]
+    one[1] = vd1[1:5]
+    send[...] = pack_two(leave_one(vr1, vd1, vi1), 0) + pack_two(vd1[1:5], 64)
 
 
 def both_halves(tile):
@@ -274,37 +282,35 @@
     return jnp.where(half, tile, other), jnp.where(half, other, tile)
 
 
-def up_kernel(wide, narrow, got, r0, d0, i0, r1, d1, i1, z, q, low, high, sums, scratch):
+def turn_kernel(wide, narrow, got, r0, d0, i0, one, below, above, z, q, r1, d1, i1, low, high, send, scratch, small):
     me_w, me_n = lax.axis_index("wide"), lax.axis_index("narrow")
     tiles = split_two(got, wide)
     r2 = each(lambda t: both_halves(t)[0], tiles)
     d2 = each(lambda t: both_halves(t)[1], tiles)
     e2 = solve_coarse(r2, d2, me_n, narrow)
-    e1 = rise(e2, scratch, me_w, r1[...], d1[...], i1[...])
-    vz, vq = finish(e1, r0, d0, i0)
+    vr1 = jnp.concatenate([below[0], one[0], above[0]], axis=0)
+    vd1 = jnp.concatenate([below[1], one[1], above[1]], axis=0)
+    vi1 = invert_one(vd1, -4, me_w, me_n, wide, narrow)
+    e1 = rise(e2, scratch, me_w, 2, vr1, vd1, vi1)
+    up = double_rows(e1)[1:-1]
+    source, extra, inverse = (rows_of(ref, 0, EXT) for ref in (r0, d0, i0))
+    vz, vq = finish(up, source, extra, inverse)
+    own_z = [v[4:12, :, :128] for v in vz]
+    own_q = [v[3:11, :, :128] for v in vq]
+    own_r = [v[HALO : HALO + OWN, :, :128] for v in source]
     for p in range(2):
-        z[p] = vz[p][:, :, :128]
+        z[p] = own_z[p]
         q[p] = vq[p]
-        low[p] = vq[p][:HALO]
-        high[p] = vq[p][OWN - HALO :]
-    mine = [v[:, :, :128] for v in vz]
-    image = [v[:, :, :128] for v in vq]
-    residual = [r0[p, HALO : HALO + OWN, :, :128] for p in range(2)]
-    sums[...] = place([total(residual, mine), total(mine, image)], (8, 128), SUMS)
-
-
-def down_again_kernel(q, low, high, d0, i0, d1, i1, sums, source, r1, send, scratch):
-    full, extra, inverse = [], [], []
-    for p in range(2):
-        full.append(jnp.concatenate([low[p], q[p], high[p]], axis=0))
-        extra.append(d0[p])
-        inverse.append(i0[p])
-        source[p] = full[p]
-    vr1 = descend(full, extra, inverse)
-    r1[...] = vr1
-    rows = pack_rows(leave_one(vr1, d1[...], i1[...]), scratch)
+    below_two = descend(vq, rows_of(d0, 2, 16), rows_of(i0, 2, 16))
+    r1[...] = below_two
+    d1[...] = vd1[2:10]
+    i1[...] = vi1[2:10]
+    low[...] = below_two[2:3]
+    high[...] = below_two[3:4]
+    rows = pack_rows(leave_one(below_two, vd1[3:9], vi1[3:9]), small)
+    sums = place([total(own_r, own_z), total(own_z, own_q)], rows.shape, SUMS)
     lane = iota(rows.shape, 1)
-    send[...] = jnp.where((lane == SUMS) | (lane == SUMS + 1), sums[0:4, :], rows)
+    send[...] = jnp.where((lane == SUMS) | (lane == SUMS + 1), sums, rows)
 
 
 def window_kernel(narrow, got, send, own, right, left):
@@ -332,13 +338,16 @@
     return sides
 
 
-def up_again_kernel(wide, narrow, got, first, source, r0, d0, i0, r1, d1, i1, z0, z1, image1, res1, sums, known, scratch):
+def up_again_kernel(wide, narrow, got, first, source, r0, d0, i0, below, r1, above, d1, i1, z0, z1, image1, res1, sums, known, scratch):
     me_w, me_n = lax.axis_index("wide"), lax.axis_index("narrow")
     r2 = split_deep(got, wide)
     d2 = each(lambda t: both_halves(t)[1], split_two(first, wide))
     e2 = solve_coarse(r2, d2, me_n, narrow)
-    e1 = rise(e2, scratch, me_w, r1[...], d1[...], i1[...])
-    vw, vy = finish(e1, source, d0, i0)
+    vr1 = jnp.concatenate([below[...], r1[...], above[...]], axis=0)
+    e1 = rise(e2, scratch, me_w, 1, vr1, d1[...], i1[...])
+    extra, inverse = rows_of(d0, 3, 15), rows_of(i0, 3, 15)
+    vw, vy = finish(double_rows(e1), rows_of(source, 1, 13), extra, inverse)
+    vw = [v[1:-1] for v in vw]
     stride = 4 * (wide // DEEP)
     scalars = jnp.sum(got[pl.ds(0, DEEP, stride=stride), :], axis=0, keepdims=True)
     lane = iota((1, 128), 1)
@@ -347,7 +356,7 @@
     alpha = (rho / curve).reshape(1, 1, 1)
     own = slice(HALO, HALO + OWN)
     vz0 = [z0[p] for p in range(2)]
-    vq0 = [source[p, own, :, :128] for p in range(2)]
+    vq0 = [source[p, 3:11, :, :128] for p in range(2)]
     vz1 = [vz0[p] - alpha * vw[p][:, :, :128] for p in range(2)]
     vi1 = [vq0[p] - alpha * vy[p][:, :, :128] for p in range(2)]
     vr1 = [r0[p, own, :, :128] - alpha * vq0[p] for p in range(2)]
@@ -375,19 +384,19 @@
     for p in range(2):
         for x in range(OWN):
             rows = pl.ds(x + 8 * p, 8, stride=16)
-            z, q = z0[p, x], source[p, HALO + x, :, :128]
+            z, q = z0[p, x], source[p, 3 + x, :, :128]
             field[rows, :] = alpha * z + alpha_next * (z1[p, x] + beta * z)
             residual[rows, :] = res1[p, x] - alpha_next * (image1[p, x] + beta * q)
 
 
-def call(kernel, outs, *args, scratch=(), space=pltpu.VMEM):
+def call(kernel, outs, *args, scratch=(), space=pltpu.VMEM, limit=40):
     return pl.pallas_call(
         kernel,
         out_shape=tuple(jax.ShapeDtypeStruct(s, F32) for s in outs),
         in_specs=[pl.BlockSpec(memory_space=space)] * len(args),
         out_specs=tuple(pl.BlockSpec(memory_space=pltpu.VMEM) for _ in outs),
         scratch_shapes=scratch,
-        compiler_params=pltpu.CompilerParams(vmem_limit_bytes=40 * 1024 * 1024),
+        compiler_params=pltpu.CompilerParams(vmem_limit_bytes=limit * 1024 * 1024),
     )(*args)
 
 
@@ -418,34 +427,29 @@
         *flat,
         scratch=staged + [pltpu.SemaphoreType.DMA((4,))],
         space=pl.ANY,
+        limit=63,
     )
     below, above = to_next(high, "wide"), to_previous(low, "wide")
     a = jnp.concatenate([below[0], own[0], above[0]], axis=1)
     b = jnp.concatenate([below[1], own[1], above[1]], axis=1)
     from_left, from_right = to_next(b, "narrow"), to_previous(a, "narrow")
-    fine, coarse = (2, EXT, 8, LANES), (8, 8, LANES)
-    r0, d0, i0, r1, d1, i1, send = call(
+    fine = (2, EXT, 8, LANES)
+    r0, d0, i0, one, send = call(
         functools.partial(down_kernel, wide, narrow),
-        [fine, fine, fine, coarse, coarse, coarse, (8, 128)],
+        [fine, fine, fine, (2, 4, 8, LANES), (8, 128)],
         a, b, from_left, from_right,
     )
+    below, above = to_next(one, "wide"), to_previous(one, "wide")
     first = gathered(send, "wide").reshape(8 * wide, 128)
-    block = (2, OWN, 8, 128)
-    band = (2, HALO, 8, LANES)
+    block, coarse, line = (2, OWN, 8, 128), (8, 8, LANES), (1, 8, LANES)
     scratch = [pltpu.VMEM((8, wide + 16, 128), F32)]
-    z0, q0, low, high, sums = call(
-        functools.partial(up_kernel, wide, narrow),
-        [block, (2, OWN, 8, LANES), band, band, (8, 128)],
-        first, r0, d0, i0, r1, d1, i1,
-        scratch=scratch,
+    z0, source, r1, d1, i1, low, high, send = call(
+        functools.partial(turn_kernel, wide, narrow),
+        [block, (2, 14, 8, LANES), (6, 8, LANES), coarse, coarse, line, line, (4, 128)],
+        first, r0, d0, i0, one, below, above,
+        scratch=scratch + [pltpu.VMEM((8, 128), F32)],
     )
     below, above = to_next(high, "wide"), to_previous(low, "wide")
-    source, r1, send = call(
-        down_again_kernel,
-        [fine, coarse, (4, 128)],
-        q0, below, above, d0, i0, d1, i1, sums,
-        scratch=[pltpu.VMEM((8, 128), F32)],
-    )
     across = wide // DEEP
     near = [
         [(DEEP * y + z) * narrow + n for y in range(across) for n in range(narrow)]
@@ -463,7 +467,7 @@
     z1, image1, res1, sums, known = call(
         functools.partial(up_again_kernel, wide, narrow),
         [block, block, block, (1, 128), (1, 128)],
-        second, first, source, r0, d0, i0, r1, d1, i1, z0,
+        second, first, source, r0, d0, i0, below, r1, above, d1, i1, z0,
         scratch=scratch,
     )
     sums = jnp.sum(gathered(sums, "narrow"), axis=0)

time: 139 us -> 130 us (0.935)
  blocking collectives: 100 us -> 47 us
  starting transfers between devices: 18 us -> 44 us
  waiting for transfers between devices: 10.4 us -> 28.4 us
    all_to_all x5 -> x3, blocking collectives: 100 us -> 47 us  [gathered(): return lax.all_to_all(slots, axis, 0, 0, axis_index_groups=groups)]
    all_to_all x0 -> x2, starting transfers between devices: none -> 20.1 us  [gathered(): return lax.all_to_all(slots, axis, 0, 0, axis_index_groups=groups)]
    all_to_all x0 -> x2, waiting for transfers between devices: none -> 12.1 us  [gathered(): return lax.all_to_all(slots, axis, 0, 0, axis_index_groups=groups)]
    ppermute x3 -> x4, waiting for transfers between devices: 7.7 us -> 14.3 us  [to_previous(): return lax.ppermute(array, axis, [(i + 1, i) for i in range(n - 1)])]
    ppermute x3 -> x4, starting transfers between devices: 8.72 us -> 13.4 us  [to_next(): return lax.ppermute(array, axis, [(i, i + 1) for i in range(n - 1)])]
    unnamed x8 -> x0, local copies, waits for them, and re-layouts: 3.35 us -> none
    ppermute x3 -> x4, starting transfers between devices: 9.26 us -> 10.5 us  [to_previous(): return lax.ppermute(array, axis, [(i + 1, i) for i in range(n - 1)])]
    pallas_call x7 -> x6, Pallas kernels: 5.62 us -> 6.83 us  [call(): pl.pallas_call(kernel, out_shape=tuple((jax.ShapeDtypeStruct(s, F32) for...]
  transfers between devices with their start and end apart: 6 -> 10, of which waited for: 5 -> 6; matrix products, arithmetic and copies ran while one was open for 0% -> 1% of each run, Pallas kernels for 0% -> 0%
where the time goes in v4:
time: 130 us; the launch traced here: 129 us
  blocking collectives  47 us (36%)
  starting transfers between devices  44 us (34%)
  waiting for transfers between devices  28.4 us (22%)
  Pallas kernels  6.83 us (5%)
  local copies, waits for them, and re-layouts  2.32 us (2%)
    all_to_all x3, blocking collectives, gathered(): return lax.all_to_all(slots, axis, 0, 0, axis_index_groups=groups)  47 us
    all_to_all x2, starting transfers between devices, gathered(): return lax.all_to_all(slots, axis, 0, 0, axis_index_groups=groups)  20.1 us
    ppermute x4, waiting for transfers between devices, to_previous(): return lax.ppermute(array, axis, [(i + 1, i) for i in range(n - 1)])  14.3 us
    ppermute x4, starting transfers between devices, to_next(): return lax.ppermute(array, axis, [(i, i + 1) for i in range(n - 1)])  13.4 us
    all_to_all x2, waiting for transfers between devices, gathered(): return lax.all_to_all(slots, axis, 0, 0, axis_index_groups=groups)  12.1 us
    ppermute x4, starting transfers between devices, to_previous(): return lax.ppermute(array, axis, [(i + 1, i) for i in range(n - 1)])  10.5 us
    pallas_call x6, Pallas kernels, call(): pl.pallas_call(kernel, out_shape=tuple((jax.ShapeDtypeStruct(s, F32) for...  6.83 us
  transfers between devices with their start and end apart: 10, of which 6 were waited for; matrix products, arithmetic and copies ran while one was open for 1% of the time, Pallas kernels for 0%

profile of v4, /device:TPU:1, one launch (start us, length us, event | category | flops | bytes accessed | tf_op | source)
XLA Modules:
  0.0 129.4 jit_solution(8323660188518836669)
XLA Ops:
  0.6 1.8 %shard_map.59 = (f32[2,2,8,8,128]{4,3,2,1,0:T(8,128)}, f32[2,2,5,8,128]{4,3,2,1,0:T(8,128)}, f32[2,2,5,8,128]{4,3,2,1,0:T(8,128)}) custom-call(f32[128,128]{1,0:T(8,128)} %bitcast.28, f32[128,128]{1,0:T(8,128)} %bitcast.29, s32[128,128]{1,0:T(8,128)} %bitcast.30, s32[128,128]{1,0:T(8,128)} %bitcast.31), custom_call_target="tpu_custom_call" | custom-call | tf_op jit(solution)/shard_map/pallas_call | solution.py:393
  2.4 4.4 %collective-permute-start = (f32[2,2,5,8,128]{4,3,2,1,0:T(8,128)}, f32[2,2,5,8,128]{4,3,2,1,0:T(8,128)S(1)}, u32[]{:S(2)}, u32[]{:S(2)}) collective-permute-start(f32[2,2,5,8,128]{4,3,2,1,0:T(8,128)} %get-tuple-element.25), channel_id=1, source_target_pairs={{0,8},{8,16},{16,24},{24,32},{32,40},{40,48},{48,56},{56,64},{64,7... | collective-permute-start | bytes 245768 | tf_op jit(solution)/shard_map/ppermute | solution.py:411
  6.8 1.3 collective-permute-start.1
  8.1 0.9 slice_bitcast_fusion
  9.0 3.4 %collective-permute-done.1 = f32[2,2,5,8,128]{4,3,2,1,0:T(8,128)S(1)} collective-permute-done((f32[2,2,5,8,128]{4,3,2,1,0:T(8,128)}, f32[2,2,5,8,128]{4,3,2,1,0:T(8,128)S(1)}, u32[]{:S(2)}, u32[]{:S(2)}) %collective-permute-start.1) | collective-permute-done | bytes 81952 | tf_op jit(solution)/shard_map/ppermute | solution.py:416
  12.4 6.7 %collective-permute-start.3 = (f32[2,18,8,128]{3,2,1,0:T(8,128)S(1)}, f32[2,18,8,128]{3,2,1,0:T(8,128)S(1)}, u32[]{:S(2)}, u32[]{:S(2)}) collective-permute-start(f32[2,18,8,128]{3,2,1,0:T(8,128)S(1)} %pad_maximum_fusion.a), channel_id=1, source_target_pairs={{1,0},{2,1},{3,2},{4,3},{5,4},{6,5},{7,6},{9,8},{10,9},{11,10},{12... | collective-permute-start | bytes 442376 | tf_op jit(solution)/shard_map/ppermute | solution.py:416
  19.1 1.9 %collective-permute-start.2 = (f32[2,18,8,128]{3,2,1,0:T(8,128)S(1)}, f32[2,18,8,128]{3,2,1,0:T(8,128)S(1)}, u32[]{:S(2)}, u32[]{:S(2)}) collective-permute-start(f32[2,18,8,128]{3,2,1,0:T(8,128)S(1)} %pad_maximum_fusion.1.b), channel_id=1, source_target_pairs={{0,1},{1,2},{2,3},{3,4},{4,5},{5,6},{6,7},{8,9},{9,10},{10,11},{11... | collective-permute-start | bytes 442376 | tf_op jit(solution)/shard_map/ppermute | solution.py:411
  21.1 2.1 %collective-permute-done.2.from_left = f32[2,18,8,128]{3,2,1,0:T(8,128)S(1)} collective-permute-done((f32[2,18,8,128]{3,2,1,0:T(8,128)S(1)}, f32[2,18,8,128]{3,2,1,0:T(8,128)S(1)}, u32[]{:S(2)}, u32[]{:S(2)}) %collective-permute-start.2) | collective-permute-done | bytes 147488 | tf_op jit(solution)/shard_map/ppermute | solution.py:411
  24.5 16.6 %all-to-all-start = ((f32[64,8,128]{2,1,0:T(8,128)}), f32[64,8,128]{2,1,0:T(8,128)S(1)}, u32[]{:S(2)}, u32[]{:S(2)}) async-start(f32[64,8,128]{2,1,0:T(8,128)} %broadcast_in_dim.12), calls=%async_computation | async-start | bytes 524288 | tf_op jit(solution)/shard_map/all_to_all | solution.py:406
  41.0 1.3 collective-permute-start.5
  42.3 4.0 %collective-permute-start.4 = (f32[2,4,8,256]{3,2,1,0:T(8,128)S(1)}, f32[2,4,8,256]{3,2,1,0:T(8,128)S(1)}, u32[]{:S(2)}, u32[]{:S(2)}) collective-permute-start(f32[2,4,8,256]{3,2,1,0:T(8,128)S(1)} %get-tuple-element.32.one), channel_id=1, source_target_pairs={{0,8},{8,16},{16,24},{24,32},{32,40},{40,48},{48,56},{56,64},{64,7... | collective-permute-start | bytes 196616 | tf_op jit(solution)/shard_map/ppermute | solution.py:411
  46.3 7.5 %collective-permute-done.5.above = f32[2,4,8,256]{3,2,1,0:T(8,128)S(1)} collective-permute-done((f32[2,4,8,256]{3,2,1,0:T(8,128)S(1)}, f32[2,4,8,256]{3,2,1,0:T(8,128)S(1)}, u32[]{:S(2)}, u32[]{:S(2)}) %collective-permute-start.5) | collective-permute-done | bytes 65568 | tf_op jit(solution)/shard_map/ppermute | solution.py:416
  53.8 8.0 %all-to-all-done = f32[64,8,128]{2,1,0:T(8,128)S(1)} async-done(((f32[64,8,128]{2,1,0:T(8,128)}), f32[64,8,128]{2,1,0:T(8,128)S(1)}, u32[]{:S(2)}, u32[]{:S(2)}) %all-to-all-start) | async-done | bytes 262176 | tf_op jit(solution)/shard_map/all_to_all | solution.py:406
  61.8 2.0 %shard_map.61 = (f32[2,8,8,128]{3,2,1,0:T(8,128)S(1)}, f32[2,14,8,256]{3,2,1,0:T(8,128)S(1)}, f32[6,8,256]{2,1,0:T(8,128)S(1)}, f32[8,8,256]{2,1,0:T(8,128)S(1)}...) custom-call(f32[512,128]{1,0:T(8,128)S(1)} %bitcast.23, ...), custom_call_target="tpu_custom_call" | custom-call | tf_op jit(solution)/shard_map/pallas_call | solution.py:393
  63.8 16.1 %all_to_all.25.got = f32[32,4,128]{2,1,0:T(4,128)S(1)} all-to-all(f32[32,4,128]{2,1,0:T(4,128)S(1)} %broadcast_in_dim.13), channel_id=1, replica_groups={{0,1,2,3,4,5,6,7,128,129,130,131,132,133,134,135,256,257,258,259,260,26..., dimensions={0} | all-to-all | bytes 131072 | tf_op jit(solution)/shard_map/all_to_all | solution.py:406
  80.6 3.5 %all-to-all-start.2 = ((f32[16,16,128]{2,1,0:T(8,128)}), f32[16,16,128]{2,1,0:T(8,128)S(1)}, u32[]{:S(2)}, u32[]{:S(2)}) async-start(f32[16,16,128]{2,1,0:T(8,128)} %broadcast_in_dim.14), calls=%async_computation.2 | async-start | bytes 262144 | tf_op jit(solution)/shard_map/all_to_all | solution.py:406
  84.1 3.1 %collective-permute-start.6 = (f32[1,8,256]{2,1,0:T(8,128)S(1)}, f32[1,8,256]{2,1,0:T(8,128)S(1)}, u32[]{:S(2)}, u32[]{:S(2)}) collective-permute-start(f32[1,8,256]{2,1,0:T(8,128)S(1)} %get-tuple-element.35), channel_id=1, source_target_pairs={{0,8},{8,16},{16,24},{24,32},{32,40},{40,48},{48,56},{56,64},{64,7... | collective-permute-start | bytes 24584 | tf_op jit(solution)/shard_map/ppermute | solution.py:411
  87.3 1.3 collective-permute-start.7
  88.6 3.4 %collective-permute-done.7.above = f32[1,8,256]{2,1,0:T(8,128)S(1)} collective-permute-done((f32[1,8,256]{2,1,0:T(8,128)S(1)}, f32[1,8,256]{2,1,0:T(8,128)S(1)}, u32[]{:S(2)}, u32[]{:S(2)}) %collective-permute-start.7) | collective-permute-done | bytes 8224 | tf_op jit(solution)/shard_map/ppermute | solution.py:416
  92.0 4.1 %all-to-all-done.2 = f32[16,16,128]{2,1,0:T(8,128)S(1)} async-done(((f32[16,16,128]{2,1,0:T(8,128)}), f32[16,16,128]{2,1,0:T(8,128)S(1)}, u32[]{:S(2)}, u32[]{:S(2)}) %all-to-all-start.2) | async-done | bytes 131104 | tf_op jit(solution)/shard_map/all_to_all | solution.py:406
  96.2 1.5 %shard_map.63 = (f32[2,8,8,128]{3,2,1,0:T(8,128)S(1)}, f32[2,8,8,128]{3,2,1,0:T(8,128)S(1)}, f32[2,8,8,128]{3,2,1,0:T(8,128)S(1)}, f32[1,128]{1,0:T(1,128)S(1)}, f32[1,128]{1,0:T(1,128)S(1)}) custom-call(f32[256,128]{1,0:T(8,128)S(1)} %bitcast.25, f32[512,128]{1,0:T(8,128)S(1)} %bitcast.24, f32[2,14,8,256]{3,2,1,0:T(8,128)S(1)} %get-tuple-element.34.source, ...), custom_call_target="tpu_custom_call" | custom-call | tf_op jit(solution)/shard_map/pallas_call | solution.py:393
  97.7 9.8 %all_to_all.26 = f32[8,1,128]{2,1,0:T(1,128)S(1)} all-to-all(f32[8,1,128]{2,1,0:T(1,128)S(1)} %broadcast_in_dim.16), channel_id=1, replica_groups=mesh['wide'=64,'narrow'=8] {'narrow'}, dimensions={0} | all-to-all | bytes 8192 | tf_op jit(solution)/shard_map/all_to_all | solution.py:406
  107.6 21.1 %all_to_all.27 = f32[64,1,128]{2,1,0:T(1,128)S(1)} all-to-all(f32[64,1,128]{2,1,0:T(1,128)S(1)} %broadcast_in_dim.17), channel_id=1, replica_groups=mesh['wide'=64,'narrow'=8] {'wide'}, dimensions={0} | all-to-all | bytes 65536 | tf_op jit(solution)/shard_map/all_to_all | solution.py:406
  128.6 0.8 shard_map.64
  (16 shorter events, 2.2 us)
Async XLA Ops:
  2.4 6.6 %collective-permute-start = (f32[2,2,5,8,128]{4,3,2,1,0:T(8,128)}, f32[2,2,5,8,128]{4,3,2,1,0:T(8,128)S(1)}, u32[]{:S(2)}, u32[]{:S(2)}) collective-permute-start(f32[2,2,5,8,128]{4,3,2,1,0:T(8,128)} %get-tuple-element.25), channel_id=1, source_target_pairs={{0,8},{8,16},{16,24},{24,32},{32,40},{40,48},{48,56},{56,64},{64,7... | collective-permute-start | bytes 245768 | tf_op jit(solution)/shard_map/ppermute | solution.py:411
  6.8 5.6 %collective-permute-start.1 = (f32[2,2,5,8,128]{4,3,2,1,0:T(8,128)}, f32[2,2,5,8,128]{4,3,2,1,0:T(8,128)S(1)}, u32[]{:S(2)}, u32[]{:S(2)}) collective-permute-start(f32[2,2,5,8,128]{4,3,2,1,0:T(8,128)} %get-tuple-element.27), channel_id=1, source_target_pairs={{8,0},{16,8},{24,16},{32,24},{40,32},{48,40},{56,48},{64,56},{72,6... | collective-permute-start | bytes 245768 | tf_op jit(solution)/shard_map/ppermute | solution.py:416
  12.4 8.6 %collective-permute-start.3 = (f32[2,18,8,128]{3,2,1,0:T(8,128)S(1)}, f32[2,18,8,128]{3,2,1,0:T(8,128)S(1)}, u32[]{:S(2)}, u32[]{:S(2)}) collective-permute-start(f32[2,18,8,128]{3,2,1,0:T(8,128)S(1)} %pad_maximum_fusion.a), channel_id=1, source_target_pairs={{1,0},{2,1},{3,2},{4,3},{5,4},{6,5},{7,6},{9,8},{10,9},{11,10},{12... | collective-permute-start | bytes 442376 | tf_op jit(solution)/shard_map/ppermute | solution.py:416
  19.1 4.0 %collective-permute-start.2 = (f32[2,18,8,128]{3,2,1,0:T(8,128)S(1)}, f32[2,18,8,128]{3,2,1,0:T(8,128)S(1)}, u32[]{:S(2)}, u32[]{:S(2)}) collective-permute-start(f32[2,18,8,128]{3,2,1,0:T(8,128)S(1)} %pad_maximum_fusion.1.b), channel_id=1, source_target_pairs={{0,1},{1,2},{2,3},{3,4},{4,5},{5,6},{6,7},{8,9},{9,10},{10,11},{11... | collective-permute-start | bytes 442376 | tf_op jit(solution)/shard_map/ppermute | solution.py:411
  24.5 37.3 %all-to-all-start = ((f32[64,8,128]{2,1,0:T(8,128)}), f32[64,8,128]{2,1,0:T(8,128)S(1)}, u32[]{:S(2)}, u32[]{:S(2)}) async-start(f32[64,8,128]{2,1,0:T(8,128)} %broadcast_in_dim.12), calls=%async_computation | async-start | bytes 524288 | tf_op jit(solution)/shard_map/all_to_all | solution.py:406
  41.0 12.8 %collective-permute-start.5 = (f32[2,4,8,256]{3,2,1,0:T(8,128)S(1)}, f32[2,4,8,256]{3,2,1,0:T(8,128)S(1)}, u32[]{:S(2)}, u32[]{:S(2)}) collective-permute-start(f32[2,4,8,256]{3,2,1,0:T(8,128)S(1)} %get-tuple-element.32.one), channel_id=1, source_target_pairs={{8,0},{16,8},{24,16},{32,24},{40,32},{48,40},{56,48},{64,56},{72,6... | collective-permute-start | bytes 196616 | tf_op jit(solution)/shard_map/ppermute | solution.py:416
  42.3 11.5 %collective-permute-start.4 = (f32[2,4,8,256]{3,2,1,0:T(8,128)S(1)}, f32[2,4,8,256]{3,2,1,0:T(8,128)S(1)}, u32[]{:S(2)}, u32[]{:S(2)}) collective-permute-start(f32[2,4,8,256]{3,2,1,0:T(8,128)S(1)} %get-tuple-element.32.one), channel_id=1, source_target_pairs={{0,8},{8,16},{16,24},{24,32},{32,40},{40,48},{48,56},{56,64},{64,7... | collective-permute-start | bytes 196616 | tf_op jit(solution)/shard_map/ppermute | solution.py:411
  80.6 15.5 %all-to-all-start.2 = ((f32[16,16,128]{2,1,0:T(8,128)}), f32[16,16,128]{2,1,0:T(8,128)S(1)}, u32[]{:S(2)}, u32[]{:S(2)}) async-start(f32[16,16,128]{2,1,0:T(8,128)} %broadcast_in_dim.14), calls=%async_computation.2 | async-start | bytes 262144 | tf_op jit(solution)/shard_map/all_to_all | solution.py:406
  84.1 4.4 %collective-permute-start.6 = (f32[1,8,256]{2,1,0:T(8,128)S(1)}, f32[1,8,256]{2,1,0:T(8,128)S(1)}, u32[]{:S(2)}, u32[]{:S(2)}) collective-permute-start(f32[1,8,256]{2,1,0:T(8,128)S(1)} %get-tuple-element.35), channel_id=1, source_target_pairs={{0,8},{8,16},{16,24},{24,32},{32,40},{40,48},{48,56},{56,64},{64,7... | collective-permute-start | bytes 24584 | tf_op jit(solution)/shard_map/ppermute | solution.py:411
  87.3 4.7 %collective-permute-start.7 = (f32[1,8,256]{2,1,0:T(8,128)S(1)}, f32[1,8,256]{2,1,0:T(8,128)S(1)}, u32[]{:S(2)}, u32[]{:S(2)}) collective-permute-start(f32[1,8,256]{2,1,0:T(8,128)S(1)} %get-tuple-element.37), channel_id=1, source_target_pairs={{8,0},{16,8},{24,16},{32,24},{40,32},{48,40},{56,48},{64,56},{72,6... | collective-permute-start | bytes 24584 | tf_op jit(solution)/shard_map/ppermute | solution.py:416

commit v5 on v4

--- a/solution.py
+++ b/solution.py
@@ -13,7 +13,6 @@
 EXT = OWN + 2 * HALO
 LANES = 256
 F32 = jnp.float32
-DEEP = 16
 SUMS = 44
 
 
@@ -310,83 +309,95 @@
     rows = pack_rows(leave_one(below_two, vd1[3:9], vi1[3:9]), small)
     sums = place([total(own_r, own_z), total(own_z, own_q)], rows.shape, SUMS)
     lane = iota(rows.shape, 1)
-    send[...] = jnp.where((lane == SUMS) | (lane == SUMS + 1), sums, rows)
-
-
-def window_kernel(narrow, got, send, own, right, left):
-    me = lax.axis_index("narrow")
-    for y in range(got.shape[0] // narrow):
-        rows = slice(4 * y, 4 * y + 4)
-        own[rows, :] = got[y * narrow + me]
-        right[rows, :] = got[y * narrow + jnp.minimum(me + 1, narrow - 1)]
-        left[rows, :] = got[y * narrow + jnp.maximum(me - 1, 0)]
+    send[0:4, :] = jnp.where((lane == SUMS) | (lane == SUMS + 1), sums, rows)
+    send[4:8, :] = jnp.zeros(rows.shape, F32)
+
+
+def window_kernel(own, right, left, send):
     lane = iota(own.shape, 1)
     cell = lane % 64
     halo = jnp.where(cell < 48, roll(right[...], 32, 1), roll(left[...], 32, 1))
-    tile = jnp.where(cell < 32, own[...], halo)
-    scalars = jnp.sum(jnp.sum(got[...], axis=0), axis=0, keepdims=True) * 0.25
-    send[...] = jnp.where((lane == SUMS) | (lane == SUMS + 1), scalars, tile)
-
-
-def split_deep(ref, wide):
+    keep = (cell < 32) | (lane == SUMS) | (lane == SUMS + 1)
+    send[...] = jnp.where(keep, own[...], halo)[0:4]
+
+
+def split_rows(ref, wide):
     sides = [[], []]
-    across = wide // DEEP
     for z in range(4):
-        rows = [ref[pl.ds(4 * y + z, DEEP, stride=4 * across), :] for y in range(across)]
-        for side, value in zip(sides, both_halves(jnp.concatenate(rows, 0))):
+        for side, value in zip(sides, both_halves(ref[pl.ds(z, wide, stride=4), :])):
             side.append(value)
     return sides
 
 
-def up_again_kernel(wide, narrow, got, first, source, r0, d0, i0, below, r1, above, d1, i1, z0, z1, image1, res1, sums, known, scratch):
+def up_again_kernel(wide, narrow, got, first, source, r0, d0, i0, below, r1, above, d1, i1, z0, w0, y0, sums, scratch):
     me_w, me_n = lax.axis_index("wide"), lax.axis_index("narrow")
-    r2 = split_deep(got, wide)
+    r2 = split_rows(got, wide)
     d2 = each(lambda t: both_halves(t)[1], split_two(first, wide))
     e2 = solve_coarse(r2, d2, me_n, narrow)
     vr1 = jnp.concatenate([below[...], r1[...], above[...]], axis=0)
     e1 = rise(e2, scratch, me_w, 1, vr1, d1[...], i1[...])
     extra, inverse = rows_of(d0, 3, 15), rows_of(i0, 3, 15)
     vw, vy = finish(double_rows(e1), rows_of(source, 1, 13), extra, inverse)
-    vw = [v[1:-1] for v in vw]
-    stride = 4 * (wide // DEEP)
-    scalars = jnp.sum(got[pl.ds(0, DEEP, stride=stride), :], axis=0, keepdims=True)
+    w = [v[1:-1, :, :128] for v in vw]
+    y = [v[:, :, :128] for v in vy]
+    scalars = jnp.sum(got[pl.ds(0, wide, stride=4), :], axis=0, keepdims=True)
     lane = iota((1, 128), 1)
     rho = jnp.sum(jnp.where(lane == SUMS, scalars, 0.0), keepdims=True)
     curve = jnp.sum(jnp.where(lane == SUMS + 1, scalars, 0.0), keepdims=True)
-    alpha = (rho / curve).reshape(1, 1, 1)
-    own = slice(HALO, HALO + OWN)
-    vz0 = [z0[p] for p in range(2)]
-    vq0 = [source[p, 3:11, :, :128] for p in range(2)]
-    vz1 = [vz0[p] - alpha * vw[p][:, :, :128] for p in range(2)]
-    vi1 = [vq0[p] - alpha * vy[p][:, :, :128] for p in range(2)]
-    vr1 = [r0[p, own, :, :128] - alpha * vq0[p] for p in range(2)]
+    ratio = rho / jnp.where(curve > 0.0, curve, 1.0)
+    shift = jnp.where(curve > 0.0, jnp.minimum(jnp.maximum(ratio, 0.0), 8.0), 0.0)
+    s = shift.reshape(1, 1, 1)
+    z = [z0[p] for p in range(2)]
+    q = [source[p, 3:11, :, :128] for p in range(2)]
+    r = [r0[p, HALO : HALO + OWN, :, :128] for p in range(2)]
     for p in range(2):
-        z1[p] = vz1[p]
-        image1[p] = vi1[p]
-        res1[p] = vr1[p]
-    cross = total(vz1, vq0) + total(vz0, vi1)
-    sums[...] = place([total(vr1, vz1), total(vz1, vi1), cross], (1, 128), 0)
-    known[...] = place([rho, curve], (1, 128), 0)
-
-
-def last_kernel(got, known, z0, source, z1, image1, res1, field, residual):
-    scalars = jnp.sum(got[...], axis=0, keepdims=True)
-    lane = iota((1, 128), 1)
-
-    def pick(vector, at):
-        return jnp.sum(jnp.where(lane == at, vector, 0.0), keepdims=True)
-
-    rho, curve = pick(known[...], 0), pick(known[...], 1)
-    rho_next, square, cross = (pick(scalars, i) for i in range(3))
+        w0[p] = w[p]
+        y0[p] = y[p]
+    rs = [r[p] - s * q[p] for p in range(2)]
+    zs = [z[p] - s * w[p] for p in range(2)]
+    ys = [q[p] - s * y[p] for p in range(2)]
+    values = [
+        shift,
+        total(r, z),
+        total(z, q),
+        total(rs, zs),
+        total(rs, w) + total(q, zs),
+        total(q, w),
+        total(zs, ys),
+        total(w, ys) + total(zs, y),
+        total(w, y),
+        total(zs, q) + total(z, ys),
+        total(w, q) + total(z, y),
+    ]
+    sums[...] = place(values, (1, 128), 0)
+
+
+def last_kernel(got, z0, source, w0, y0, r0, field, residual):
+    lane = iota(got.shape, 1)
+
+    def pick(at):
+        return jnp.sum(jnp.where(lane == at, got[...], 0.0), axis=1, keepdims=True)
+
+    def whole(columns):
+        return jnp.sum(columns, axis=0, keepdims=True)
+
+    shift, g = pick(0), [pick(i) for i in range(1, 11)]
+    rho, curve = whole(g[0]), whole(g[1])
     alpha = rho / curve
+    t = alpha - shift
+    rho_next = whole(g[2] - t * (g[3] - t * g[4]))
+    square = whole(g[5] - t * (g[6] - t * g[7]))
+    cross = whole(g[8] - t * g[9])
     beta = rho_next / rho
     alpha_next = rho_next / (square + beta * cross + beta * beta * curve)
     for p in range(2):
         for x in range(OWN):
             rows = pl.ds(x + 8 * p, 8, stride=16)
             z, q = z0[p, x], source[p, 3 + x, :, :128]
-            field[rows, :] = alpha * z + alpha_next * (z1[p, x] + beta * z)
-            residual[rows, :] = res1[p, x] - alpha_next * (image1[p, x] + beta * q)
+            step = (z - alpha * w0[p, x]) + beta * z
+            image = (q - alpha * y0[p, x]) + beta * q
+            field[rows, :] = alpha * z + alpha_next * step
+            residual[rows, :] = (r0[p, HALO + x, :, :128] - alpha * q) - alpha_next * image
 
 
 def call(kernel, outs, *args, scratch=(), space=pltpu.VMEM, limit=40):
@@ -400,10 +411,10 @@
     )(*args)
 
 
-def gathered(array, axis, groups=None):
-    peers = lax.axis_size(axis) if groups is None else len(groups[0])
+def gathered(array, axis):
+    peers = lax.axis_size(axis)
     slots = jnp.broadcast_to(array[None], (peers,) + array.shape)
-    return lax.all_to_all(slots, axis, 0, 0, axis_index_groups=groups)
+    return lax.all_to_all(slots, axis, 0, 0)
 
 
 def to_next(array, axis):
@@ -414,6 +425,11 @@
 def to_previous(array, axis):
     n = lax.axis_size(axis)
     return lax.ppermute(array, axis, [(i + 1, i) for i in range(n - 1)])
+
+
+def around(array, axis, step):
+    n = lax.axis_size(axis)
+    return lax.ppermute(array, axis, [(i, (i + step) % n) for i in range(n)])
 
 
 def on_device(right_side, capacity, phase, mold_flags):
@@ -432,7 +448,7 @@
     below, above = to_next(high, "wide"), to_previous(low, "wide")
     a = jnp.concatenate([below[0], own[0], above[0]], axis=1)
     b = jnp.concatenate([below[1], own[1], above[1]], axis=1)
-    from_left, from_right = to_next(b, "narrow"), to_previous(a, "narrow")
+    from_left, from_right = around(b, "narrow", 1), around(a, "narrow", -1)
     fine = (2, EXT, 8, LANES)
     r0, d0, i0, one, send = call(
         functools.partial(down_kernel, wide, narrow),
@@ -445,35 +461,26 @@
     scratch = [pltpu.VMEM((8, wide + 16, 128), F32)]
     z0, source, r1, d1, i1, low, high, send = call(
         functools.partial(turn_kernel, wide, narrow),
-        [block, (2, 14, 8, LANES), (6, 8, LANES), coarse, coarse, line, line, (4, 128)],
+        [block, (2, 14, 8, LANES), (6, 8, LANES), coarse, coarse, line, line, (8, 128)],
         first, r0, d0, i0, one, below, above,
         scratch=scratch + [pltpu.VMEM((8, 128), F32)],
     )
     below, above = to_next(high, "wide"), to_previous(low, "wide")
-    across = wide // DEEP
-    near = [
-        [(DEEP * y + z) * narrow + n for y in range(across) for n in range(narrow)]
-        for z in range(DEEP)
-    ]
-    far = [[DEEP * y + z for z in range(DEEP)] for y in range(across)]
-    rows = (4 * across, 128)
-    (send,) = call(
-        functools.partial(window_kernel, narrow),
-        [rows],
-        gathered(send, ("wide", "narrow"), near),
-        scratch=[pltpu.VMEM(rows, F32)] * 3,
-    )
-    second = gathered(send, "wide", far).reshape(DEEP * 4 * across, 128)
-    z1, image1, res1, sums, known = call(
+    from_left, from_right = around(send, "narrow", 1), around(send, "narrow", -1)
+    (send,) = call(window_kernel, [(4, 128)], send, from_right, from_left)
+    second = gathered(send, "wide").reshape(4 * wide, 128)
+    w0, y0, sums = call(
         functools.partial(up_again_kernel, wide, narrow),
-        [block, block, block, (1, 128), (1, 128)],
+        [block, block, (1, 128)],
         second, first, source, r0, d0, i0, below, r1, above, d1, i1, z0,
         scratch=scratch,
     )
-    sums = jnp.sum(gathered(sums, "narrow"), axis=0)
-    third = gathered(sums, "wide").reshape(wide, 128)
+    parts = gathered(sums, "wide")
+    first_lane = jnp.arange(128) == 0
+    sums = jnp.where(first_lane, parts[0], jnp.sum(parts, axis=0))
+    third = gathered(sums, "narrow").reshape(narrow, 128)
     field, residual = call(
-        last_kernel, [(128, 128), (128, 128)], third, known, z0, source, z1, image1, res1
+        last_kernel, [(128, 128), (128, 128)], third, z0, source, w0, y0, r0
     )
     return field.reshape(right_side.shape), residual.reshape(right_side.shape)
 

time: 130 us -> 123 us (0.946)
  blocking collectives: 47 us -> 31 us
  starting transfers between devices: 44 us -> 50.4 us
  waiting for transfers between devices: 28.4 us -> 31.4 us
    all_to_all x3 -> x2, blocking collectives: 47 us -> 31 us  [gathered(): return lax.all_to_all(slots, axis, 0, 0)]
    ppermute x0 -> x4, starting transfers between devices: none -> 11.2 us  [around(): return lax.ppermute(array, axis, [(i, (i + step) % n) for i in range(n)])]
    ppermute x4 -> x3, starting transfers between devices: 10.5 us -> 3.88 us  [to_previous(): return lax.ppermute(array, axis, [(i + 1, i) for i in range(n - 1)])]
    ppermute x0 -> x4, waiting for transfers between devices: none -> 5.12 us  [around(): return lax.ppermute(array, axis, [(i, (i + step) % n) for i in range(n)])]
    all_to_all x2, starting transfers between devices: 20.1 us -> 24.1 us  [gathered(): return lax.all_to_all(slots, axis, 0, 0)]
    ppermute x4 -> x3, waiting for transfers between devices: 14.3 us -> 11.8 us  [to_previous(): return lax.ppermute(array, axis, [(i + 1, i) for i in range(n - 1)])]
    ppermute x4 -> x3, starting transfers between devices: 13.4 us -> 11.3 us  [to_next(): return lax.ppermute(array, axis, [(i, i + 1) for i in range(n - 1)])]
    all_to_all x2, waiting for transfers between devices: 12.1 us -> 13.6 us  [gathered(): return lax.all_to_all(slots, axis, 0, 0)]
  transfers between devices with their start and end apart: 10 -> 12, of which waited for: 6 -> 10; matrix products, arithmetic and copies ran while one was open for 1% -> 1% of each run, Pallas kernels for 0% -> 0%
where the time goes in v5:
time: 123 us
  starting transfers between devices  50.4 us (41%)
  waiting for transfers between devices  31.4 us (26%)
  blocking collectives  31 us (25%)
  Pallas kernels  6.78 us (6%)
  local copies, waits for them, and re-layouts  2.32 us (2%)
    all_to_all x2, blocking collectives, gathered(): return lax.all_to_all(slots, axis, 0, 0)  31 us
    all_to_all x2, starting transfers between devices, gathered(): return lax.all_to_all(slots, axis, 0, 0)  24.1 us
    all_to_all x2, waiting for transfers between devices, gathered(): return lax.all_to_all(slots, axis, 0, 0)  13.6 us
    ppermute x3, waiting for transfers between devices, to_previous(): return lax.ppermute(array, axis, [(i + 1, i) for i in range(n - 1)])  11.8 us
    ppermute x3, starting transfers between devices, to_next(): return lax.ppermute(array, axis, [(i, i + 1) for i in range(n - 1)])  11.3 us
    ppermute x4, starting transfers between devices, around(): return lax.ppermute(array, axis, [(i, (i + step) % n) for i in range(n)])  11.2 us
    pallas_call x6, Pallas kernels, call(): pl.pallas_call(kernel, out_shape=tuple((jax.ShapeDtypeStruct(s, F32) for...  6.78 us
    ppermute x4, waiting for transfers between devices, around(): return lax.ppermute(array, axis, [(i, (i + step) % n) for i in range(n)])  5.12 us
  transfers between devices with their start and end apart: 12, of which 10 were waited for; matrix products, arithmetic and copies ran while one was open for 1% of the time, Pallas kernels for 0%

profile of v5, /device:TPU:1, one launch (start us, length us, event | category | flops | bytes accessed | tf_op | source)
XLA Modules:
  0.0 122.8 jit_solution(8036133637103319812)
XLA Ops:
  0.6 1.8 %shard_map.59 = (f32[2,2,8,8,128]{4,3,2,1,0:T(8,128)}, f32[2,2,5,8,128]{4,3,2,1,0:T(8,128)}, f32[2,2,5,8,128]{4,3,2,1,0:T(8,128)}) custom-call(f32[128,128]{1,0:T(8,128)} %bitcast.31, f32[128,128]{1,0:T(8,128)} %bitcast.32, s32[128,128]{1,0:T(8,128)} %bitcast.33, s32[128,128]{1,0:T(8,128)} %bitcast.34), custom_call_target="tpu_custom_call" | custom-call | tf_op jit(solution)/shard_map/pallas_call | solution.py:404
  2.4 4.4 %collective-permute-start = (f32[2,2,5,8,128]{4,3,2,1,0:T(8,128)}, f32[2,2,5,8,128]{4,3,2,1,0:T(8,128)S(1)}, u32[]{:S(2)}, u32[]{:S(2)}) collective-permute-start(f32[2,2,5,8,128]{4,3,2,1,0:T(8,128)} %get-tuple-element.23), channel_id=1, source_target_pairs={{0,8},{8,16},{16,24},{24,32},{32,40},{40,48},{48,56},{56,64},{64,7... | collective-permute-start | bytes 245768 | tf_op jit(solution)/shard_map/ppermute | solution.py:422
  6.8 1.3 %collective-permute-start.1 = (f32[2,2,5,8,128]{4,3,2,1,0:T(8,128)}, f32[2,2,5,8,128]{4,3,2,1,0:T(8,128)S(1)}, u32[]{:S(2)}, u32[]{:S(2)}) collective-permute-start(f32[2,2,5,8,128]{4,3,2,1,0:T(8,128)} %get-tuple-element.25), channel_id=1, source_target_pairs={{8,0},{16,8},{24,16},{32,24},{40,32},{48,40},{56,48},{64,56},{72,6... | collective-permute-start | bytes 245768 | tf_op jit(solution)/shard_map/ppermute | solution.py:427
  8.1 0.9 slice_bitcast_fusion
  9.0 3.4 %collective-permute-done.1 = f32[2,2,5,8,128]{4,3,2,1,0:T(8,128)S(1)} collective-permute-done((f32[2,2,5,8,128]{4,3,2,1,0:T(8,128)}, f32[2,2,5,8,128]{4,3,2,1,0:T(8,128)S(1)}, u32[]{:S(2)}, u32[]{:S(2)}) %collective-permute-start.1) | collective-permute-done | bytes 81952 | tf_op jit(solution)/shard_map/ppermute | solution.py:427
  12.4 4.8 %collective-permute-start.3 = (f32[2,18,8,128]{3,2,1,0:T(8,128)S(1)}, f32[2,18,8,128]{3,2,1,0:T(8,128)S(1)}, u32[]{:S(2)}, u32[]{:S(2)}) collective-permute-start(f32[2,18,8,128]{3,2,1,0:T(8,128)S(1)} %pad_maximum_fusion.a), channel_id=1, source_target_pairs={{0,7},{1,0},{2,1},{3,2},{4,3},{5,4},{6,5},{7,6},{8,15},{9,8},{10,9... | collective-permute-start | bytes 442376 | tf_op jit(solution)/shard_map/ppermute | solution.py:432
  17.2 1.0 collective-permute-done.3.from_right
  18.3 1.1 collective-permute-done.2.from_left
  20.7 17.3 %all-to-all-start = ((f32[64,8,128]{2,1,0:T(8,128)}), f32[64,8,128]{2,1,0:T(8,128)S(1)}, u32[]{:S(2)}, u32[]{:S(2)}) async-start(f32[64,8,128]{2,1,0:T(8,128)} %broadcast_in_dim.14), calls=%async_computation | async-start | bytes 524288 | tf_op jit(solution)/shard_map/all_to_all | solution.py:417
  37.9 1.3 %collective-permute-start.5 = (f32[2,4,8,256]{3,2,1,0:T(8,128)S(1)}, f32[2,4,8,256]{3,2,1,0:T(8,128)S(1)}, u32[]{:S(2)}, u32[]{:S(2)}) collective-permute-start(f32[2,4,8,256]{3,2,1,0:T(8,128)S(1)} %get-tuple-element.30.one), channel_id=1, source_target_pairs={{8,0},{16,8},{24,16},{32,24},{40,32},{48,40},{56,48},{64,56},{72,6... | collective-permute-start | bytes 196616 | tf_op jit(solution)/shard_map/ppermute | solution.py:427
  39.2 4.0 %collective-permute-start.4 = (f32[2,4,8,256]{3,2,1,0:T(8,128)S(1)}, f32[2,4,8,256]{3,2,1,0:T(8,128)S(1)}, u32[]{:S(2)}, u32[]{:S(2)}) collective-permute-start(f32[2,4,8,256]{3,2,1,0:T(8,128)S(1)} %get-tuple-element.30.one), channel_id=1, source_target_pairs={{0,8},{8,16},{16,24},{24,32},{32,40},{40,48},{48,56},{56,64},{64,7... | collective-permute-start | bytes 196616 | tf_op jit(solution)/shard_map/ppermute | solution.py:422
  43.2 5.0 %collective-permute-done.5.above = f32[2,4,8,256]{3,2,1,0:T(8,128)S(1)} collective-permute-done((f32[2,4,8,256]{3,2,1,0:T(8,128)S(1)}, f32[2,4,8,256]{3,2,1,0:T(8,128)S(1)}, u32[]{:S(2)}, u32[]{:S(2)}) %collective-permute-start.5) | collective-permute-done | bytes 65568 | tf_op jit(solution)/shard_map/ppermute | solution.py:427
  49.1 5.9 %all-to-all-done = f32[64,8,128]{2,1,0:T(8,128)S(1)} async-done(((f32[64,8,128]{2,1,0:T(8,128)}), f32[64,8,128]{2,1,0:T(8,128)S(1)}, u32[]{:S(2)}, u32[]{:S(2)}) %all-to-all-start) | async-done | bytes 262176 | tf_op jit(solution)/shard_map/all_to_all | solution.py:417
  55.1 2.0 %shard_map.61 = (f32[2,8,8,128]{3,2,1,0:T(8,128)S(1)}, f32[2,14,8,256]{3,2,1,0:T(8,128)S(1)}, f32[6,8,256]{2,1,0:T(8,128)S(1)}, f32[8,8,256]{2,1,0:T(8,128)S(1)}...) custom-call(f32[512,128]{1,0:T(8,128)S(1)} %bitcast.26, ...), custom_call_target="tpu_custom_call" | custom-call | tf_op jit(solution)/shard_map/pallas_call | solution.py:404
  57.1 6.4 %collective-permute-start.7 = (f32[8,128]{1,0:T(8,128)S(1)}, f32[8,128]{1,0:T(8,128)S(1)}, u32[]{:S(2)}, u32[]{:S(2)}) collective-permute-start(f32[8,128]{1,0:T(8,128)S(1)} %get-tuple-element.31.own), channel_id=1, source_target_pairs={{0,1},{1,2},{2,3},{3,4},{4,5},{5,6},{6,7},{7,0},{8,9},{9,10},{10,1... | collective-permute-start | bytes 12296 | tf_op jit(solution)/shard_map/ppermute | solution.py:432
  64.3 2.3 %collective-permute-done.6.right = f32[8,128]{1,0:T(8,128)S(1)} collective-permute-done((f32[8,128]{1,0:T(8,128)S(1)}, f32[8,128]{1,0:T(8,128)S(1)}, u32[]{:S(2)}, u32[]{:S(2)}) %collective-permute-start.6) | collective-permute-done | bytes 4128 | tf_op jit(solution)/shard_map/ppermute | solution.py:432
  67.3 6.8 %all-to-all-start.1 = ((f32[64,4,128]{2,1,0:T(4,128)}), f32[64,4,128]{2,1,0:T(4,128)S(1)}, u32[]{:S(2)}, u32[]{:S(2)}) async-start(f32[64,4,128]{2,1,0:T(4,128)} %broadcast_in_dim.15), calls=%async_computation.1 | async-start | bytes 262144 | tf_op jit(solution)/shard_map/all_to_all | solution.py:417
  74.1 2.9 %collective-permute-start.8 = (f32[1,8,256]{2,1,0:T(8,128)S(1)}, f32[1,8,256]{2,1,0:T(8,128)S(1)}, u32[]{:S(2)}, u32[]{:S(2)}) collective-permute-start(f32[1,8,256]{2,1,0:T(8,128)S(1)} %get-tuple-element.33), channel_id=1, source_target_pairs={{0,8},{8,16},{16,24},{24,32},{32,40},{40,48},{48,56},{56,64},{64,7... | collective-permute-start | bytes 24584 | tf_op jit(solution)/shard_map/ppermute | solution.py:422
  77.0 1.3 %collective-permute-start.9 = (f32[1,8,256]{2,1,0:T(8,128)S(1)}, f32[1,8,256]{2,1,0:T(8,128)S(1)}, u32[]{:S(2)}, u32[]{:S(2)}) collective-permute-start(f32[1,8,256]{2,1,0:T(8,128)S(1)} %get-tuple-element.35), channel_id=1, source_target_pairs={{8,0},{16,8},{24,16},{32,24},{40,32},{48,40},{56,48},{64,56},{72,6... | collective-permute-start | bytes 24584 | tf_op jit(solution)/shard_map/ppermute | solution.py:427
  78.3 3.4 %collective-permute-done.9.above = f32[1,8,256]{2,1,0:T(8,128)S(1)} collective-permute-done((f32[1,8,256]{2,1,0:T(8,128)S(1)}, f32[1,8,256]{2,1,0:T(8,128)S(1)}, u32[]{:S(2)}, u32[]{:S(2)}) %collective-permute-start.9) | collective-permute-done | bytes 8224 | tf_op jit(solution)/shard_map/ppermute | solution.py:427
  81.7 7.6 %all-to-all-done.1 = f32[64,4,128]{2,1,0:T(4,128)S(1)} async-done(((f32[64,4,128]{2,1,0:T(4,128)}), f32[64,4,128]{2,1,0:T(4,128)S(1)}, u32[]{:S(2)}, u32[]{:S(2)}) %all-to-all-start.1) | async-done | bytes 131104 | tf_op jit(solution)/shard_map/all_to_all | solution.py:417
  89.4 1.5 %shard_map.63 = (f32[2,8,8,128]{3,2,1,0:T(8,128)S(1)}, f32[2,8,8,128]{3,2,1,0:T(8,128)S(1)}, f32[1,128]{1,0:T(1,128)S(1)}) custom-call(f32[256,128]{1,0:T(8,128)S(1)} %bitcast.28, f32[512,128]{1,0:T(8,128)S(1)} %bitcast.27, f32[2,14,8,256]{3,2,1,0:T(8,128)S(1)} %get-tuple-element.32.source, f32[2,18,8,256]{3,2,1,0:T(8,128)S(1)} %get-tuple-element.27.r0, ...), custom_call_target="tpu_custom_call" | custom-call | tf_op jit(solution)/shard_map/pallas_call | solution.py:404
  90.9 20.2 %all_to_all.20 = f32[64,1,128]{2,1,0:T(1,128)S(1)} all-to-all(f32[64,1,128]{2,1,0:T(1,128)S(1)} %broadcast_in_dim.17), channel_id=1, replica_groups=mesh['wide'=64,'narrow'=8] {'wide'}, dimensions={0} | all-to-all | bytes 65536 | tf_op jit(solution)/shard_map/all_to_all | solution.py:417
  111.2 10.7 %all_to_all.21 = f32[8,1,128]{2,1,0:T(1,128)S(1)} all-to-all(f32[8,1,128]{2,1,0:T(1,128)S(1)} %broadcast_in_dim.35), channel_id=1, replica_groups=mesh['wide'=64,'narrow'=8] {'narrow'}, dimensions={0} | all-to-all | bytes 8192 | tf_op jit(solution)/shard_map/all_to_all | solution.py:417
  (19 shorter events, 4.7 us)
Async XLA Ops:
  2.4 6.6 %collective-permute-start = (f32[2,2,5,8,128]{4,3,2,1,0:T(8,128)}, f32[2,2,5,8,128]{4,3,2,1,0:T(8,128)S(1)}, u32[]{:S(2)}, u32[]{:S(2)}) collective-permute-start(f32[2,2,5,8,128]{4,3,2,1,0:T(8,128)} %get-tuple-element.23), channel_id=1, source_target_pairs={{0,8},{8,16},{16,24},{24,32},{32,40},{40,48},{48,56},{56,64},{64,7... | collective-permute-start | bytes 245768 | tf_op jit(solution)/shard_map/ppermute | solution.py:422
  6.8 5.6 %collective-permute-start.1 = (f32[2,2,5,8,128]{4,3,2,1,0:T(8,128)}, f32[2,2,5,8,128]{4,3,2,1,0:T(8,128)S(1)}, u32[]{:S(2)}, u32[]{:S(2)}) collective-permute-start(f32[2,2,5,8,128]{4,3,2,1,0:T(8,128)} %get-tuple-element.25), channel_id=1, source_target_pairs={{8,0},{16,8},{24,16},{32,24},{40,32},{48,40},{56,48},{64,56},{72,6... | collective-permute-start | bytes 245768 | tf_op jit(solution)/shard_map/ppermute | solution.py:427
  12.4 5.9 %collective-permute-start.3 = (f32[2,18,8,128]{3,2,1,0:T(8,128)S(1)}, f32[2,18,8,128]{3,2,1,0:T(8,128)S(1)}, u32[]{:S(2)}, u32[]{:S(2)}) collective-permute-start(f32[2,18,8,128]{3,2,1,0:T(8,128)S(1)} %pad_maximum_fusion.a), channel_id=1, source_target_pairs={{0,7},{1,0},{2,1},{3,2},{4,3},{5,4},{6,5},{7,6},{8,15},{9,8},{10,9... | collective-permute-start | bytes 442376 | tf_op jit(solution)/shard_map/ppermute | solution.py:432
  17.2 2.1 %collective-permute-start.2 = (f32[2,18,8,128]{3,2,1,0:T(8,128)S(1)}, f32[2,18,8,128]{3,2,1,0:T(8,128)S(1)}, u32[]{:S(2)}, u32[]{:S(2)}) collective-permute-start(f32[2,18,8,128]{3,2,1,0:T(8,128)S(1)} %pad_maximum_fusion.1.b), channel_id=1, source_target_pairs={{0,1},{1,2},{2,3},{3,4},{4,5},{5,6},{6,7},{7,0},{8,9},{9,10},{10,1... | collective-permute-start | bytes 442376 | tf_op jit(solution)/shard_map/ppermute | solution.py:432
  20.7 34.4 %all-to-all-start = ((f32[64,8,128]{2,1,0:T(8,128)}), f32[64,8,128]{2,1,0:T(8,128)S(1)}, u32[]{:S(2)}, u32[]{:S(2)}) async-start(f32[64,8,128]{2,1,0:T(8,128)} %broadcast_in_dim.14), calls=%async_computation | async-start | bytes 524288 | tf_op jit(solution)/shard_map/all_to_all | solution.py:417
  37.9 10.3 %collective-permute-start.5 = (f32[2,4,8,256]{3,2,1,0:T(8,128)S(1)}, f32[2,4,8,256]{3,2,1,0:T(8,128)S(1)}, u32[]{:S(2)}, u32[]{:S(2)}) collective-permute-start(f32[2,4,8,256]{3,2,1,0:T(8,128)S(1)} %get-tuple-element.30.one), channel_id=1, source_target_pairs={{8,0},{16,8},{24,16},{32,24},{40,32},{48,40},{56,48},{64,56},{72,6... | collective-permute-start | bytes 196616 | tf_op jit(solution)/shard_map/ppermute | solution.py:427
  39.2 9.9 %collective-permute-start.4 = (f32[2,4,8,256]{3,2,1,0:T(8,128)S(1)}, f32[2,4,8,256]{3,2,1,0:T(8,128)S(1)}, u32[]{:S(2)}, u32[]{:S(2)}) collective-permute-start(f32[2,4,8,256]{3,2,1,0:T(8,128)S(1)} %get-tuple-element.30.one), channel_id=1, source_target_pairs={{0,8},{8,16},{16,24},{24,32},{32,40},{40,48},{48,56},{56,64},{64,7... | collective-permute-start | bytes 196616 | tf_op jit(solution)/shard_map/ppermute | solution.py:422
  57.1 7.2 %collective-permute-start.7 = (f32[8,128]{1,0:T(8,128)S(1)}, f32[8,128]{1,0:T(8,128)S(1)}, u32[]{:S(2)}, u32[]{:S(2)}) collective-permute-start(f32[8,128]{1,0:T(8,128)S(1)} %get-tuple-element.31.own), channel_id=1, source_target_pairs={{0,1},{1,2},{2,3},{3,4},{4,5},{5,6},{6,7},{7,0},{8,9},{9,10},{10,1... | collective-permute-start | bytes 12296 | tf_op jit(solution)/shard_map/ppermute | solution.py:432
  63.5 3.0 %collective-permute-start.6 = (f32[8,128]{1,0:T(8,128)S(1)}, f32[8,128]{1,0:T(8,128)S(1)}, u32[]{:S(2)}, u32[]{:S(2)}) collective-permute-start(f32[8,128]{1,0:T(8,128)S(1)} %get-tuple-element.31.own), channel_id=1, source_target_pairs={{0,7},{1,0},{2,1},{3,2},{4,3},{5,4},{6,5},{7,6},{8,15},{9,8},{10,9... | collective-permute-start | bytes 12296 | tf_op jit(solution)/shard_map/ppermute | solution.py:432
  67.3 22.1 %all-to-all-start.1 = ((f32[64,4,128]{2,1,0:T(4,128)}), f32[64,4,128]{2,1,0:T(4,128)S(1)}, u32[]{:S(2)}, u32[]{:S(2)}) async-start(f32[64,4,128]{2,1,0:T(4,128)} %broadcast_in_dim.15), calls=%async_computation.1 | async-start | bytes 262144 | tf_op jit(solution)/shard_map/all_to_all | solution.py:417
  74.1 4.2 %collective-permute-start.8 = (f32[1,8,256]{2,1,0:T(8,128)S(1)}, f32[1,8,256]{2,1,0:T(8,128)S(1)}, u32[]{:S(2)}, u32[]{:S(2)}) collective-permute-start(f32[1,8,256]{2,1,0:T(8,128)S(1)} %get-tuple-element.33), channel_id=1, source_target_pairs={{0,8},{8,16},{16,24},{24,32},{32,40},{40,48},{48,56},{56,64},{64,7... | collective-permute-start | bytes 24584 | tf_op jit(solution)/shard_map/ppermute | solution.py:422
  77.0 4.7 %collective-permute-start.9 = (f32[1,8,256]{2,1,0:T(8,128)S(1)}, f32[1,8,256]{2,1,0:T(8,128)S(1)}, u32[]{:S(2)}, u32[]{:S(2)}) collective-permute-start(f32[1,8,256]{2,1,0:T(8,128)S(1)} %get-tuple-element.35), channel_id=1, source_target_pairs={{8,0},{16,8},{24,16},{32,24},{40,32},{48,40},{56,48},{64,56},{72,6... | collective-permute-start | bytes 24584 | tf_op jit(solution)/shard_map/ppermute | solution.py:427

commit v6 on v5

--- a/solution.py
+++ b/solution.py
@@ -13,6 +13,7 @@
 EXT = OWN + 2 * HALO
 LANES = 256
 F32 = jnp.float32
+DEEP = 16
 SUMS = 44
 
 
@@ -245,7 +246,7 @@
                     high[side, p, x - (OWN - HALO)] = value
 
 
-def down_kernel(wide, narrow, a, b, from_left, from_right, r0, d0, i0, one, send):
+def down_kernel(wide, narrow, a, b, from_left, from_right, r0, d0, i0, one, low, high, send):
     me_w, me_n = lax.axis_index("wide"), lax.axis_index("narrow")
     shape = (EXT, 8, 128)
     half = iota(shape, 2) < 64
@@ -267,12 +268,16 @@
         r0[p] = source[p]
         d0[p] = extra[p]
         i0[p] = inverse[p]
-    vr1 = descend(source, extra, inverse)[1:7]
-    vd1 = restrict_fine(extra[0][3:15], extra[1][3:15])
-    vi1 = invert_one(vd1, -1, me_w, me_n, wide, narrow)
-    one[0] = vr1[1:5]
-    one[1] = vd1[1:5]
-    send[...] = pack_two(leave_one(vr1, vd1, vi1), 0) + pack_two(vd1[1:5], 64)
+    vr1 = descend(source, extra, inverse)
+    vd1 = restrict_fine(extra[0][1:17], extra[1][1:17])
+    vi1 = invert_one(vd1, -2, me_w, me_n, wide, narrow)
+    for side, value in ((0, vr1), (1, vd1)):
+        one[side] = value
+        high[side] = value[2:4]
+        low[side] = value[4:6]
+    left = leave_one(vr1[1:7], vd1[1:7], vi1[1:7])
+    tile = pack_two(left, 0) + pack_two(vd1[2:6], 64)
+    send[...] = jnp.broadcast_to(tile, send.shape)
 
 
 def both_halves(tile):
@@ -318,7 +323,7 @@
     cell = lane % 64
     halo = jnp.where(cell < 48, roll(right[...], 32, 1), roll(left[...], 32, 1))
     keep = (cell < 32) | (lane == SUMS) | (lane == SUMS + 1)
-    send[...] = jnp.where(keep, own[...], halo)[0:4]
+    send[...] = jnp.broadcast_to(jnp.where(keep, own[...], halo)[0:4], send.shape)
 
 
 def split_rows(ref, wide):
@@ -369,7 +374,7 @@
         total(zs, q) + total(z, ys),
         total(w, q) + total(z, y),
     ]
-    sums[...] = place(values, (1, 128), 0)
+    sums[...] = jnp.broadcast_to(place(values, (1, 128), 0), sums.shape)
 
 
 def last_kernel(got, z0, source, w0, y0, r0, field, residual):
@@ -411,10 +416,8 @@
     )(*args)
 
 
-def gathered(array, axis):
-    peers = lax.axis_size(axis)
-    slots = jnp.broadcast_to(array[None], (peers,) + array.shape)
-    return lax.all_to_all(slots, axis, 0, 0)
+def exchange(slots, axis, groups=None):
+    return lax.all_to_all(slots, axis, 0, 0, axis_index_groups=groups)
 
 
 def to_next(array, axis):
@@ -449,14 +452,14 @@
     a = jnp.concatenate([below[0], own[0], above[0]], axis=1)
     b = jnp.concatenate([below[1], own[1], above[1]], axis=1)
     from_left, from_right = around(b, "narrow", 1), around(a, "narrow", -1)
-    fine = (2, EXT, 8, LANES)
-    r0, d0, i0, one, send = call(
+    fine, pair = (2, EXT, 8, LANES), (2, 2, 8, LANES)
+    r0, d0, i0, one, low, high, send = call(
         functools.partial(down_kernel, wide, narrow),
-        [fine, fine, fine, (2, 4, 8, LANES), (8, 128)],
+        [fine, fine, fine, (2, 8, 8, LANES), pair, pair, (wide, 8, 128)],
         a, b, from_left, from_right,
     )
-    below, above = to_next(one, "wide"), to_previous(one, "wide")
-    first = gathered(send, "wide").reshape(8 * wide, 128)
+    below, above = to_next(high, "wide"), to_previous(low, "wide")
+    first = exchange(send, "wide").reshape(8 * wide, 128)
     block, coarse, line = (2, OWN, 8, 128), (8, 8, LANES), (1, 8, LANES)
     scratch = [pltpu.VMEM((8, wide + 16, 128), F32)]
     z0, source, r1, d1, i1, low, high, send = call(
@@ -467,18 +470,24 @@
     )
     below, above = to_next(high, "wide"), to_previous(low, "wide")
     from_left, from_right = around(send, "narrow", 1), around(send, "narrow", -1)
-    (send,) = call(window_kernel, [(4, 128)], send, from_right, from_left)
-    second = gathered(send, "wide").reshape(4 * wide, 128)
+    (send,) = call(window_kernel, [(wide, 4, 128)], send, from_right, from_left)
+    second = exchange(send, "wide").reshape(4 * wide, 128)
     w0, y0, sums = call(
         functools.partial(up_again_kernel, wide, narrow),
-        [block, block, (1, 128)],
+        [block, block, (DEEP, 1, 128)],
         second, first, source, r0, d0, i0, below, r1, above, d1, i1, z0,
         scratch=scratch,
     )
-    parts = gathered(sums, "wide")
-    first_lane = jnp.arange(128) == 0
-    sums = jnp.where(first_lane, parts[0], jnp.sum(parts, axis=0))
-    third = gathered(sums, "narrow").reshape(narrow, 128)
+    across = wide // DEEP
+    far = [[DEEP * y + z for z in range(DEEP)] for y in range(across)]
+    near = [
+        [(DEEP * y + z) * narrow + n for y in range(across) for n in range(narrow)]
+        for z in range(DEEP)
+    ]
+    parts = exchange(sums, "wide", far)
+    sums = jnp.where(jnp.arange(128) == 0, parts[0], jnp.sum(parts, axis=0))
+    sums = jnp.broadcast_to(sums[None], (across * narrow,) + sums.shape)
+    third = exchange(sums, ("wide", "narrow"), near).reshape(across * narrow, 128)
     field, residual = call(
         last_kernel, [(128, 128), (128, 128)], third, z0, source, w0, y0, r0
     )

time: 123 us -> 122 us (level)
  Pallas kernels: 6.78 us -> 8.22 us
  local copies, waits for them, and re-layouts: 2.32 us -> 0.91 us
    pallas_call x6, Pallas kernels: 6.78 us -> 8.22 us  [call(): pl.pallas_call(kernel, out_shape=tuple((jax.ShapeDtypeStruct(s, F32) for...]
    broadcast_in_dim x4 -> x1, local copies, waits for them, and re-layouts: 1.42 us -> 0.01 us  [on_device(): sums = jnp.broadcast_to(sums[None], (across * narrow,) + sums.shape)]
where the time goes in v6:
time: 122 us
  starting transfers between devices  49.2 us (40%)
  waiting for transfers between devices  32.2 us (26%)
  blocking collectives  30.6 us (25%)
  Pallas kernels  8.22 us (7%)
    all_to_all x2, blocking collectives, exchange(): return lax.all_to_all(slots, axis, 0, 0, axis_index_groups=groups)  30.6 us
    all_to_all x2, starting transfers between devices, exchange(): return lax.all_to_all(slots, axis, 0, 0, axis_index_groups=groups)  23.7 us
    all_to_all x2, waiting for transfers between devices, exchange(): return lax.all_to_all(slots, axis, 0, 0, axis_index_groups=groups)  14.2 us
    ppermute x4, starting transfers between devices, around(): return lax.ppermute(array, axis, [(i, (i + step) % n) for i in range(n)])  11.4 us
    ppermute x3, waiting for transfers between devices, to_previous(): return lax.ppermute(array, axis, [(i + 1, i) for i in range(n - 1)])  11.1 us
    ppermute x3, starting transfers between devices, to_next(): return lax.ppermute(array, axis, [(i, i + 1) for i in range(n - 1)])  10.2 us
    pallas_call x6, Pallas kernels, call(): pl.pallas_call(kernel, out_shape=tuple((jax.ShapeDtypeStruct(s, F32) for...  8.22 us
    ppermute x4, waiting for transfers between devices, around(): return lax.ppermute(array, axis, [(i, (i + step) % n) for i in range(n)])  5.12 us
  transfers between devices with their start and end apart: 12, of which 10 were waited for; matrix products, arithmetic and copies ran while one was open for 1% of the time, Pallas kernels for 0%

profile of v6, /device:TPU:1, one launch (start us, length us, event | category | flops | bytes accessed | tf_op | source)
XLA Modules:
  0.0 122.0 jit_solution(12902698206655249632)
XLA Ops:
  0.6 1.8 %shard_map.59 = (f32[2,2,8,8,128]{4,3,2,1,0:T(8,128)}, f32[2,2,5,8,128]{4,3,2,1,0:T(8,128)}, f32[2,2,5,8,128]{4,3,2,1,0:T(8,128)}) custom-call(f32[128,128]{1,0:T(8,128)} %bitcast.29, f32[128,128]{1,0:T(8,128)} %bitcast.30, s32[128,128]{1,0:T(8,128)} %bitcast.31, s32[128,128]{1,0:T(8,128)} %bitcast.32), custom_call_target="tpu_custom_call" | custom-call | tf_op jit(solution)/shard_map/pallas_call | solution.py:409
  2.4 4.4 %collective-permute-start = (f32[2,2,5,8,128]{4,3,2,1,0:T(8,128)}, f32[2,2,5,8,128]{4,3,2,1,0:T(8,128)S(1)}, u32[]{:S(2)}, u32[]{:S(2)}) collective-permute-start(f32[2,2,5,8,128]{4,3,2,1,0:T(8,128)} %get-tuple-element.25), channel_id=1, source_target_pairs={{0,8},{8,16},{16,24},{24,32},{32,40},{40,48},{48,56},{56,64},{64,7... | collective-permute-start | bytes 245768 | tf_op jit(solution)/shard_map/ppermute | solution.py:425
  6.8 1.3 %collective-permute-start.1 = (f32[2,2,5,8,128]{4,3,2,1,0:T(8,128)}, f32[2,2,5,8,128]{4,3,2,1,0:T(8,128)S(1)}, u32[]{:S(2)}, u32[]{:S(2)}) collective-permute-start(f32[2,2,5,8,128]{4,3,2,1,0:T(8,128)} %get-tuple-element.27), channel_id=1, source_target_pairs={{8,0},{16,8},{24,16},{32,24},{40,32},{48,40},{56,48},{64,56},{72,6... | collective-permute-start | bytes 245768 | tf_op jit(solution)/shard_map/ppermute | solution.py:430
  9.0 3.4 %collective-permute-done.1 = f32[2,2,5,8,128]{4,3,2,1,0:T(8,128)S(1)} collective-permute-done((f32[2,2,5,8,128]{4,3,2,1,0:T(8,128)}, f32[2,2,5,8,128]{4,3,2,1,0:T(8,128)S(1)}, u32[]{:S(2)}, u32[]{:S(2)}) %collective-permute-start.1) | collective-permute-done | bytes 81952 | tf_op jit(solution)/shard_map/ppermute | solution.py:430
  12.4 4.8 %collective-permute-start.3 = (f32[2,18,8,128]{3,2,1,0:T(8,128)S(1)}, f32[2,18,8,128]{3,2,1,0:T(8,128)S(1)}, u32[]{:S(2)}, u32[]{:S(2)}) collective-permute-start(f32[2,18,8,128]{3,2,1,0:T(8,128)S(1)} %pad_maximum_fusion.a), channel_id=1, source_target_pairs={{0,7},{1,0},{2,1},{3,2},{4,3},{5,4},{6,5},{7,6},{8,15},{9,8},{10,9... | collective-permute-start | bytes 442376 | tf_op jit(solution)/shard_map/ppermute | solution.py:435
  18.3 1.1 collective-permute-done.2.from_left
  19.3 1.3 %shard_map.60 = (f32[2,18,8,256]{3,2,1,0:T(8,128)S(1)}, f32[2,18,8,256]{3,2,1,0:T(8,128)S(1)}, f32[2,18,8,256]{3,2,1,0:T(8,128)S(1)}, f32[2,8,8,256]{3,2,1,0:T(8...) custom-call(f32[2,18,8,128]{3,2,1,0:T(8,128)S(1)} %pad_maximum_fusion.a, ...), custom_call_target="tpu_custom_call" | custom-call | tf_op jit(solution)/shard_map/pallas_call | solution.py:409
  20.7 17.3 %all-to-all-start = ((f32[64,8,128]{2,1,0:T(8,128)}), f32[64,8,128]{2,1,0:T(8,128)S(1)}, u32[]{:S(2)}, u32[]{:S(2)}) async-start(f32[64,8,128]{2,1,0:T(8,128)} %get-tuple-element.28), calls=%async_computation | async-start | bytes 524288 | tf_op jit(solution)/shard_map/all_to_all | solution.py:420
  37.9 2.9 %collective-permute-start.4 = (f32[2,2,8,256]{3,2,1,0:T(8,128)S(1)}, f32[2,2,8,256]{3,2,1,0:T(8,128)S(1)}, u32[]{:S(2)}, u32[]{:S(2)}) collective-permute-start(f32[2,2,8,256]{3,2,1,0:T(8,128)S(1)} %get-tuple-element.33), channel_id=1, source_target_pairs={{0,8},{8,16},{16,24},{24,32},{32,40},{40,48},{48,56},{56,64},{64,7... | collective-permute-start | bytes 98312 | tf_op jit(solution)/shard_map/ppermute | solution.py:425
  40.9 1.3 %collective-permute-start.5 = (f32[2,2,8,256]{3,2,1,0:T(8,128)S(1)}, f32[2,2,8,256]{3,2,1,0:T(8,128)S(1)}, u32[]{:S(2)}, u32[]{:S(2)}) collective-permute-start(f32[2,2,8,256]{3,2,1,0:T(8,128)S(1)} %get-tuple-element.34), channel_id=1, source_target_pairs={{8,0},{16,8},{24,16},{32,24},{40,32},{48,40},{56,48},{64,56},{72,6... | collective-permute-start | bytes 98312 | tf_op jit(solution)/shard_map/ppermute | solution.py:430
  42.2 1.8 %collective-permute-done.4.below = f32[2,2,8,256]{3,2,1,0:T(8,128)S(1)} collective-permute-done((f32[2,2,8,256]{3,2,1,0:T(8,128)S(1)}, f32[2,2,8,256]{3,2,1,0:T(8,128)S(1)}, u32[]{:S(2)}, u32[]{:S(2)}) %collective-permute-start.4) | collective-permute-done | bytes 32800 | tf_op jit(solution)/shard_map/ppermute | solution.py:425
  44.0 4.3 %collective-permute-done.5.above = f32[2,2,8,256]{3,2,1,0:T(8,128)S(1)} collective-permute-done((f32[2,2,8,256]{3,2,1,0:T(8,128)S(1)}, f32[2,2,8,256]{3,2,1,0:T(8,128)S(1)}, u32[]{:S(2)}, u32[]{:S(2)}) %collective-permute-start.5) | collective-permute-done | bytes 32800 | tf_op jit(solution)/shard_map/ppermute | solution.py:430
  48.3 6.6 %all-to-all-done = f32[64,8,128]{2,1,0:T(8,128)S(1)} async-done(((f32[64,8,128]{2,1,0:T(8,128)}), f32[64,8,128]{2,1,0:T(8,128)S(1)}, u32[]{:S(2)}, u32[]{:S(2)}) %all-to-all-start) | async-done | bytes 262176 | tf_op jit(solution)/shard_map/all_to_all | solution.py:420
  54.9 2.0 %shard_map.61 = (f32[2,8,8,128]{3,2,1,0:T(8,128)S(1)}, f32[2,14,8,256]{3,2,1,0:T(8,128)S(1)}, f32[6,8,256]{2,1,0:T(8,128)S(1)}, f32[8,8,256]{2,1,0:T(8,128)S(1)}...) custom-call(f32[512,128]{1,0:T(8,128)S(1)} %bitcast.25, ...), custom_call_target="tpu_custom_call" | custom-call | tf_op jit(solution)/shard_map/pallas_call | solution.py:409
  56.9 6.6 %collective-permute-start.7 = (f32[8,128]{1,0:T(8,128)S(1)}, f32[8,128]{1,0:T(8,128)S(1)}, u32[]{:S(2)}, u32[]{:S(2)}) collective-permute-start(f32[8,128]{1,0:T(8,128)S(1)} %get-tuple-element.35.own), channel_id=1, source_target_pairs={{0,1},{1,2},{2,3},{3,4},{4,5},{5,6},{6,7},{7,0},{8,9},{9,10},{10,1... | collective-permute-start | bytes 12296 | tf_op jit(solution)/shard_map/ppermute | solution.py:435
  64.3 2.3 %collective-permute-done.6.right = f32[8,128]{1,0:T(8,128)S(1)} collective-permute-done((f32[8,128]{1,0:T(8,128)S(1)}, f32[8,128]{1,0:T(8,128)S(1)}, u32[]{:S(2)}, u32[]{:S(2)}) %collective-permute-start.6) | collective-permute-done | bytes 4128 | tf_op jit(solution)/shard_map/ppermute | solution.py:435
  67.3 6.4 %all-to-all-start.1 = ((f32[64,4,128]{2,1,0:T(4,128)}), f32[64,4,128]{2,1,0:T(4,128)S(1)}, u32[]{:S(2)}, u32[]{:S(2)}) async-start(f32[64,4,128]{2,1,0:T(4,128)} %shard_map.62), calls=%async_computation.1 | async-start | bytes 262144 | tf_op jit(solution)/shard_map/all_to_all | solution.py:420
  73.7 2.9 %collective-permute-start.8 = (f32[1,8,256]{2,1,0:T(8,128)S(1)}, f32[1,8,256]{2,1,0:T(8,128)S(1)}, u32[]{:S(2)}, u32[]{:S(2)}) collective-permute-start(f32[1,8,256]{2,1,0:T(8,128)S(1)} %get-tuple-element.37), channel_id=1, source_target_pairs={{0,8},{8,16},{16,24},{24,32},{32,40},{40,48},{48,56},{56,64},{64,7... | collective-permute-start | bytes 24584 | tf_op jit(solution)/shard_map/ppermute | solution.py:425
  76.7 1.3 %collective-permute-start.9 = (f32[1,8,256]{2,1,0:T(8,128)S(1)}, f32[1,8,256]{2,1,0:T(8,128)S(1)}, u32[]{:S(2)}, u32[]{:S(2)}) collective-permute-start(f32[1,8,256]{2,1,0:T(8,128)S(1)} %get-tuple-element.39), channel_id=1, source_target_pairs={{8,0},{16,8},{24,16},{32,24},{40,32},{48,40},{56,48},{64,56},{72,6... | collective-permute-start | bytes 24584 | tf_op jit(solution)/shard_map/ppermute | solution.py:430
  78.0 3.4 %collective-permute-done.9.above = f32[1,8,256]{2,1,0:T(8,128)S(1)} collective-permute-done((f32[1,8,256]{2,1,0:T(8,128)S(1)}, f32[1,8,256]{2,1,0:T(8,128)S(1)}, u32[]{:S(2)}, u32[]{:S(2)}) %collective-permute-start.9) | collective-permute-done | bytes 8224 | tf_op jit(solution)/shard_map/ppermute | solution.py:430
  81.4 7.6 %all-to-all-done.1 = f32[64,4,128]{2,1,0:T(4,128)S(1)} async-done(((f32[64,4,128]{2,1,0:T(4,128)}), f32[64,4,128]{2,1,0:T(4,128)S(1)}, u32[]{:S(2)}, u32[]{:S(2)}) %all-to-all-start.1) | async-done | bytes 131104 | tf_op jit(solution)/shard_map/all_to_all | solution.py:420
  89.0 1.5 %shard_map.63 = (f32[2,8,8,128]{3,2,1,0:T(8,128)S(1)}, f32[2,8,8,128]{3,2,1,0:T(8,128)S(1)}, f32[16,1,128]{2,1,0:T(1,128)S(1)}) custom-call(f32[256,128]{1,0:T(8,128)S(1)} %bitcast.27, f32[512,128]{1,0:T(8,128)S(1)} %bitcast.26, f32[2,14,8,256]{3,2,1,0:T(8,128)S(1)} %get-tuple-element.36.source, f32[2,18,8,256]{3,2,1,0:T(8,128)S(1)} %get-tuple-element.29.r0, ...), custom_call_target="tpu_custom_call" | custom-call | tf_op jit(solution)/shard_map/pallas_call | solution.py:409
  90.5 15.6 %all_to_all.20 = f32[16,1,128]{2,1,0:T(1,128)S(1)} all-to-all(f32[16,1,128]{2,1,0:T(1,128)S(1)} %get-tuple-element.43), channel_id=1, replica_groups={{0,8,16,24,32,40,48,56,64,72,80,88,96,104,112,120},{128,136,144,152,160..., dimensions={0} | all-to-all | bytes 16384 | tf_op jit(solution)/shard_map/all_to_all | solution.py:420
  106.2 15.0 %all_to_all.21 = f32[32,1,128]{2,1,0:T(1,128)S(1)} all-to-all(f32[32,1,128]{2,1,0:T(1,128)S(1)} %broadcast_in_dim.11), channel_id=1, replica_groups={{0,1,2,3,4,5,6,7,128,129,130,131,132,133,134,135,256,257,258,259,260,26..., dimensions={0} | all-to-all | bytes 32768 | tf_op jit(solution)/shard_map/all_to_all | solution.py:420
  (16 shorter events, 4.3 us)
Async XLA Ops:
  2.4 6.6 %collective-permute-start = (f32[2,2,5,8,128]{4,3,2,1,0:T(8,128)}, f32[2,2,5,8,128]{4,3,2,1,0:T(8,128)S(1)}, u32[]{:S(2)}, u32[]{:S(2)}) collective-permute-start(f32[2,2,5,8,128]{4,3,2,1,0:T(8,128)} %get-tuple-element.25), channel_id=1, source_target_pairs={{0,8},{8,16},{16,24},{24,32},{32,40},{40,48},{48,56},{56,64},{64,7... | collective-permute-start | bytes 245768 | tf_op jit(solution)/shard_map/ppermute | solution.py:425
  6.8 5.6 %collective-permute-start.1 = (f32[2,2,5,8,128]{4,3,2,1,0:T(8,128)}, f32[2,2,5,8,128]{4,3,2,1,0:T(8,128)S(1)}, u32[]{:S(2)}, u32[]{:S(2)}) collective-permute-start(f32[2,2,5,8,128]{4,3,2,1,0:T(8,128)} %get-tuple-element.27), channel_id=1, source_target_pairs={{8,0},{16,8},{24,16},{32,24},{40,32},{48,40},{56,48},{64,56},{72,6... | collective-permute-start | bytes 245768 | tf_op jit(solution)/shard_map/ppermute | solution.py:430
  12.4 5.9 %collective-permute-start.3 = (f32[2,18,8,128]{3,2,1,0:T(8,128)S(1)}, f32[2,18,8,128]{3,2,1,0:T(8,128)S(1)}, u32[]{:S(2)}, u32[]{:S(2)}) collective-permute-start(f32[2,18,8,128]{3,2,1,0:T(8,128)S(1)} %pad_maximum_fusion.a), channel_id=1, source_target_pairs={{0,7},{1,0},{2,1},{3,2},{4,3},{5,4},{6,5},{7,6},{8,15},{9,8},{10,9... | collective-permute-start | bytes 442376 | tf_op jit(solution)/shard_map/ppermute | solution.py:435
  17.2 2.1 %collective-permute-start.2 = (f32[2,18,8,128]{3,2,1,0:T(8,128)S(1)}, f32[2,18,8,128]{3,2,1,0:T(8,128)S(1)}, u32[]{:S(2)}, u32[]{:S(2)}) collective-permute-start(f32[2,18,8,128]{3,2,1,0:T(8,128)S(1)} %pad_maximum_fusion.1.b), channel_id=1, source_target_pairs={{0,1},{1,2},{2,3},{3,4},{4,5},{5,6},{6,7},{7,0},{8,9},{9,10},{10,1... | collective-permute-start | bytes 442376 | tf_op jit(solution)/shard_map/ppermute | solution.py:435
  20.7 34.2 %all-to-all-start = ((f32[64,8,128]{2,1,0:T(8,128)}), f32[64,8,128]{2,1,0:T(8,128)S(1)}, u32[]{:S(2)}, u32[]{:S(2)}) async-start(f32[64,8,128]{2,1,0:T(8,128)} %get-tuple-element.28), calls=%async_computation | async-start | bytes 524288 | tf_op jit(solution)/shard_map/all_to_all | solution.py:420
  37.9 6.0 %collective-permute-start.4 = (f32[2,2,8,256]{3,2,1,0:T(8,128)S(1)}, f32[2,2,8,256]{3,2,1,0:T(8,128)S(1)}, u32[]{:S(2)}, u32[]{:S(2)}) collective-permute-start(f32[2,2,8,256]{3,2,1,0:T(8,128)S(1)} %get-tuple-element.33), channel_id=1, source_target_pairs={{0,8},{8,16},{16,24},{24,32},{32,40},{40,48},{48,56},{56,64},{64,7... | collective-permute-start | bytes 98312 | tf_op jit(solution)/shard_map/ppermute | solution.py:425
  40.9 7.4 %collective-permute-start.5 = (f32[2,2,8,256]{3,2,1,0:T(8,128)S(1)}, f32[2,2,8,256]{3,2,1,0:T(8,128)S(1)}, u32[]{:S(2)}, u32[]{:S(2)}) collective-permute-start(f32[2,2,8,256]{3,2,1,0:T(8,128)S(1)} %get-tuple-element.34), channel_id=1, source_target_pairs={{8,0},{16,8},{24,16},{32,24},{40,32},{48,40},{56,48},{64,56},{72,6... | collective-permute-start | bytes 98312 | tf_op jit(solution)/shard_map/ppermute | solution.py:430
  56.9 7.4 %collective-permute-start.7 = (f32[8,128]{1,0:T(8,128)S(1)}, f32[8,128]{1,0:T(8,128)S(1)}, u32[]{:S(2)}, u32[]{:S(2)}) collective-permute-start(f32[8,128]{1,0:T(8,128)S(1)} %get-tuple-element.35.own), channel_id=1, source_target_pairs={{0,1},{1,2},{2,3},{3,4},{4,5},{5,6},{6,7},{7,0},{8,9},{9,10},{10,1... | collective-permute-start | bytes 12296 | tf_op jit(solution)/shard_map/ppermute | solution.py:435
  63.5 3.0 %collective-permute-start.6 = (f32[8,128]{1,0:T(8,128)S(1)}, f32[8,128]{1,0:T(8,128)S(1)}, u32[]{:S(2)}, u32[]{:S(2)}) collective-permute-start(f32[8,128]{1,0:T(8,128)S(1)} %get-tuple-element.35.own), channel_id=1, source_target_pairs={{0,7},{1,0},{2,1},{3,2},{4,3},{5,4},{6,5},{7,6},{8,15},{9,8},{10,9... | collective-permute-start | bytes 12296 | tf_op jit(solution)/shard_map/ppermute | solution.py:435
  67.3 21.6 %all-to-all-start.1 = ((f32[64,4,128]{2,1,0:T(4,128)}), f32[64,4,128]{2,1,0:T(4,128)S(1)}, u32[]{:S(2)}, u32[]{:S(2)}) async-start(f32[64,4,128]{2,1,0:T(4,128)} %shard_map.62), calls=%async_computation.1 | async-start | bytes 262144 | tf_op jit(solution)/shard_map/all_to_all | solution.py:420
  73.7 4.2 %collective-permute-start.8 = (f32[1,8,256]{2,1,0:T(8,128)S(1)}, f32[1,8,256]{2,1,0:T(8,128)S(1)}, u32[]{:S(2)}, u32[]{:S(2)}) collective-permute-start(f32[1,8,256]{2,1,0:T(8,128)S(1)} %get-tuple-element.37), channel_id=1, source_target_pairs={{0,8},{8,16},{16,24},{24,32},{32,40},{40,48},{48,56},{56,64},{64,7... | collective-permute-start | bytes 24584 | tf_op jit(solution)/shard_map/ppermute | solution.py:425
  76.7 4.7 %collective-permute-start.9 = (f32[1,8,256]{2,1,0:T(8,128)S(1)}, f32[1,8,256]{2,1,0:T(8,128)S(1)}, u32[]{:S(2)}, u32[]{:S(2)}) collective-permute-start(f32[1,8,256]{2,1,0:T(8,128)S(1)} %get-tuple-element.39), channel_id=1, source_target_pairs={{8,0},{16,8},{24,16},{32,24},{40,32},{48,40},{56,48},{64,56},{72,6... | collective-permute-start | bytes 24584 | tf_op jit(solution)/shard_map/ppermute | solution.py:430

commit v7 on v6

--- a/solution.py
+++ b/solution.py
@@ -85,7 +85,13 @@
 
 
 def split_two(ref, wide):
-    return [[ref[pl.ds(2 * z + x, wide, stride=8), :] for z in range(4)] for x in range(2)]
+    across = wide // DEEP
+
+    def one(row):
+        parts = [ref[pl.ds(8 * y + row, DEEP, stride=8 * across), :] for y in range(across)]
+        return jnp.concatenate(parts, axis=0)
+
+    return [[one(2 * z + x) for z in range(4)] for x in range(2)]
 
 
 def add(terms):
@@ -437,6 +443,13 @@
 
 def on_device(right_side, capacity, phase, mold_flags):
     wide, narrow = lax.axis_size("wide"), lax.axis_size("narrow")
+    across = wide // DEEP
+    far = [[DEEP * y + z for z in range(DEEP)] for y in range(across)]
+    near = [
+        [(DEEP * y + z) * narrow + n for y in range(across) for n in range(narrow)]
+        for z in range(DEEP)
+    ]
+    side = [[DEEP * y + z for y in range(across)] for z in range(DEEP)]
     flat = [v.reshape(128, 128) for v in (right_side, capacity, phase, mold_flags)]
     edge = (2, 2, HALO, 8, 128)
     staged = [pltpu.VMEM((128, 128), v.dtype) for v in flat]
@@ -455,11 +468,13 @@
     fine, pair = (2, EXT, 8, LANES), (2, 2, 8, LANES)
     r0, d0, i0, one, low, high, send = call(
         functools.partial(down_kernel, wide, narrow),
-        [fine, fine, fine, (2, 8, 8, LANES), pair, pair, (wide, 8, 128)],
+        [fine, fine, fine, (2, 8, 8, LANES), pair, pair, (across, 8, 128)],
         a, b, from_left, from_right,
     )
     below, above = to_next(high, "wide"), to_previous(low, "wide")
-    first = exchange(send, "wide").reshape(8 * wide, 128)
+    send = exchange(send, "wide", side).reshape(8 * across, 128)
+    send = jnp.broadcast_to(send[None], (DEEP,) + send.shape)
+    first = exchange(send, "wide", far).reshape(8 * wide, 128)
     block, coarse, line = (2, OWN, 8, 128), (8, 8, LANES), (1, 8, LANES)
     scratch = [pltpu.VMEM((8, wide + 16, 128), F32)]
     z0, source, r1, d1, i1, low, high, send = call(
@@ -478,12 +493,6 @@
         second, first, source, r0, d0, i0, below, r1, above, d1, i1, z0,
         scratch=scratch,
     )
-    across = wide // DEEP
-    far = [[DEEP * y + z for z in range(DEEP)] for y in range(across)]
-    near = [
-        [(DEEP * y + z) * narrow + n for y in range(across) for n in range(narrow)]
-        for z in range(DEEP)
-    ]
     parts = exchange(sums, "wide", far)
     sums = jnp.where(jnp.arange(128) == 0, parts[0], jnp.sum(parts, axis=0))
     sums = jnp.broadcast_to(sums[None], (across * narrow,) + sums.shape)

time: 122 us -> 126 us (1.033)
  blocking collectives: 30.6 us -> 42.9 us
  starting transfers between devices: 49.2 us -> 44.5 us
  waiting for transfers between devices: 32.2 us -> 27.9 us
    all_to_all x2 -> x3, blocking collectives: 30.6 us -> 42.9 us  [exchange(): return lax.all_to_all(slots, axis, 0, 0, axis_index_groups=groups)]
    all_to_all x2, starting transfers between devices: 23.7 us -> 16.6 us  [exchange(): return lax.all_to_all(slots, axis, 0, 0, axis_index_groups=groups)]
    all_to_all x2, waiting for transfers between devices: 14.2 us -> 10.9 us  [exchange(): return lax.all_to_all(slots, axis, 0, 0, axis_index_groups=groups)]
    ppermute x4, starting transfers between devices: 11.4 us -> 13.5 us  [around(): return lax.ppermute(array, axis, [(i, (i + step) % n) for i in range(n)])]
where the time goes in v7:
time: 126 us; the launch traced here: 125 us
  starting transfers between devices  44.5 us (35%)
  blocking collectives  42.9 us (34%)
  waiting for transfers between devices  27.9 us (22%)
  Pallas kernels  7.66 us (6%)
  local copies, waits for them, and re-layouts  1.63 us (1%)
    all_to_all x3, blocking collectives, exchange(): return lax.all_to_all(slots, axis, 0, 0, axis_index_groups=groups)  42.9 us
    all_to_all x2, starting transfers between devices, exchange(): return lax.all_to_all(slots, axis, 0, 0, axis_index_groups=groups)  16.6 us
    ppermute x4, starting transfers between devices, around(): return lax.ppermute(array, axis, [(i, (i + step) % n) for i in range(n)])  13.5 us
    all_to_all x2, waiting for transfers between devices, exchange(): return lax.all_to_all(slots, axis, 0, 0, axis_index_groups=groups)  10.9 us
    ppermute x3, starting transfers between devices, to_next(): return lax.ppermute(array, axis, [(i, i + 1) for i in range(n - 1)])  10.5 us
    ppermute x3, waiting for transfers between devices, to_previous(): return lax.ppermute(array, axis, [(i + 1, i) for i in range(n - 1)])  10.4 us
    pallas_call x6, Pallas kernels, call(): pl.pallas_call(kernel, out_shape=tuple((jax.ShapeDtypeStruct(s, F32) for...  7.66 us
    ppermute x4, waiting for transfers between devices, around(): return lax.ppermute(array, axis, [(i, (i + step) % n) for i in range(n)])  5.12 us
  transfers between devices with their start and end apart: 12, of which 10 were waited for; matrix products, arithmetic and copies ran while one was open for 1% of the time, Pallas kernels for 0%

profile of v7, /device:TPU:1, one launch (start us, length us, event | category | flops | bytes accessed | tf_op | source)
XLA Modules:
  0.0 125.5 jit_solution(5782447152741805792)
XLA Ops:
  0.6 1.8 %shard_map.59 = (f32[2,2,8,8,128]{4,3,2,1,0:T(8,128)}, f32[2,2,5,8,128]{4,3,2,1,0:T(8,128)}, f32[2,2,5,8,128]{4,3,2,1,0:T(8,128)}) custom-call(f32[128,128]{1,0:T(8,128)} %bitcast.31, f32[128,128]{1,0:T(8,128)} %bitcast.32, s32[128,128]{1,0:T(8,128)} %bitcast.33, s32[128,128]{1,0:T(8,128)} %bitcast.34), custom_call_target="tpu_custom_call" | custom-call | tf_op jit(solution)/shard_map/pallas_call | solution.py:415
  2.4 4.4 %collective-permute-start = (f32[2,2,5,8,128]{4,3,2,1,0:T(8,128)}, f32[2,2,5,8,128]{4,3,2,1,0:T(8,128)S(1)}, u32[]{:S(2)}, u32[]{:S(2)}) collective-permute-start(f32[2,2,5,8,128]{4,3,2,1,0:T(8,128)} %get-tuple-element.25), channel_id=1, source_target_pairs={{0,8},{8,16},{16,24},{24,32},{32,40},{40,48},{48,56},{56,64},{64,7... | collective-permute-start | bytes 245768 | tf_op jit(solution)/shard_map/ppermute | solution.py:431
  6.8 1.3 %collective-permute-start.1 = (f32[2,2,5,8,128]{4,3,2,1,0:T(8,128)}, f32[2,2,5,8,128]{4,3,2,1,0:T(8,128)S(1)}, u32[]{:S(2)}, u32[]{:S(2)}) collective-permute-start(f32[2,2,5,8,128]{4,3,2,1,0:T(8,128)} %get-tuple-element.27), channel_id=1, source_target_pairs={{8,0},{16,8},{24,16},{32,24},{40,32},{48,40},{56,48},{64,56},{72,6... | collective-permute-start | bytes 245768 | tf_op jit(solution)/shard_map/ppermute | solution.py:436
  9.0 3.4 %collective-permute-done.1 = f32[2,2,5,8,128]{4,3,2,1,0:T(8,128)S(1)} collective-permute-done((f32[2,2,5,8,128]{4,3,2,1,0:T(8,128)}, f32[2,2,5,8,128]{4,3,2,1,0:T(8,128)S(1)}, u32[]{:S(2)}, u32[]{:S(2)}) %collective-permute-start.1) | collective-permute-done | bytes 81952 | tf_op jit(solution)/shard_map/ppermute | solution.py:436
  12.4 4.8 %collective-permute-start.3 = (f32[2,18,8,128]{3,2,1,0:T(8,128)S(1)}, f32[2,18,8,128]{3,2,1,0:T(8,128)S(1)}, u32[]{:S(2)}, u32[]{:S(2)}) collective-permute-start(f32[2,18,8,128]{3,2,1,0:T(8,128)S(1)} %pad_maximum_fusion.a), channel_id=1, source_target_pairs={{0,7},{1,0},{2,1},{3,2},{4,3},{5,4},{6,5},{7,6},{8,15},{9,8},{10,9... | collective-permute-start | bytes 442376 | tf_op jit(solution)/shard_map/ppermute | solution.py:441
  18.3 1.1 collective-permute-done.2.from_left
  20.0 12.5 %all_to_all.25 = f32[4,8,128]{2,1,0:T(8,128)S(1)} all-to-all(f32[4,8,128]{2,1,0:T(8,128)S(1)} %get-tuple-element.28), channel_id=1, replica_groups={{0,128,256,384},{8,136,264,392},{16,144,272,400},{24,152,280,408},{32,1..., dimensions={0} | all-to-all | bytes 32768 | tf_op jit(solution)/shard_map/all_to_all | solution.py:426
  33.2 9.5 %all-to-all-start.1 = ((f32[16,32,128]{2,1,0:T(8,128)}), f32[16,32,128]{2,1,0:T(8,128)S(1)}, u32[]{:S(2)}, u32[]{:S(2)}) async-start(f32[16,32,128]{2,1,0:T(8,128)} %broadcast_in_dim.18), calls=%async_computation.1 | async-start | bytes 524288 | tf_op jit(solution)/shard_map/all_to_all | solution.py:426
  42.7 3.3 %collective-permute-start.4 = (f32[2,2,8,256]{3,2,1,0:T(8,128)S(1)}, f32[2,2,8,256]{3,2,1,0:T(8,128)S(1)}, u32[]{:S(2)}, u32[]{:S(2)}) collective-permute-start(f32[2,2,8,256]{3,2,1,0:T(8,128)S(1)} %get-tuple-element.33), channel_id=1, source_target_pairs={{0,8},{8,16},{16,24},{24,32},{32,40},{40,48},{48,56},{56,64},{64,7... | collective-permute-start | bytes 98312 | tf_op jit(solution)/shard_map/ppermute | solution.py:431
  45.9 1.3 %collective-permute-start.5 = (f32[2,2,8,256]{3,2,1,0:T(8,128)S(1)}, f32[2,2,8,256]{3,2,1,0:T(8,128)S(1)}, u32[]{:S(2)}, u32[]{:S(2)}) collective-permute-start(f32[2,2,8,256]{3,2,1,0:T(8,128)S(1)} %get-tuple-element.34), channel_id=1, source_target_pairs={{8,0},{16,8},{24,16},{32,24},{40,32},{48,40},{56,48},{64,56},{72,6... | collective-permute-start | bytes 98312 | tf_op jit(solution)/shard_map/ppermute | solution.py:436
  47.2 1.5 %collective-permute-done.4.below = f32[2,2,8,256]{3,2,1,0:T(8,128)S(1)} collective-permute-done((f32[2,2,8,256]{3,2,1,0:T(8,128)S(1)}, f32[2,2,8,256]{3,2,1,0:T(8,128)S(1)}, u32[]{:S(2)}, u32[]{:S(2)}) %collective-permute-start.4) | collective-permute-done | bytes 32800 | tf_op jit(solution)/shard_map/ppermute | solution.py:431
  48.7 3.6 %collective-permute-done.5.above = f32[2,2,8,256]{3,2,1,0:T(8,128)S(1)} collective-permute-done((f32[2,2,8,256]{3,2,1,0:T(8,128)S(1)}, f32[2,2,8,256]{3,2,1,0:T(8,128)S(1)}, u32[]{:S(2)}, u32[]{:S(2)}) %collective-permute-start.5) | collective-permute-done | bytes 32800 | tf_op jit(solution)/shard_map/ppermute | solution.py:436
  52.3 3.1 %all-to-all-done.1 = f32[16,32,128]{2,1,0:T(8,128)S(1)} async-done(((f32[16,32,128]{2,1,0:T(8,128)}), f32[16,32,128]{2,1,0:T(8,128)S(1)}, u32[]{:S(2)}, u32[]{:S(2)}) %all-to-all-start.1) | async-done | bytes 262176 | tf_op jit(solution)/shard_map/all_to_all | solution.py:426
  55.5 2.1 %shard_map.61 = (f32[2,8,8,128]{3,2,1,0:T(8,128)S(1)}, f32[2,14,8,256]{3,2,1,0:T(8,128)S(1)}, f32[6,8,256]{2,1,0:T(8,128)S(1)}, f32[8,8,256]{2,1,0:T(8,128)S(1)}...) custom-call(f32[512,128]{1,0:T(8,128)S(1)} %bitcast.26, ...), custom_call_target="tpu_custom_call" | custom-call | tf_op jit(solution)/shard_map/pallas_call | solution.py:415
  57.6 8.7 %collective-permute-start.7 = (f32[8,128]{1,0:T(8,128)S(1)}, f32[8,128]{1,0:T(8,128)S(1)}, u32[]{:S(2)}, u32[]{:S(2)}) collective-permute-start(f32[8,128]{1,0:T(8,128)S(1)} %get-tuple-element.35.own), channel_id=1, source_target_pairs={{0,1},{1,2},{2,3},{3,4},{4,5},{5,6},{6,7},{7,0},{8,9},{9,10},{10,1... | collective-permute-start | bytes 12296 | tf_op jit(solution)/shard_map/ppermute | solution.py:441
  67.0 2.3 %collective-permute-done.6.right = f32[8,128]{1,0:T(8,128)S(1)} collective-permute-done((f32[8,128]{1,0:T(8,128)S(1)}, f32[8,128]{1,0:T(8,128)S(1)}, u32[]{:S(2)}, u32[]{:S(2)}) %collective-permute-start.6) | collective-permute-done | bytes 4128 | tf_op jit(solution)/shard_map/ppermute | solution.py:441
  70.0 7.2 %all-to-all-start.2 = ((f32[64,4,128]{2,1,0:T(4,128)}), f32[64,4,128]{2,1,0:T(4,128)S(1)}, u32[]{:S(2)}, u32[]{:S(2)}) async-start(f32[64,4,128]{2,1,0:T(4,128)} %shard_map.62), calls=%async_computation.2 | async-start | bytes 262144 | tf_op jit(solution)/shard_map/all_to_all | solution.py:426
  77.2 2.9 %collective-permute-start.8 = (f32[1,8,256]{2,1,0:T(8,128)S(1)}, f32[1,8,256]{2,1,0:T(8,128)S(1)}, u32[]{:S(2)}, u32[]{:S(2)}) collective-permute-start(f32[1,8,256]{2,1,0:T(8,128)S(1)} %get-tuple-element.37), channel_id=1, source_target_pairs={{0,8},{8,16},{16,24},{24,32},{32,40},{40,48},{48,56},{56,64},{64,7... | collective-permute-start | bytes 24584 | tf_op jit(solution)/shard_map/ppermute | solution.py:431
  80.1 1.3 %collective-permute-start.9 = (f32[1,8,256]{2,1,0:T(8,128)S(1)}, f32[1,8,256]{2,1,0:T(8,128)S(1)}, u32[]{:S(2)}, u32[]{:S(2)}) collective-permute-start(f32[1,8,256]{2,1,0:T(8,128)S(1)} %get-tuple-element.39), channel_id=1, source_target_pairs={{8,0},{16,8},{24,16},{32,24},{40,32},{48,40},{56,48},{64,56},{72,6... | collective-permute-start | bytes 24584 | tf_op jit(solution)/shard_map/ppermute | solution.py:436
  81.4 3.5 %collective-permute-done.9.above = f32[1,8,256]{2,1,0:T(8,128)S(1)} collective-permute-done((f32[1,8,256]{2,1,0:T(8,128)S(1)}, f32[1,8,256]{2,1,0:T(8,128)S(1)}, u32[]{:S(2)}, u32[]{:S(2)}) %collective-permute-start.9) | collective-permute-done | bytes 8224 | tf_op jit(solution)/shard_map/ppermute | solution.py:436
  84.9 7.7 %all-to-all-done.2 = f32[64,4,128]{2,1,0:T(4,128)S(1)} async-done(((f32[64,4,128]{2,1,0:T(4,128)}), f32[64,4,128]{2,1,0:T(4,128)S(1)}, u32[]{:S(2)}, u32[]{:S(2)}) %all-to-all-start.2) | async-done | bytes 131104 | tf_op jit(solution)/shard_map/all_to_all | solution.py:426
  92.6 1.6 %shard_map.63 = (f32[2,8,8,128]{3,2,1,0:T(8,128)S(1)}, f32[2,8,8,128]{3,2,1,0:T(8,128)S(1)}, f32[16,1,128]{2,1,0:T(1,128)S(1)}) custom-call(f32[256,128]{1,0:T(8,128)S(1)} %bitcast.28, f32[512,128]{1,0:T(8,128)S(1)} %bitcast.27, f32[2,14,8,256]{3,2,1,0:T(8,128)S(1)} %get-tuple-element.36.source, f32[2,18,8,256]{3,2,1,0:T(8,128)S(1)} %get-tuple-element.29.r0, ...), custom_call_target="tpu_custom_call" | custom-call | tf_op jit(solution)/shard_map/pallas_call | solution.py:415
  94.2 15.5 %all_to_all.26 = f32[16,1,128]{2,1,0:T(1,128)S(1)} all-to-all(f32[16,1,128]{2,1,0:T(1,128)S(1)} %get-tuple-element.43), channel_id=1, replica_groups={{0,8,16,24,32,40,48,56,64,72,80,88,96,104,112,120},{128,136,144,152,160..., dimensions={0} | all-to-all | bytes 16384 | tf_op jit(solution)/shard_map/all_to_all | solution.py:426
  109.7 15.0 %all_to_all.27 = f32[32,1,128]{2,1,0:T(1,128)S(1)} all-to-all(f32[32,1,128]{2,1,0:T(1,128)S(1)} %broadcast_in_dim.20), channel_id=1, replica_groups={{0,1,2,3,4,5,6,7,128,129,130,131,132,133,134,135,256,257,258,259,260,26..., dimensions={0} | all-to-all | bytes 32768 | tf_op jit(solution)/shard_map/all_to_all | solution.py:426
  (18 shorter events, 5.7 us)
Async XLA Ops:
  2.4 6.6 %collective-permute-start = (f32[2,2,5,8,128]{4,3,2,1,0:T(8,128)}, f32[2,2,5,8,128]{4,3,2,1,0:T(8,128)S(1)}, u32[]{:S(2)}, u32[]{:S(2)}) collective-permute-start(f32[2,2,5,8,128]{4,3,2,1,0:T(8,128)} %get-tuple-element.25), channel_id=1, source_target_pairs={{0,8},{8,16},{16,24},{24,32},{32,40},{40,48},{48,56},{56,64},{64,7... | collective-permute-start | bytes 245768 | tf_op jit(solution)/shard_map/ppermute | solution.py:431
  6.8 5.6 %collective-permute-start.1 = (f32[2,2,5,8,128]{4,3,2,1,0:T(8,128)}, f32[2,2,5,8,128]{4,3,2,1,0:T(8,128)S(1)}, u32[]{:S(2)}, u32[]{:S(2)}) collective-permute-start(f32[2,2,5,8,128]{4,3,2,1,0:T(8,128)} %get-tuple-element.27), channel_id=1, source_target_pairs={{8,0},{16,8},{24,16},{32,24},{40,32},{48,40},{56,48},{64,56},{72,6... | collective-permute-start | bytes 245768 | tf_op jit(solution)/shard_map/ppermute | solution.py:436
  12.4 5.9 %collective-permute-start.3 = (f32[2,18,8,128]{3,2,1,0:T(8,128)S(1)}, f32[2,18,8,128]{3,2,1,0:T(8,128)S(1)}, u32[]{:S(2)}, u32[]{:S(2)}) collective-permute-start(f32[2,18,8,128]{3,2,1,0:T(8,128)S(1)} %pad_maximum_fusion.a), channel_id=1, source_target_pairs={{0,7},{1,0},{2,1},{3,2},{4,3},{5,4},{6,5},{7,6},{8,15},{9,8},{10,9... | collective-permute-start | bytes 442376 | tf_op jit(solution)/shard_map/ppermute | solution.py:441
  17.2 2.1 %collective-permute-start.2 = (f32[2,18,8,128]{3,2,1,0:T(8,128)S(1)}, f32[2,18,8,128]{3,2,1,0:T(8,128)S(1)}, u32[]{:S(2)}, u32[]{:S(2)}) collective-permute-start(f32[2,18,8,128]{3,2,1,0:T(8,128)S(1)} %pad_maximum_fusion.1.b), channel_id=1, source_target_pairs={{0,1},{1,2},{2,3},{3,4},{4,5},{5,6},{6,7},{7,0},{8,9},{9,10},{10,1... | collective-permute-start | bytes 442376 | tf_op jit(solution)/shard_map/ppermute | solution.py:441
  33.2 22.3 %all-to-all-start.1 = ((f32[16,32,128]{2,1,0:T(8,128)}), f32[16,32,128]{2,1,0:T(8,128)S(1)}, u32[]{:S(2)}, u32[]{:S(2)}) async-start(f32[16,32,128]{2,1,0:T(8,128)} %broadcast_in_dim.18), calls=%async_computation.1 | async-start | bytes 524288 | tf_op jit(solution)/shard_map/all_to_all | solution.py:426
  42.7 6.1 %collective-permute-start.4 = (f32[2,2,8,256]{3,2,1,0:T(8,128)S(1)}, f32[2,2,8,256]{3,2,1,0:T(8,128)S(1)}, u32[]{:S(2)}, u32[]{:S(2)}) collective-permute-start(f32[2,2,8,256]{3,2,1,0:T(8,128)S(1)} %get-tuple-element.33), channel_id=1, source_target_pairs={{0,8},{8,16},{16,24},{24,32},{32,40},{40,48},{48,56},{56,64},{64,7... | collective-permute-start | bytes 98312 | tf_op jit(solution)/shard_map/ppermute | solution.py:431
  45.9 6.4 %collective-permute-start.5 = (f32[2,2,8,256]{3,2,1,0:T(8,128)S(1)}, f32[2,2,8,256]{3,2,1,0:T(8,128)S(1)}, u32[]{:S(2)}, u32[]{:S(2)}) collective-permute-start(f32[2,2,8,256]{3,2,1,0:T(8,128)S(1)} %get-tuple-element.34), channel_id=1, source_target_pairs={{8,0},{16,8},{24,16},{32,24},{40,32},{48,40},{56,48},{64,56},{72,6... | collective-permute-start | bytes 98312 | tf_op jit(solution)/shard_map/ppermute | solution.py:436
  57.6 9.4 %collective-permute-start.7 = (f32[8,128]{1,0:T(8,128)S(1)}, f32[8,128]{1,0:T(8,128)S(1)}, u32[]{:S(2)}, u32[]{:S(2)}) collective-permute-start(f32[8,128]{1,0:T(8,128)S(1)} %get-tuple-element.35.own), channel_id=1, source_target_pairs={{0,1},{1,2},{2,3},{3,4},{4,5},{5,6},{6,7},{7,0},{8,9},{9,10},{10,1... | collective-permute-start | bytes 12296 | tf_op jit(solution)/shard_map/ppermute | solution.py:441
  66.2 3.0 %collective-permute-start.6 = (f32[8,128]{1,0:T(8,128)S(1)}, f32[8,128]{1,0:T(8,128)S(1)}, u32[]{:S(2)}, u32[]{:S(2)}) collective-permute-start(f32[8,128]{1,0:T(8,128)S(1)} %get-tuple-element.35.own), channel_id=1, source_target_pairs={{0,7},{1,0},{2,1},{3,2},{4,3},{5,4},{6,5},{7,6},{8,15},{9,8},{10,9... | collective-permute-start | bytes 12296 | tf_op jit(solution)/shard_map/ppermute | solution.py:441
  70.0 22.6 %all-to-all-start.2 = ((f32[64,4,128]{2,1,0:T(4,128)}), f32[64,4,128]{2,1,0:T(4,128)S(1)}, u32[]{:S(2)}, u32[]{:S(2)}) async-start(f32[64,4,128]{2,1,0:T(4,128)} %shard_map.62), calls=%async_computation.2 | async-start | bytes 262144 | tf_op jit(solution)/shard_map/all_to_all | solution.py:426
  77.2 4.2 %collective-permute-start.8 = (f32[1,8,256]{2,1,0:T(8,128)S(1)}, f32[1,8,256]{2,1,0:T(8,128)S(1)}, u32[]{:S(2)}, u32[]{:S(2)}) collective-permute-start(f32[1,8,256]{2,1,0:T(8,128)S(1)} %get-tuple-element.37), channel_id=1, source_target_pairs={{0,8},{8,16},{16,24},{24,32},{32,40},{40,48},{48,56},{56,64},{64,7... | collective-permute-start | bytes 24584 | tf_op jit(solution)/shard_map/ppermute | solution.py:431
  80.1 4.8 %collective-permute-start.9 = (f32[1,8,256]{2,1,0:T(8,128)S(1)}, f32[1,8,256]{2,1,0:T(8,128)S(1)}, u32[]{:S(2)}, u32[]{:S(2)}) collective-permute-start(f32[1,8,256]{2,1,0:T(8,128)S(1)} %get-tuple-element.39), channel_id=1, source_target_pairs={{8,0},{16,8},{24,16},{32,24},{40,32},{48,40},{56,48},{64,56},{72,6... | collective-permute-start | bytes 24584 | tf_op jit(solution)/shard_map/ppermute | solution.py:436

commit v8 on v6

--- a/solution.py
+++ b/solution.py
@@ -8,7 +8,7 @@
 from jax.sharding import PartitionSpec as P
 
 OMEGA = 0.8
-HALO = 5
+HALO = 7
 OWN = 8
 EXT = OWN + 2 * HALO
 LANES = 256
@@ -175,7 +175,9 @@
     shape = (128, LANES)
     matrix = jnp.where(iota(shape, 0) == iota(shape, 1) // 4, 1.0, 0.0).astype(F32)
     spread = jnp.dot(jnp.concatenate(rows, 0), matrix, precision=lax.Precision.HIGHEST)
-    e1 = i1 * r1 + double_rows(spread.reshape(len(rows), 8, LANES))
+    up = double_rows(spread.reshape(len(rows), 8, LANES))
+    trim = (up.shape[0] - r1.shape[0]) // 2
+    e1 = i1 * r1 + up[trim : trim + r1.shape[0]]
     return e1[1:-1] + i1[1:-1] * (r1[1:-1] - apply_one(e1, d1[1:-1]))
 
 
@@ -269,14 +271,14 @@
         d0[p] = extra[p]
         i0[p] = inverse[p]
     vr1 = descend(source, extra, inverse)
-    vd1 = restrict_fine(extra[0][1:17], extra[1][1:17])
-    vi1 = invert_one(vd1, -2, me_w, me_n, wide, narrow)
+    vd1 = restrict_fine(extra[0][1:-1], extra[1][1:-1])
+    vi1 = invert_one(vd1, -3, me_w, me_n, wide, narrow)
     for side, value in ((0, vr1), (1, vd1)):
         one[side] = value
         high[side] = value[2:4]
-        low[side] = value[4:6]
-    left = leave_one(vr1[1:7], vd1[1:7], vi1[1:7])
-    tile = pack_two(left, 0) + pack_two(vd1[2:6], 64)
+        low[side] = value[6:8]
+    left = leave_one(vr1[2:8], vd1[2:8], vi1[2:8])
+    tile = pack_two(left, 0) + pack_two(vd1[3:7], 64)
     send[...] = jnp.broadcast_to(tile, send.shape)
 
 
@@ -286,7 +288,7 @@
     return jnp.where(half, tile, other), jnp.where(half, other, tile)
 
 
-def turn_kernel(wide, narrow, got, r0, d0, i0, one, below, above, z, q, r1, d1, i1, low, high, send, scratch, small):
+def turn_kernel(wide, narrow, got, r0, d0, i0, one, below, above, z, q, r1, d1, i1, send, scratch, small):
     me_w, me_n = lax.axis_index("wide"), lax.axis_index("narrow")
     tiles = split_two(got, wide)
     r2 = each(lambda t: both_halves(t)[0], tiles)
@@ -294,24 +296,22 @@
     e2 = solve_coarse(r2, d2, me_n, narrow)
     vr1 = jnp.concatenate([below[0], one[0], above[0]], axis=0)
     vd1 = jnp.concatenate([below[1], one[1], above[1]], axis=0)
-    vi1 = invert_one(vd1, -4, me_w, me_n, wide, narrow)
-    e1 = rise(e2, scratch, me_w, 2, vr1, vd1, vi1)
+    vi1 = invert_one(vd1, -5, me_w, me_n, wide, narrow)
+    e1 = rise(e2, scratch, me_w, 3, vr1, vd1, vi1)
     up = double_rows(e1)[1:-1]
     source, extra, inverse = (rows_of(ref, 0, EXT) for ref in (r0, d0, i0))
     vz, vq = finish(up, source, extra, inverse)
-    own_z = [v[4:12, :, :128] for v in vz]
-    own_q = [v[3:11, :, :128] for v in vq]
+    own_z = [v[6:14, :, :128] for v in vz]
+    own_q = [v[5:13, :, :128] for v in vq]
     own_r = [v[HALO : HALO + OWN, :, :128] for v in source]
     for p in range(2):
         z[p] = own_z[p]
         q[p] = vq[p]
-    below_two = descend(vq, rows_of(d0, 2, 16), rows_of(i0, 2, 16))
+    below_two = descend(vq, rows_of(d0, 2, 20), rows_of(i0, 2, 20))
     r1[...] = below_two
-    d1[...] = vd1[2:10]
-    i1[...] = vi1[2:10]
-    low[...] = below_two[2:3]
-    high[...] = below_two[3:4]
-    rows = pack_rows(leave_one(below_two, vd1[3:9], vi1[3:9]), small)
+    d1[...] = vd1[3:11]
+    i1[...] = vi1[3:11]
+    rows = pack_rows(leave_one(below_two[1:7], vd1[4:10], vi1[4:10]), small)
     sums = place([total(own_r, own_z), total(own_z, own_q)], rows.shape, SUMS)
     lane = iota(rows.shape, 1)
     send[0:4, :] = jnp.where((lane == SUMS) | (lane == SUMS + 1), sums, rows)
@@ -334,15 +334,14 @@
     return sides
 
 
-def up_again_kernel(wide, narrow, got, first, source, r0, d0, i0, below, r1, above, d1, i1, z0, w0, y0, sums, scratch):
+def up_again_kernel(wide, narrow, got, first, source, r0, d0, i0, r1, d1, i1, z0, w0, y0, sums, scratch):
     me_w, me_n = lax.axis_index("wide"), lax.axis_index("narrow")
     r2 = split_rows(got, wide)
     d2 = each(lambda t: both_halves(t)[1], split_two(first, wide))
     e2 = solve_coarse(r2, d2, me_n, narrow)
-    vr1 = jnp.concatenate([below[...], r1[...], above[...]], axis=0)
-    e1 = rise(e2, scratch, me_w, 1, vr1, d1[...], i1[...])
-    extra, inverse = rows_of(d0, 3, 15), rows_of(i0, 3, 15)
-    vw, vy = finish(double_rows(e1), rows_of(source, 1, 13), extra, inverse)
+    e1 = rise(e2, scratch, me_w, 1, r1[...], d1[...], i1[...])
+    extra, inverse = rows_of(d0, 5, 17), rows_of(i0, 5, 17)
+    vw, vy = finish(double_rows(e1), rows_of(source, 3, 15), extra, inverse)
     w = [v[1:-1, :, :128] for v in vw]
     y = [v[:, :, :128] for v in vy]
     scalars = jnp.sum(got[pl.ds(0, wide, stride=4), :], axis=0, keepdims=True)
@@ -353,7 +352,7 @@
     shift = jnp.where(curve > 0.0, jnp.minimum(jnp.maximum(ratio, 0.0), 8.0), 0.0)
     s = shift.reshape(1, 1, 1)
     z = [z0[p] for p in range(2)]
-    q = [source[p, 3:11, :, :128] for p in range(2)]
+    q = [source[p, 5:13, :, :128] for p in range(2)]
     r = [r0[p, HALO : HALO + OWN, :, :128] for p in range(2)]
     for p in range(2):
         w0[p] = w[p]
@@ -398,7 +397,7 @@
     for p in range(2):
         for x in range(OWN):
             rows = pl.ds(x + 8 * p, 8, stride=16)
-            z, q = z0[p, x], source[p, 3 + x, :, :128]
+            z, q = z0[p, x], source[p, 5 + x, :, :128]
             step = (z - alpha * w0[p, x]) + beta * z
             image = (q - alpha * y0[p, x]) + beta * q
             field[rows, :] = alpha * z + alpha_next * step
@@ -455,27 +454,26 @@
     fine, pair = (2, EXT, 8, LANES), (2, 2, 8, LANES)
     r0, d0, i0, one, low, high, send = call(
         functools.partial(down_kernel, wide, narrow),
-        [fine, fine, fine, (2, 8, 8, LANES), pair, pair, (wide, 8, 128)],
+        [fine, fine, fine, (2, 10, 8, LANES), pair, pair, (wide, 8, 128)],
         a, b, from_left, from_right,
     )
     below, above = to_next(high, "wide"), to_previous(low, "wide")
     first = exchange(send, "wide").reshape(8 * wide, 128)
-    block, coarse, line = (2, OWN, 8, 128), (8, 8, LANES), (1, 8, LANES)
+    block, coarse = (2, OWN, 8, 128), (8, 8, LANES)
     scratch = [pltpu.VMEM((8, wide + 16, 128), F32)]
-    z0, source, r1, d1, i1, low, high, send = call(
+    z0, source, r1, d1, i1, send = call(
         functools.partial(turn_kernel, wide, narrow),
-        [block, (2, 14, 8, LANES), (6, 8, LANES), coarse, coarse, line, line, (8, 128)],
+        [block, (2, 18, 8, LANES), coarse, coarse, coarse, (8, 128)],
         first, r0, d0, i0, one, below, above,
         scratch=scratch + [pltpu.VMEM((8, 128), F32)],
     )
-    below, above = to_next(high, "wide"), to_previous(low, "wide")
     from_left, from_right = around(send, "narrow", 1), around(send, "narrow", -1)
     (send,) = call(window_kernel, [(wide, 4, 128)], send, from_right, from_left)
     second = exchange(send, "wide").reshape(4 * wide, 128)
     w0, y0, sums = call(
         functools.partial(up_again_kernel, wide, narrow),
         [block, block, (DEEP, 1, 128)],
-        second, first, source, r0, d0, i0, below, r1, above, d1, i1, z0,
+        second, first, source, r0, d0, i0, r1, d1, i1, z0,
         scratch=scratch,
     )
     across = wide // DEEP

time: 122 us -> 121 us (level)
  blocking collectives: 30.6 us -> 50.7 us
  starting transfers between devices: 49.2 us -> 38.6 us
  waiting for transfers between devices: 32.2 us -> 21.9 us
    all_to_all x2 -> x3, blocking collectives: 30.6 us -> 50.7 us  [exchange(): return lax.all_to_all(slots, axis, 0, 0, axis_index_groups=groups)]
    all_to_all x2 -> x1, waiting for transfers between devices: 14.2 us -> 6.63 us  [exchange(): return lax.all_to_all(slots, axis, 0, 0, axis_index_groups=groups)]
    all_to_all x2 -> x1, starting transfers between devices: 23.7 us -> 17.3 us  [exchange(): return lax.all_to_all(slots, axis, 0, 0, axis_index_groups=groups)]
    ppermute x3 -> x2, waiting for transfers between devices: 11.1 us -> 8.04 us  [to_previous(): return lax.ppermute(array, axis, [(i + 1, i) for i in range(n - 1)])]
    ppermute x3 -> x2, starting transfers between devices: 10.2 us -> 7.29 us  [to_next(): return lax.ppermute(array, axis, [(i, i + 1) for i in range(n - 1)])]
    ppermute x3 -> x2, starting transfers between devices: 3.88 us -> 2.58 us  [to_previous(): return lax.ppermute(array, axis, [(i + 1, i) for i in range(n - 1)])]
  transfers between devices with their start and end apart: 12 -> 9, of which waited for: 10 -> 8; matrix products, arithmetic and copies ran while one was open for 1% -> 1% of each run, Pallas kernels for 0% -> 0%
where the time goes in v8:
time: 121 us
  blocking collectives  50.7 us (42%)
  starting transfers between devices  38.6 us (32%)
  waiting for transfers between devices  21.9 us (18%)
  Pallas kernels  7.78 us (6%)
    all_to_all x3, blocking collectives, exchange(): return lax.all_to_all(slots, axis, 0, 0, axis_index_groups=groups)  50.7 us
    all_to_all x1, starting transfers between devices, exchange(): return lax.all_to_all(slots, axis, 0, 0, axis_index_groups=groups)  17.3 us
    ppermute x4, starting transfers between devices, around(): return lax.ppermute(array, axis, [(i, (i + step) % n) for i in range(n)])  11.4 us
    ppermute x2, waiting for transfers between devices, to_previous(): return lax.ppermute(array, axis, [(i + 1, i) for i in range(n - 1)])  8.04 us
    pallas_call x6, Pallas kernels, call(): pl.pallas_call(kernel, out_shape=tuple((jax.ShapeDtypeStruct(s, F32) for...  7.78 us
    ppermute x2, starting transfers between devices, to_next(): return lax.ppermute(array, axis, [(i, i + 1) for i in range(n - 1)])  7.29 us
    all_to_all x1, waiting for transfers between devices, exchange(): return lax.all_to_all(slots, axis, 0, 0, axis_index_groups=groups)  6.63 us
    ppermute x4, waiting for transfers between devices, around(): return lax.ppermute(array, axis, [(i, (i + step) % n) for i in range(n)])  5.46 us
  transfers between devices with their start and end apart: 9, of which 8 were waited for; matrix products, arithmetic and copies ran while one was open for 1% of the time, Pallas kernels for 0%

profile of v8, /device:TPU:1, one launch (start us, length us, event | category | flops | bytes accessed | tf_op | source)
XLA Modules:
  0.0 120.7 jit_solution(6597886827818099049)
XLA Ops:
  0.6 1.9 %shard_map.59 = (f32[2,2,8,8,128]{4,3,2,1,0:T(8,128)}, f32[2,2,7,8,128]{4,3,2,1,0:T(8,128)}, f32[2,2,7,8,128]{4,3,2,1,0:T(8,128)}) custom-call(f32[128,128]{1,0:T(8,128)} %bitcast.29, f32[128,128]{1,0:T(8,128)} %bitcast.30, s32[128,128]{1,0:T(8,128)} %bitcast.31, s32[128,128]{1,0:T(8,128)} %bitcast.32), custom_call_target="tpu_custom_call" | custom-call | tf_op jit(solution)/shard_map/pallas_call | solution.py:408
  2.5 4.4 %collective-permute-start = (f32[2,2,7,8,128]{4,3,2,1,0:T(8,128)}, f32[2,2,7,8,128]{4,3,2,1,0:T(8,128)S(1)}, u32[]{:S(2)}, u32[]{:S(2)}) collective-permute-start(f32[2,2,7,8,128]{4,3,2,1,0:T(8,128)} %get-tuple-element.23), channel_id=1, source_target_pairs={{0,8},{8,16},{16,24},{24,32},{32,40},{40,48},{48,56},{56,64},{64,7... | collective-permute-start | bytes 344072 | tf_op jit(solution)/shard_map/ppermute | solution.py:424
  6.9 1.3 %collective-permute-start.1 = (f32[2,2,7,8,128]{4,3,2,1,0:T(8,128)}, f32[2,2,7,8,128]{4,3,2,1,0:T(8,128)S(1)}, u32[]{:S(2)}, u32[]{:S(2)}) collective-permute-start(f32[2,2,7,8,128]{4,3,2,1,0:T(8,128)} %get-tuple-element.25), channel_id=1, source_target_pairs={{8,0},{16,8},{24,16},{32,24},{40,32},{48,40},{56,48},{64,56},{72,6... | collective-permute-start | bytes 344072 | tf_op jit(solution)/shard_map/ppermute | solution.py:429
  8.2 0.9 slice_bitcast_fusion
  9.1 3.7 %collective-permute-done.1 = f32[2,2,7,8,128]{4,3,2,1,0:T(8,128)S(1)} collective-permute-done((f32[2,2,7,8,128]{4,3,2,1,0:T(8,128)}, f32[2,2,7,8,128]{4,3,2,1,0:T(8,128)S(1)}, u32[]{:S(2)}, u32[]{:S(2)}) %collective-permute-start.1) | collective-permute-done | bytes 114720 | tf_op jit(solution)/shard_map/ppermute | solution.py:429
  12.8 4.8 %collective-permute-start.3 = (f32[2,22,8,128]{3,2,1,0:T(8,128)S(1)}, f32[2,22,8,128]{3,2,1,0:T(8,128)S(1)}, u32[]{:S(2)}, u32[]{:S(2)}) collective-permute-start(f32[2,22,8,128]{3,2,1,0:T(8,128)S(1)} %pad_maximum_fusion.a), channel_id=1, source_target_pairs={{0,7},{1,0},{2,1},{3,2},{4,3},{5,4},{6,5},{7,6},{8,15},{9,8},{10,9... | collective-permute-start | bytes 540680 | tf_op jit(solution)/shard_map/ppermute | solution.py:434
  17.7 1.4 %collective-permute-done.3.from_right = f32[2,22,8,128]{3,2,1,0:T(8,128)S(1)} collective-permute-done((f32[2,22,8,128]{3,2,1,0:T(8,128)S(1)}, f32[2,22,8,128]{3,2,1,0:T(8,128)S(1)}, u32[]{:S(2)}, u32[]{:S(2)}) %collective-permute-start.3) | collective-permute-done | bytes 180256 | tf_op jit(solution)/shard_map/ppermute | solution.py:434
  19.1 1.0 collective-permute-done.2.from_left
  20.1 1.4 %shard_map.60 = (f32[2,22,8,256]{3,2,1,0:T(8,128)S(1)}, f32[2,22,8,256]{3,2,1,0:T(8,128)S(1)}, f32[2,22,8,256]{3,2,1,0:T(8,128)S(1)}, f32[2,10,8,256]{3,2,1,0:T(...) custom-call(f32[2,22,8,128]{3,2,1,0:T(8,128)S(1)} %pad_maximum_fusion.a, ...), custom_call_target="tpu_custom_call" | custom-call | tf_op jit(solution)/shard_map/pallas_call | solution.py:408
  21.5 17.3 %all-to-all-start = ((f32[64,8,128]{2,1,0:T(8,128)}), f32[64,8,128]{2,1,0:T(8,128)S(1)}, u32[]{:S(2)}, u32[]{:S(2)}) async-start(f32[64,8,128]{2,1,0:T(8,128)} %get-tuple-element.26), calls=%async_computation | async-start | bytes 524288 | tf_op jit(solution)/shard_map/all_to_all | solution.py:419
  38.8 2.9 %collective-permute-start.4 = (f32[2,2,8,256]{3,2,1,0:T(8,128)S(1)}, f32[2,2,8,256]{3,2,1,0:T(8,128)S(1)}, u32[]{:S(2)}, u32[]{:S(2)}) collective-permute-start(f32[2,2,8,256]{3,2,1,0:T(8,128)S(1)} %get-tuple-element.31), channel_id=1, source_target_pairs={{0,8},{8,16},{16,24},{24,32},{32,40},{40,48},{48,56},{56,64},{64,7... | collective-permute-start | bytes 98312 | tf_op jit(solution)/shard_map/ppermute | solution.py:424
  41.7 1.3 %collective-permute-start.5 = (f32[2,2,8,256]{3,2,1,0:T(8,128)S(1)}, f32[2,2,8,256]{3,2,1,0:T(8,128)S(1)}, u32[]{:S(2)}, u32[]{:S(2)}) collective-permute-start(f32[2,2,8,256]{3,2,1,0:T(8,128)S(1)} %get-tuple-element.32), channel_id=1, source_target_pairs={{8,0},{16,8},{24,16},{32,24},{40,32},{48,40},{56,48},{64,56},{72,6... | collective-permute-start | bytes 98312 | tf_op jit(solution)/shard_map/ppermute | solution.py:429
  43.0 1.8 %collective-permute-done.4.below = f32[2,2,8,256]{3,2,1,0:T(8,128)S(1)} collective-permute-done((f32[2,2,8,256]{3,2,1,0:T(8,128)S(1)}, f32[2,2,8,256]{3,2,1,0:T(8,128)S(1)}, u32[]{:S(2)}, u32[]{:S(2)}) %collective-permute-start.4) | collective-permute-done | bytes 32800 | tf_op jit(solution)/shard_map/ppermute | solution.py:424
  44.8 4.3 %collective-permute-done.5.above = f32[2,2,8,256]{3,2,1,0:T(8,128)S(1)} collective-permute-done((f32[2,2,8,256]{3,2,1,0:T(8,128)S(1)}, f32[2,2,8,256]{3,2,1,0:T(8,128)S(1)}, u32[]{:S(2)}, u32[]{:S(2)}) %collective-permute-start.5) | collective-permute-done | bytes 32800 | tf_op jit(solution)/shard_map/ppermute | solution.py:429
  49.1 6.6 %all-to-all-done = f32[64,8,128]{2,1,0:T(8,128)S(1)} async-done(((f32[64,8,128]{2,1,0:T(8,128)}), f32[64,8,128]{2,1,0:T(8,128)S(1)}, u32[]{:S(2)}, u32[]{:S(2)}) %all-to-all-start) | async-done | bytes 262176 | tf_op jit(solution)/shard_map/all_to_all | solution.py:419
  55.8 2.1 %shard_map.61 = (f32[2,8,8,128]{3,2,1,0:T(8,128)S(1)}, f32[2,18,8,256]{3,2,1,0:T(8,128)S(1)}, f32[8,8,256]{2,1,0:T(8,128)S(1)}, f32[8,8,256]{2,1,0:T(8,128)S(1)}...) custom-call(f32[512,128]{1,0:T(8,128)S(1)} %bitcast.25, f32[2,22,8,256]{3,2,1,0:T(8,128)S(1)} %get-tuple-element.27.r0, ...), custom_call_target="tpu_custom_call" | custom-call | tf_op jit(solution)/shard_map/pallas_call | solution.py:408
  57.8 6.6 %collective-permute-start.7 = (f32[8,128]{1,0:T(8,128)S(1)}, f32[8,128]{1,0:T(8,128)S(1)}, u32[]{:S(2)}, u32[]{:S(2)}) collective-permute-start(f32[8,128]{1,0:T(8,128)S(1)} %get-tuple-element.33.own), channel_id=1, source_target_pairs={{0,1},{1,2},{2,3},{3,4},{4,5},{5,6},{6,7},{7,0},{8,9},{9,10},{10,1... | collective-permute-start | bytes 12296 | tf_op jit(solution)/shard_map/ppermute | solution.py:434
  64.5 0.8 collective-permute-done.7.left
  65.2 2.3 %collective-permute-done.6.right = f32[8,128]{1,0:T(8,128)S(1)} collective-permute-done((f32[8,128]{1,0:T(8,128)S(1)}, f32[8,128]{1,0:T(8,128)S(1)}, u32[]{:S(2)}, u32[]{:S(2)}) %collective-permute-start.6) | collective-permute-done | bytes 4128 | tf_op jit(solution)/shard_map/ppermute | solution.py:434
  67.6 21.4 %all_to_all.20 = f32[64,4,128]{2,1,0:T(4,128)S(1)} all-to-all(f32[64,4,128]{2,1,0:T(4,128)S(1)} %shard_map.62), channel_id=1, replica_groups=mesh['wide'=64,'narrow'=8] {'wide'}, dimensions={0} | all-to-all | bytes 262144 | tf_op jit(solution)/shard_map/all_to_all | solution.py:419
  89.0 1.5 %shard_map.63 = (f32[2,8,8,128]{3,2,1,0:T(8,128)S(1)}, f32[2,8,8,128]{3,2,1,0:T(8,128)S(1)}, f32[16,1,128]{2,1,0:T(1,128)S(1)}) custom-call(f32[256,128]{1,0:T(8,128)S(1)} %bitcast.27, f32[512,128]{1,0:T(8,128)S(1)} %bitcast.26, f32[2,18,8,256]{3,2,1,0:T(8,128)S(1)} %get-tuple-element.34.source, f32[2,22,8,256]{3,2,1,0:T(8,128)S(1)} %get-tuple-element.27.r0, ...), custom_call_target="tpu_custom_call" | custom-call | tf_op jit(solution)/shard_map/pallas_call | solution.py:408
  90.5 15.7 %all_to_all.21 = f32[16,1,128]{2,1,0:T(1,128)S(1)} all-to-all(f32[16,1,128]{2,1,0:T(1,128)S(1)} %get-tuple-element.39), channel_id=1, replica_groups={{0,8,16,24,32,40,48,56,64,72,80,88,96,104,112,120},{128,136,144,152,160..., dimensions={0} | all-to-all | bytes 16384 | tf_op jit(solution)/shard_map/all_to_all | solution.py:419
  106.3 13.6 %all_to_all.22 = f32[32,1,128]{2,1,0:T(1,128)S(1)} all-to-all(f32[32,1,128]{2,1,0:T(1,128)S(1)} %broadcast_in_dim.11), channel_id=1, replica_groups={{0,1,2,3,4,5,6,7,128,129,130,131,132,133,134,135,256,257,258,259,260,26..., dimensions={0} | all-to-all | bytes 32768 | tf_op jit(solution)/shard_map/all_to_all | solution.py:419
  119.9 0.8 shard_map.64
  (11 shorter events, 0.2 us)
Async XLA Ops:
  2.5 6.6 %collective-permute-start = (f32[2,2,7,8,128]{4,3,2,1,0:T(8,128)}, f32[2,2,7,8,128]{4,3,2,1,0:T(8,128)S(1)}, u32[]{:S(2)}, u32[]{:S(2)}) collective-permute-start(f32[2,2,7,8,128]{4,3,2,1,0:T(8,128)} %get-tuple-element.23), channel_id=1, source_target_pairs={{0,8},{8,16},{16,24},{24,32},{32,40},{40,48},{48,56},{56,64},{64,7... | collective-permute-start | bytes 344072 | tf_op jit(solution)/shard_map/ppermute | solution.py:424
  6.9 5.9 %collective-permute-start.1 = (f32[2,2,7,8,128]{4,3,2,1,0:T(8,128)}, f32[2,2,7,8,128]{4,3,2,1,0:T(8,128)S(1)}, u32[]{:S(2)}, u32[]{:S(2)}) collective-permute-start(f32[2,2,7,8,128]{4,3,2,1,0:T(8,128)} %get-tuple-element.25), channel_id=1, source_target_pairs={{8,0},{16,8},{24,16},{32,24},{40,32},{48,40},{56,48},{64,56},{72,6... | collective-permute-start | bytes 344072 | tf_op jit(solution)/shard_map/ppermute | solution.py:429
  12.8 6.2 %collective-permute-start.3 = (f32[2,22,8,128]{3,2,1,0:T(8,128)S(1)}, f32[2,22,8,128]{3,2,1,0:T(8,128)S(1)}, u32[]{:S(2)}, u32[]{:S(2)}) collective-permute-start(f32[2,22,8,128]{3,2,1,0:T(8,128)S(1)} %pad_maximum_fusion.a), channel_id=1, source_target_pairs={{0,7},{1,0},{2,1},{3,2},{4,3},{5,4},{6,5},{7,6},{8,15},{9,8},{10,9... | collective-permute-start | bytes 540680 | tf_op jit(solution)/shard_map/ppermute | solution.py:434
  17.6 2.5 %collective-permute-start.2 = (f32[2,22,8,128]{3,2,1,0:T(8,128)S(1)}, f32[2,22,8,128]{3,2,1,0:T(8,128)S(1)}, u32[]{:S(2)}, u32[]{:S(2)}) collective-permute-start(f32[2,22,8,128]{3,2,1,0:T(8,128)S(1)} %pad_maximum_fusion.1.b), channel_id=1, source_target_pairs={{0,1},{1,2},{2,3},{3,4},{4,5},{5,6},{6,7},{7,0},{8,9},{9,10},{10,1... | collective-permute-start | bytes 540680 | tf_op jit(solution)/shard_map/ppermute | solution.py:434
  21.5 34.2 %all-to-all-start = ((f32[64,8,128]{2,1,0:T(8,128)}), f32[64,8,128]{2,1,0:T(8,128)S(1)}, u32[]{:S(2)}, u32[]{:S(2)}) async-start(f32[64,8,128]{2,1,0:T(8,128)} %get-tuple-element.26), calls=%async_computation | async-start | bytes 524288 | tf_op jit(solution)/shard_map/all_to_all | solution.py:419
  38.8 6.0 %collective-permute-start.4 = (f32[2,2,8,256]{3,2,1,0:T(8,128)S(1)}, f32[2,2,8,256]{3,2,1,0:T(8,128)S(1)}, u32[]{:S(2)}, u32[]{:S(2)}) collective-permute-start(f32[2,2,8,256]{3,2,1,0:T(8,128)S(1)} %get-tuple-element.31), channel_id=1, source_target_pairs={{0,8},{8,16},{16,24},{24,32},{32,40},{40,48},{48,56},{56,64},{64,7... | collective-permute-start | bytes 98312 | tf_op jit(solution)/shard_map/ppermute | solution.py:424
  41.7 7.4 %collective-permute-start.5 = (f32[2,2,8,256]{3,2,1,0:T(8,128)S(1)}, f32[2,2,8,256]{3,2,1,0:T(8,128)S(1)}, u32[]{:S(2)}, u32[]{:S(2)}) collective-permute-start(f32[2,2,8,256]{3,2,1,0:T(8,128)S(1)} %get-tuple-element.32), channel_id=1, source_target_pairs={{8,0},{16,8},{24,16},{32,24},{40,32},{48,40},{56,48},{64,56},{72,6... | collective-permute-start | bytes 98312 | tf_op jit(solution)/shard_map/ppermute | solution.py:429
  57.8 7.4 %collective-permute-start.7 = (f32[8,128]{1,0:T(8,128)S(1)}, f32[8,128]{1,0:T(8,128)S(1)}, u32[]{:S(2)}, u32[]{:S(2)}) collective-permute-start(f32[8,128]{1,0:T(8,128)S(1)} %get-tuple-element.33.own), channel_id=1, source_target_pairs={{0,1},{1,2},{2,3},{3,4},{4,5},{5,6},{6,7},{7,0},{8,9},{9,10},{10,1... | collective-permute-start | bytes 12296 | tf_op jit(solution)/shard_map/ppermute | solution.py:434
  64.5 3.0 %collective-permute-start.6 = (f32[8,128]{1,0:T(8,128)S(1)}, f32[8,128]{1,0:T(8,128)S(1)}, u32[]{:S(2)}, u32[]{:S(2)}) collective-permute-start(f32[8,128]{1,0:T(8,128)S(1)} %get-tuple-element.33.own), channel_id=1, source_target_pairs={{0,7},{1,0},{2,1},{3,2},{4,3},{5,4},{6,5},{7,6},{8,15},{9,8},{10,9... | collective-permute-start | bytes 12296 | tf_op jit(solution)/shard_map/ppermute | solution.py:434

commit v9 on v8

--- a/solution.py
+++ b/solution.py
@@ -224,20 +224,12 @@
     return out
 
 
-def prepare_kernel(right_in, capacity_in, phase_in, flags_in, own, low, high, right, capacity, phase, flags, done):
-    pairs = ((right_in, right), (capacity_in, capacity), (phase_in, phase), (flags_in, flags))
-    copies = [pltpu.make_async_copy(a, b, done.at[i]) for i, (a, b) in enumerate(pairs)]
-    for copy in copies:
-        copy.start()
-    for copy in copies:
-        copy.wait()
+def prepare_kernel(right, diagonal, own, low, high):
     half = iota((8, 128), 1) < 64
     for p in range(2):
         for x in range(OWN):
             rows = pl.ds(x + 8 * p, 8, stride=16)
-            r = right[rows, :]
-            weight = jnp.where(phase[rows, :] == 1, 4.0, 1.0)
-            d = 0.05 * capacity[rows, :] * weight + 0.5 * flags[rows, :].astype(F32)
+            r, d = right[rows, :], diagonal[rows, :]
             first = jnp.where(half, r, roll(d, 64, 1))
             second = jnp.where(half, roll(r, 64, 1), d)
             for side, value in ((0, first), (1, second)):
@@ -404,14 +396,14 @@
             residual[rows, :] = (r0[p, HALO + x, :, :128] - alpha * q) - alpha_next * image
 
 
-def call(kernel, outs, *args, scratch=(), space=pltpu.VMEM, limit=40):
+def call(kernel, outs, *args, scratch=()):
     return pl.pallas_call(
         kernel,
         out_shape=tuple(jax.ShapeDtypeStruct(s, F32) for s in outs),
-        in_specs=[pl.BlockSpec(memory_space=space)] * len(args),
+        in_specs=[pl.BlockSpec(memory_space=pltpu.VMEM)] * len(args),
         out_specs=tuple(pl.BlockSpec(memory_space=pltpu.VMEM) for _ in outs),
         scratch_shapes=scratch,
-        compiler_params=pltpu.CompilerParams(vmem_limit_bytes=limit * 1024 * 1024),
+        compiler_params=pltpu.CompilerParams(vmem_limit_bytes=40 * 1024 * 1024),
     )(*args)
 
 
@@ -436,16 +428,13 @@
 
 def on_device(right_side, capacity, phase, mold_flags):
     wide, narrow = lax.axis_size("wide"), lax.axis_size("narrow")
-    flat = [v.reshape(128, 128) for v in (right_side, capacity, phase, mold_flags)]
     edge = (2, 2, HALO, 8, 128)
-    staged = [pltpu.VMEM((128, 128), v.dtype) for v in flat]
+    weight = jnp.where(phase == 1, jnp.float32(4.0), jnp.float32(1.0))
+    diagonal = 0.05 * capacity * weight + 0.5 * mold_flags.astype(F32)
     own, low, high = call(
         prepare_kernel,
         [(2, 2, OWN, 8, 128), edge, edge],
-        *flat,
-        scratch=staged + [pltpu.SemaphoreType.DMA((4,))],
-        space=pl.ANY,
-        limit=63,
+        right_side.reshape(128, 128), diagonal.reshape(128, 128),
     )
     below, above = to_next(high, "wide"), to_previous(low, "wide")
     a = jnp.concatenate([below[0], own[0], above[0]], axis=1)

time: 121 us -> 120 us (level)
  Pallas kernels: 7.78 us -> 6.02 us
    pallas_call x6, Pallas kernels: 7.78 us -> 6.02 us  [call(): pl.pallas_call(kernel, out_shape=tuple((jax.ShapeDtypeStruct(s, F32) for...]
  transfers between devices with their start and end apart: 9 -> 9, of which waited for: 8 -> 9; matrix products, arithmetic and copies ran while one was open for 1% -> 0% of each run, Pallas kernels for 0% -> 0%
where the time goes in v9:
time: 120 us
  blocking collectives  50.7 us (42%)
  starting transfers between devices  38.6 us (32%)
  waiting for transfers between devices  22.6 us (19%)
  Pallas kernels  6.02 us (5%)
    all_to_all x3, blocking collectives, exchange(): return lax.all_to_all(slots, axis, 0, 0, axis_index_groups=groups)  50.7 us
    all_to_all x1, starting transfers between devices, exchange(): return lax.all_to_all(slots, axis, 0, 0, axis_index_groups=groups)  17.3 us
    ppermute x4, starting transfers between devices, around(): return lax.ppermute(array, axis, [(i, (i + step) % n) for i in range(n)])  11.4 us
    ppermute x2, waiting for transfers between devices, to_previous(): return lax.ppermute(array, axis, [(i + 1, i) for i in range(n - 1)])  8.27 us
    ppermute x2, starting transfers between devices, to_next(): return lax.ppermute(array, axis, [(i, i + 1) for i in range(n - 1)])  7.29 us
    all_to_all x1, waiting for transfers between devices, exchange(): return lax.all_to_all(slots, axis, 0, 0, axis_index_groups=groups)  6.63 us
    pallas_call x6, Pallas kernels, call(): pl.pallas_call(kernel, out_shape=tuple((jax.ShapeDtypeStruct(s, F32) for...  6.02 us
    ppermute x4, waiting for transfers between devices, around(): return lax.ppermute(array, axis, [(i, (i + step) % n) for i in range(n)])  5.46 us
  transfers between devices with their start and end apart: 9, of which 9 were waited for; matrix products, arithmetic and copies ran while one was open for 0% of the time, Pallas kernels for 0%

profile of v9, /device:TPU:1, one launch (start us, length us, event | category | flops | bytes accessed | tf_op | source)
XLA Modules:
  0.0 119.7 jit_solution(17084518085625865840)
XLA Ops:
  0.6 1.0 add_bitcast_fusion.diagonal
  1.7 4.4 %collective-permute-start = (f32[2,2,7,8,128]{4,3,2,1,0:T(8,128)S(1)}, f32[2,2,7,8,128]{4,3,2,1,0:T(8,128)S(1)}, u32[]{:S(2)}, u32[]{:S(2)}) collective-permute-start(f32[2,2,7,8,128]{4,3,2,1,0:T(8,128)S(1)} %get-tuple-element.23), channel_id=1, source_target_pairs={{0,8},{8,16},{16,24},{24,32},{32,40},{40,48},{48,56},{56,64},{64,7... | collective-permute-start | bytes 344072 | tf_op jit(solution)/shard_map/ppermute | solution.py:416
  6.1 1.3 %collective-permute-start.1 = (f32[2,2,7,8,128]{4,3,2,1,0:T(8,128)S(1)}, f32[2,2,7,8,128]{4,3,2,1,0:T(8,128)S(1)}, u32[]{:S(2)}, u32[]{:S(2)}) collective-permute-start(f32[2,2,7,8,128]{4,3,2,1,0:T(8,128)S(1)} %get-tuple-element.25), channel_id=1, source_target_pairs={{8,0},{16,8},{24,16},{32,24},{40,32},{48,40},{56,48},{64,56},{72,6... | collective-permute-start | bytes 344072 | tf_op jit(solution)/shard_map/ppermute | solution.py:421
  7.4 0.5 collective-permute-done
  7.9 3.9 %collective-permute-done.1 = f32[2,2,7,8,128]{4,3,2,1,0:T(8,128)S(1)} collective-permute-done((f32[2,2,7,8,128]{4,3,2,1,0:T(8,128)S(1)}, f32[2,2,7,8,128]{4,3,2,1,0:T(8,128)S(1)}, u32[]{:S(2)}, u32[]{:S(2)}) %collective-permute-start.1) | collective-permute-done | bytes 114720 | tf_op jit(solution)/shard_map/ppermute | solution.py:421
  11.9 4.8 %collective-permute-start.3 = (f32[2,22,8,128]{3,2,1,0:T(8,128)S(1)}, f32[2,22,8,128]{3,2,1,0:T(8,128)S(1)}, u32[]{:S(2)}, u32[]{:S(2)}) collective-permute-start(f32[2,22,8,128]{3,2,1,0:T(8,128)S(1)} %pad_maximum_fusion.a), channel_id=1, source_target_pairs={{0,7},{1,0},{2,1},{3,2},{4,3},{5,4},{6,5},{7,6},{8,15},{9,8},{10,9... | collective-permute-start | bytes 540680 | tf_op jit(solution)/shard_map/ppermute | solution.py:426
  16.7 1.4 %collective-permute-done.3.from_right = f32[2,22,8,128]{3,2,1,0:T(8,128)S(1)} collective-permute-done((f32[2,22,8,128]{3,2,1,0:T(8,128)S(1)}, f32[2,22,8,128]{3,2,1,0:T(8,128)S(1)}, u32[]{:S(2)}, u32[]{:S(2)}) %collective-permute-start.3) | collective-permute-done | bytes 180256 | tf_op jit(solution)/shard_map/ppermute | solution.py:426
  18.1 1.0 collective-permute-done.2.from_left
  19.1 1.4 %shard_map.60 = (f32[2,22,8,256]{3,2,1,0:T(8,128)S(1)}, f32[2,22,8,256]{3,2,1,0:T(8,128)S(1)}, f32[2,22,8,256]{3,2,1,0:T(8,128)S(1)}, f32[2,10,8,256]{3,2,1,0:T(...) custom-call(f32[2,22,8,128]{3,2,1,0:T(8,128)S(1)} %pad_maximum_fusion.a, ...), custom_call_target="tpu_custom_call" | custom-call | tf_op jit(solution)/shard_map/pallas_call | solution.py:400
  20.5 17.3 %all-to-all-start = ((f32[64,8,128]{2,1,0:T(8,128)}), f32[64,8,128]{2,1,0:T(8,128)S(1)}, u32[]{:S(2)}, u32[]{:S(2)}) async-start(f32[64,8,128]{2,1,0:T(8,128)} %get-tuple-element.26), calls=%async_computation | async-start | bytes 524288 | tf_op jit(solution)/shard_map/all_to_all | solution.py:411
  37.8 2.9 %collective-permute-start.4 = (f32[2,2,8,256]{3,2,1,0:T(8,128)S(1)}, f32[2,2,8,256]{3,2,1,0:T(8,128)S(1)}, u32[]{:S(2)}, u32[]{:S(2)}) collective-permute-start(f32[2,2,8,256]{3,2,1,0:T(8,128)S(1)} %get-tuple-element.31), channel_id=1, source_target_pairs={{0,8},{8,16},{16,24},{24,32},{32,40},{40,48},{48,56},{56,64},{64,7... | collective-permute-start | bytes 98312 | tf_op jit(solution)/shard_map/ppermute | solution.py:416
  40.7 1.3 %collective-permute-start.5 = (f32[2,2,8,256]{3,2,1,0:T(8,128)S(1)}, f32[2,2,8,256]{3,2,1,0:T(8,128)S(1)}, u32[]{:S(2)}, u32[]{:S(2)}) collective-permute-start(f32[2,2,8,256]{3,2,1,0:T(8,128)S(1)} %get-tuple-element.32), channel_id=1, source_target_pairs={{8,0},{16,8},{24,16},{32,24},{40,32},{48,40},{56,48},{64,56},{72,6... | collective-permute-start | bytes 98312 | tf_op jit(solution)/shard_map/ppermute | solution.py:421
  42.0 1.8 %collective-permute-done.4.below = f32[2,2,8,256]{3,2,1,0:T(8,128)S(1)} collective-permute-done((f32[2,2,8,256]{3,2,1,0:T(8,128)S(1)}, f32[2,2,8,256]{3,2,1,0:T(8,128)S(1)}, u32[]{:S(2)}, u32[]{:S(2)}) %collective-permute-start.4) | collective-permute-done | bytes 32800 | tf_op jit(solution)/shard_map/ppermute | solution.py:416
  43.8 4.3 %collective-permute-done.5.above = f32[2,2,8,256]{3,2,1,0:T(8,128)S(1)} collective-permute-done((f32[2,2,8,256]{3,2,1,0:T(8,128)S(1)}, f32[2,2,8,256]{3,2,1,0:T(8,128)S(1)}, u32[]{:S(2)}, u32[]{:S(2)}) %collective-permute-start.5) | collective-permute-done | bytes 32800 | tf_op jit(solution)/shard_map/ppermute | solution.py:421
  48.1 6.6 %all-to-all-done = f32[64,8,128]{2,1,0:T(8,128)S(1)} async-done(((f32[64,8,128]{2,1,0:T(8,128)}), f32[64,8,128]{2,1,0:T(8,128)S(1)}, u32[]{:S(2)}, u32[]{:S(2)}) %all-to-all-start) | async-done | bytes 262176 | tf_op jit(solution)/shard_map/all_to_all | solution.py:411
  54.8 2.1 %shard_map.61 = (f32[2,8,8,128]{3,2,1,0:T(8,128)S(1)}, f32[2,18,8,256]{3,2,1,0:T(8,128)S(1)}, f32[8,8,256]{2,1,0:T(8,128)S(1)}, f32[8,8,256]{2,1,0:T(8,128)S(1)}...) custom-call(f32[512,128]{1,0:T(8,128)S(1)} %bitcast.24, f32[2,22,8,256]{3,2,1,0:T(8,128)S(1)} %get-tuple-element.27.r0, ...), custom_call_target="tpu_custom_call" | custom-call | tf_op jit(solution)/shard_map/pallas_call | solution.py:400
  56.9 6.6 %collective-permute-start.7 = (f32[8,128]{1,0:T(8,128)S(1)}, f32[8,128]{1,0:T(8,128)S(1)}, u32[]{:S(2)}, u32[]{:S(2)}) collective-permute-start(f32[8,128]{1,0:T(8,128)S(1)} %get-tuple-element.33.own), channel_id=1, source_target_pairs={{0,1},{1,2},{2,3},{3,4},{4,5},{5,6},{6,7},{7,0},{8,9},{9,10},{10,1... | collective-permute-start | bytes 12296 | tf_op jit(solution)/shard_map/ppermute | solution.py:426
  63.5 0.8 collective-permute-done.7.left
  64.2 2.3 %collective-permute-done.6.right = f32[8,128]{1,0:T(8,128)S(1)} collective-permute-done((f32[8,128]{1,0:T(8,128)S(1)}, f32[8,128]{1,0:T(8,128)S(1)}, u32[]{:S(2)}, u32[]{:S(2)}) %collective-permute-start.6) | collective-permute-done | bytes 4128 | tf_op jit(solution)/shard_map/ppermute | solution.py:426
  66.6 21.4 %all_to_all.20 = f32[64,4,128]{2,1,0:T(4,128)S(1)} all-to-all(f32[64,4,128]{2,1,0:T(4,128)S(1)} %shard_map.62), channel_id=1, replica_groups=mesh['wide'=64,'narrow'=8] {'wide'}, dimensions={0} | all-to-all | bytes 262144 | tf_op jit(solution)/shard_map/all_to_all | solution.py:411
  88.0 1.5 %shard_map.63 = (f32[2,8,8,128]{3,2,1,0:T(8,128)S(1)}, f32[2,8,8,128]{3,2,1,0:T(8,128)S(1)}, f32[16,1,128]{2,1,0:T(1,128)S(1)}) custom-call(f32[256,128]{1,0:T(8,128)S(1)} %bitcast.26, f32[512,128]{1,0:T(8,128)S(1)} %bitcast.25, f32[2,18,8,256]{3,2,1,0:T(8,128)S(1)} %get-tuple-element.34.source, f32[2,22,8,256]{3,2,1,0:T(8,128)S(1)} %get-tuple-element.27.r0, ...), custom_call_target="tpu_custom_call" | custom-call | tf_op jit(solution)/shard_map/pallas_call | solution.py:400
  89.5 15.7 %all_to_all.21 = f32[16,1,128]{2,1,0:T(1,128)S(1)} all-to-all(f32[16,1,128]{2,1,0:T(1,128)S(1)} %get-tuple-element.39), channel_id=1, replica_groups={{0,8,16,24,32,40,48,56,64,72,80,88,96,104,112,120},{128,136,144,152,160..., dimensions={0} | all-to-all | bytes 16384 | tf_op jit(solution)/shard_map/all_to_all | solution.py:411
  105.3 13.6 %all_to_all.22 = f32[32,1,128]{2,1,0:T(1,128)S(1)} all-to-all(f32[32,1,128]{2,1,0:T(1,128)S(1)} %broadcast_in_dim.21), channel_id=1, replica_groups={{0,1,2,3,4,5,6,7,128,129,130,131,132,133,134,135,256,257,258,259,260,26..., dimensions={0} | all-to-all | bytes 32768 | tf_op jit(solution)/shard_map/all_to_all | solution.py:411
  118.9 0.8 shard_map.64
  (14 shorter events, 0.3 us)
Async XLA Ops:
  0.6 1.0 copy-start
  1.7 6.2 %collective-permute-start = (f32[2,2,7,8,128]{4,3,2,1,0:T(8,128)S(1)}, f32[2,2,7,8,128]{4,3,2,1,0:T(8,128)S(1)}, u32[]{:S(2)}, u32[]{:S(2)}) collective-permute-start(f32[2,2,7,8,128]{4,3,2,1,0:T(8,128)S(1)} %get-tuple-element.23), channel_id=1, source_target_pairs={{0,8},{8,16},{16,24},{24,32},{32,40},{40,48},{48,56},{56,64},{64,7... | collective-permute-start | bytes 344072 | tf_op jit(solution)/shard_map/ppermute | solution.py:416
  6.1 5.7 %collective-permute-start.1 = (f32[2,2,7,8,128]{4,3,2,1,0:T(8,128)S(1)}, f32[2,2,7,8,128]{4,3,2,1,0:T(8,128)S(1)}, u32[]{:S(2)}, u32[]{:S(2)}) collective-permute-start(f32[2,2,7,8,128]{4,3,2,1,0:T(8,128)S(1)} %get-tuple-element.25), channel_id=1, source_target_pairs={{8,0},{16,8},{24,16},{32,24},{40,32},{48,40},{56,48},{64,56},{72,6... | collective-permute-start | bytes 344072 | tf_op jit(solution)/shard_map/ppermute | solution.py:421
  11.9 6.2 %collective-permute-start.3 = (f32[2,22,8,128]{3,2,1,0:T(8,128)S(1)}, f32[2,22,8,128]{3,2,1,0:T(8,128)S(1)}, u32[]{:S(2)}, u32[]{:S(2)}) collective-permute-start(f32[2,22,8,128]{3,2,1,0:T(8,128)S(1)} %pad_maximum_fusion.a), channel_id=1, source_target_pairs={{0,7},{1,0},{2,1},{3,2},{4,3},{5,4},{6,5},{7,6},{8,15},{9,8},{10,9... | collective-permute-start | bytes 540680 | tf_op jit(solution)/shard_map/ppermute | solution.py:426
  16.6 2.5 %collective-permute-start.2 = (f32[2,22,8,128]{3,2,1,0:T(8,128)S(1)}, f32[2,22,8,128]{3,2,1,0:T(8,128)S(1)}, u32[]{:S(2)}, u32[]{:S(2)}) collective-permute-start(f32[2,22,8,128]{3,2,1,0:T(8,128)S(1)} %pad_maximum_fusion.1.b), channel_id=1, source_target_pairs={{0,1},{1,2},{2,3},{3,4},{4,5},{5,6},{6,7},{7,0},{8,9},{9,10},{10,1... | collective-permute-start | bytes 540680 | tf_op jit(solution)/shard_map/ppermute | solution.py:426
  20.5 34.2 %all-to-all-start = ((f32[64,8,128]{2,1,0:T(8,128)}), f32[64,8,128]{2,1,0:T(8,128)S(1)}, u32[]{:S(2)}, u32[]{:S(2)}) async-start(f32[64,8,128]{2,1,0:T(8,128)} %get-tuple-element.26), calls=%async_computation | async-start | bytes 524288 | tf_op jit(solution)/shard_map/all_to_all | solution.py:411
  37.8 6.0 %collective-permute-start.4 = (f32[2,2,8,256]{3,2,1,0:T(8,128)S(1)}, f32[2,2,8,256]{3,2,1,0:T(8,128)S(1)}, u32[]{:S(2)}, u32[]{:S(2)}) collective-permute-start(f32[2,2,8,256]{3,2,1,0:T(8,128)S(1)} %get-tuple-element.31), channel_id=1, source_target_pairs={{0,8},{8,16},{16,24},{24,32},{32,40},{40,48},{48,56},{56,64},{64,7... | collective-permute-start | bytes 98312 | tf_op jit(solution)/shard_map/ppermute | solution.py:416
  40.7 7.4 %collective-permute-start.5 = (f32[2,2,8,256]{3,2,1,0:T(8,128)S(1)}, f32[2,2,8,256]{3,2,1,0:T(8,128)S(1)}, u32[]{:S(2)}, u32[]{:S(2)}) collective-permute-start(f32[2,2,8,256]{3,2,1,0:T(8,128)S(1)} %get-tuple-element.32), channel_id=1, source_target_pairs={{8,0},{16,8},{24,16},{32,24},{40,32},{48,40},{56,48},{64,56},{72,6... | collective-permute-start | bytes 98312 | tf_op jit(solution)/shard_map/ppermute | solution.py:421
  56.9 7.4 %collective-permute-start.7 = (f32[8,128]{1,0:T(8,128)S(1)}, f32[8,128]{1,0:T(8,128)S(1)}, u32[]{:S(2)}, u32[]{:S(2)}) collective-permute-start(f32[8,128]{1,0:T(8,128)S(1)} %get-tuple-element.33.own), channel_id=1, source_target_pairs={{0,1},{1,2},{2,3},{3,4},{4,5},{5,6},{6,7},{7,0},{8,9},{9,10},{10,1... | collective-permute-start | bytes 12296 | tf_op jit(solution)/shard_map/ppermute | solution.py:426
  63.5 3.0 %collective-permute-start.6 = (f32[8,128]{1,0:T(8,128)S(1)}, f32[8,128]{1,0:T(8,128)S(1)}, u32[]{:S(2)}, u32[]{:S(2)}) collective-permute-start(f32[8,128]{1,0:T(8,128)S(1)} %get-tuple-element.33.own), channel_id=1, source_target_pairs={{0,7},{1,0},{2,1},{3,2},{4,3},{5,4},{6,5},{7,6},{8,15},{9,8},{10,9... | collective-permute-start | bytes 12296 | tf_op jit(solution)/shard_map/ppermute | solution.py:426

commit v10 on v9

--- a/solution.py
+++ b/solution.py
@@ -63,24 +63,30 @@
     return 0.25 * (6.0 * v - beside) + extra * v
 
 
-def pack_two(value, first_lane):
+def pair_rows(value):
     pairs = jnp.sum(value.reshape((2, 2) + value.shape[1:]), axis=1)
-    pairs = pairs + swap(pairs, 1, 1)
-    rows = jnp.where(iota(pairs.shape[1:], 0) % 2 == 0, pairs[0], pairs[1])
+    return pairs + swap(pairs, 1, 1)
+
+
+def pack(first, second):
     shape = (LANES, 128)
-    matrix = jnp.where(iota(shape, 0) // 4 + first_lane == iota(shape, 1), 0.0625, 0.0)
-    return jnp.dot(rows, matrix.astype(F32), precision=lax.Precision.HIGHEST)
+    matrix = jnp.where(iota(shape, 0) // 4 == iota(shape, 1), 0.0625, 0.0).astype(F32)
+    both = jnp.concatenate([first, second], axis=0)
+    out = jnp.dot(both, matrix, precision=lax.Precision.HIGHEST)
+    return out[:8] + roll(out[8:], 64, 1)
+
+
+def pack_two(first, second):
+    rows = []
+    for value in (first, second):
+        pairs = pair_rows(value)
+        rows.append(jnp.where(iota(pairs.shape[1:], 0) % 2 == 0, pairs[0], pairs[1]))
+    return pack(*rows)
 
 
 def pack_rows(value, scratch):
-    pairs = jnp.sum(value.reshape((2, 2) + value.shape[1:]), axis=1)
-    pairs = pairs + swap(pairs, 1, 1)
-    shape = (LANES, 128)
-    out = jnp.zeros((8, 128), F32)
-    for x in range(2):
-        matrix = jnp.where(iota(shape, 0) // 4 + 64 * x == iota(shape, 1), 0.0625, 0.0)
-        out = out + jnp.dot(pairs[x], matrix.astype(F32), precision=lax.Precision.HIGHEST)
-    scratch[...] = out
+    pairs = pair_rows(value)
+    scratch[...] = pack(pairs[0], pairs[1])
     return scratch[pl.ds(0, 4, stride=2), :]
 
 
@@ -270,7 +276,7 @@
         high[side] = value[2:4]
         low[side] = value[6:8]
     left = leave_one(vr1[2:8], vd1[2:8], vi1[2:8])
-    tile = pack_two(left, 0) + pack_two(vd1[3:7], 64)
+    tile = pack_two(left, vd1[3:7])
     send[...] = jnp.broadcast_to(tile, send.shape)
 
 

time: 120 us -> 120 us (level)
  no operation moved by 1% of the time
where the time goes in v10:
time: 120 us
  blocking collectives  50.7 us (42%)
  starting transfers between devices  38.6 us (32%)
  waiting for transfers between devices  22.6 us (19%)
  Pallas kernels  6.01 us (5%)
    all_to_all x3, blocking collectives, exchange(): return lax.all_to_all(slots, axis, 0, 0, axis_index_groups=groups)  50.7 us
    all_to_all x1, starting transfers between devices, exchange(): return lax.all_to_all(slots, axis, 0, 0, axis_index_groups=groups)  17.3 us
    ppermute x4, starting transfers between devices, around(): return lax.ppermute(array, axis, [(i, (i + step) % n) for i in range(n)])  11.4 us
    ppermute x2, waiting for transfers between devices, to_previous(): return lax.ppermute(array, axis, [(i + 1, i) for i in range(n - 1)])  8.27 us
    ppermute x2, starting transfers between devices, to_next(): return lax.ppermute(array, axis, [(i, i + 1) for i in range(n - 1)])  7.29 us
    all_to_all x1, waiting for transfers between devices, exchange(): return lax.all_to_all(slots, axis, 0, 0, axis_index_groups=groups)  6.63 us
    pallas_call x6, Pallas kernels, call(): pl.pallas_call(kernel, out_shape=tuple((jax.ShapeDtypeStruct(s, F32) for...  6.01 us
    ppermute x4, waiting for transfers between devices, around(): return lax.ppermute(array, axis, [(i, (i + step) % n) for i in range(n)])  5.46 us
  transfers between devices with their start and end apart: 9, of which 9 were waited for; matrix products, arithmetic and copies ran while one was open for 0% of the time, Pallas kernels for 0%

profile of v10, /device:TPU:1, one launch (start us, length us, event | category | flops | bytes accessed | tf_op | source)
XLA Modules:
  0.0 119.7 jit_solution(14706448810443754327)
XLA Ops:
  0.6 1.0 add_bitcast_fusion.diagonal
  1.7 4.4 %collective-permute-start = (f32[2,2,7,8,128]{4,3,2,1,0:T(8,128)S(1)}, f32[2,2,7,8,128]{4,3,2,1,0:T(8,128)S(1)}, u32[]{:S(2)}, u32[]{:S(2)}) collective-permute-start(f32[2,2,7,8,128]{4,3,2,1,0:T(8,128)S(1)} %get-tuple-element.23), channel_id=1, source_target_pairs={{0,8},{8,16},{16,24},{24,32},{32,40},{40,48},{48,56},{56,64},{64,7... | collective-permute-start | bytes 344072 | tf_op jit(solution)/shard_map/ppermute | solution.py:422
  6.1 1.3 %collective-permute-start.1 = (f32[2,2,7,8,128]{4,3,2,1,0:T(8,128)S(1)}, f32[2,2,7,8,128]{4,3,2,1,0:T(8,128)S(1)}, u32[]{:S(2)}, u32[]{:S(2)}) collective-permute-start(f32[2,2,7,8,128]{4,3,2,1,0:T(8,128)S(1)} %get-tuple-element.25), channel_id=1, source_target_pairs={{8,0},{16,8},{24,16},{32,24},{40,32},{48,40},{56,48},{64,56},{72,6... | collective-permute-start | bytes 344072 | tf_op jit(solution)/shard_map/ppermute | solution.py:427
  7.4 0.5 collective-permute-done
  7.9 3.9 %collective-permute-done.1 = f32[2,2,7,8,128]{4,3,2,1,0:T(8,128)S(1)} collective-permute-done((f32[2,2,7,8,128]{4,3,2,1,0:T(8,128)S(1)}, f32[2,2,7,8,128]{4,3,2,1,0:T(8,128)S(1)}, u32[]{:S(2)}, u32[]{:S(2)}) %collective-permute-start.1) | collective-permute-done | bytes 114720 | tf_op jit(solution)/shard_map/ppermute | solution.py:427
  11.9 4.8 %collective-permute-start.3 = (f32[2,22,8,128]{3,2,1,0:T(8,128)S(1)}, f32[2,22,8,128]{3,2,1,0:T(8,128)S(1)}, u32[]{:S(2)}, u32[]{:S(2)}) collective-permute-start(f32[2,22,8,128]{3,2,1,0:T(8,128)S(1)} %pad_maximum_fusion.a), channel_id=1, source_target_pairs={{0,7},{1,0},{2,1},{3,2},{4,3},{5,4},{6,5},{7,6},{8,15},{9,8},{10,9... | collective-permute-start | bytes 540680 | tf_op jit(solution)/shard_map/ppermute | solution.py:432
  16.7 1.4 %collective-permute-done.3.from_right = f32[2,22,8,128]{3,2,1,0:T(8,128)S(1)} collective-permute-done((f32[2,22,8,128]{3,2,1,0:T(8,128)S(1)}, f32[2,22,8,128]{3,2,1,0:T(8,128)S(1)}, u32[]{:S(2)}, u32[]{:S(2)}) %collective-permute-start.3) | collective-permute-done | bytes 180256 | tf_op jit(solution)/shard_map/ppermute | solution.py:432
  18.1 1.0 collective-permute-done.2.from_left
  19.1 1.4 %shard_map.60 = (f32[2,22,8,256]{3,2,1,0:T(8,128)S(1)}, f32[2,22,8,256]{3,2,1,0:T(8,128)S(1)}, f32[2,22,8,256]{3,2,1,0:T(8,128)S(1)}, f32[2,10,8,256]{3,2,1,0:T(...) custom-call(f32[2,22,8,128]{3,2,1,0:T(8,128)S(1)} %pad_maximum_fusion.a, ...), custom_call_target="tpu_custom_call" | custom-call | tf_op jit(solution)/shard_map/pallas_call | solution.py:406
  20.5 17.3 %all-to-all-start = ((f32[64,8,128]{2,1,0:T(8,128)}), f32[64,8,128]{2,1,0:T(8,128)S(1)}, u32[]{:S(2)}, u32[]{:S(2)}) async-start(f32[64,8,128]{2,1,0:T(8,128)} %get-tuple-element.26), calls=%async_computation | async-start | bytes 524288 | tf_op jit(solution)/shard_map/all_to_all | solution.py:417
  37.8 2.9 %collective-permute-start.4 = (f32[2,2,8,256]{3,2,1,0:T(8,128)S(1)}, f32[2,2,8,256]{3,2,1,0:T(8,128)S(1)}, u32[]{:S(2)}, u32[]{:S(2)}) collective-permute-start(f32[2,2,8,256]{3,2,1,0:T(8,128)S(1)} %get-tuple-element.31), channel_id=1, source_target_pairs={{0,8},{8,16},{16,24},{24,32},{32,40},{40,48},{48,56},{56,64},{64,7... | collective-permute-start | bytes 98312 | tf_op jit(solution)/shard_map/ppermute | solution.py:422
  40.8 1.3 %collective-permute-start.5 = (f32[2,2,8,256]{3,2,1,0:T(8,128)S(1)}, f32[2,2,8,256]{3,2,1,0:T(8,128)S(1)}, u32[]{:S(2)}, u32[]{:S(2)}) collective-permute-start(f32[2,2,8,256]{3,2,1,0:T(8,128)S(1)} %get-tuple-element.32), channel_id=1, source_target_pairs={{8,0},{16,8},{24,16},{32,24},{40,32},{48,40},{56,48},{64,56},{72,6... | collective-permute-start | bytes 98312 | tf_op jit(solution)/shard_map/ppermute | solution.py:427
  42.1 1.8 %collective-permute-done.4.below = f32[2,2,8,256]{3,2,1,0:T(8,128)S(1)} collective-permute-done((f32[2,2,8,256]{3,2,1,0:T(8,128)S(1)}, f32[2,2,8,256]{3,2,1,0:T(8,128)S(1)}, u32[]{:S(2)}, u32[]{:S(2)}) %collective-permute-start.4) | collective-permute-done | bytes 32800 | tf_op jit(solution)/shard_map/ppermute | solution.py:422
  43.8 4.3 %collective-permute-done.5.above = f32[2,2,8,256]{3,2,1,0:T(8,128)S(1)} collective-permute-done((f32[2,2,8,256]{3,2,1,0:T(8,128)S(1)}, f32[2,2,8,256]{3,2,1,0:T(8,128)S(1)}, u32[]{:S(2)}, u32[]{:S(2)}) %collective-permute-start.5) | collective-permute-done | bytes 32800 | tf_op jit(solution)/shard_map/ppermute | solution.py:427
  48.2 6.6 %all-to-all-done = f32[64,8,128]{2,1,0:T(8,128)S(1)} async-done(((f32[64,8,128]{2,1,0:T(8,128)}), f32[64,8,128]{2,1,0:T(8,128)S(1)}, u32[]{:S(2)}, u32[]{:S(2)}) %all-to-all-start) | async-done | bytes 262176 | tf_op jit(solution)/shard_map/all_to_all | solution.py:417
  54.8 2.0 %shard_map.61 = (f32[2,8,8,128]{3,2,1,0:T(8,128)S(1)}, f32[2,18,8,256]{3,2,1,0:T(8,128)S(1)}, f32[8,8,256]{2,1,0:T(8,128)S(1)}, f32[8,8,256]{2,1,0:T(8,128)S(1)}...) custom-call(f32[512,128]{1,0:T(8,128)S(1)} %bitcast.24, f32[2,22,8,256]{3,2,1,0:T(8,128)S(1)} %get-tuple-element.27.r0, ...), custom_call_target="tpu_custom_call" | custom-call | tf_op jit(solution)/shard_map/pallas_call | solution.py:406
  56.8 6.6 %collective-permute-start.7 = (f32[8,128]{1,0:T(8,128)S(1)}, f32[8,128]{1,0:T(8,128)S(1)}, u32[]{:S(2)}, u32[]{:S(2)}) collective-permute-start(f32[8,128]{1,0:T(8,128)S(1)} %get-tuple-element.33.own), channel_id=1, source_target_pairs={{0,1},{1,2},{2,3},{3,4},{4,5},{5,6},{6,7},{7,0},{8,9},{9,10},{10,1... | collective-permute-start | bytes 12296 | tf_op jit(solution)/shard_map/ppermute | solution.py:432
  63.5 0.8 collective-permute-done.7.left
  64.2 2.3 %collective-permute-done.6.right = f32[8,128]{1,0:T(8,128)S(1)} collective-permute-done((f32[8,128]{1,0:T(8,128)S(1)}, f32[8,128]{1,0:T(8,128)S(1)}, u32[]{:S(2)}, u32[]{:S(2)}) %collective-permute-start.6) | collective-permute-done | bytes 4128 | tf_op jit(solution)/shard_map/ppermute | solution.py:432
  66.6 21.4 %all_to_all.20 = f32[64,4,128]{2,1,0:T(4,128)S(1)} all-to-all(f32[64,4,128]{2,1,0:T(4,128)S(1)} %shard_map.62), channel_id=1, replica_groups=mesh['wide'=64,'narrow'=8] {'wide'}, dimensions={0} | all-to-all | bytes 262144 | tf_op jit(solution)/shard_map/all_to_all | solution.py:417
  88.0 1.5 %shard_map.63 = (f32[2,8,8,128]{3,2,1,0:T(8,128)S(1)}, f32[2,8,8,128]{3,2,1,0:T(8,128)S(1)}, f32[16,1,128]{2,1,0:T(1,128)S(1)}) custom-call(f32[256,128]{1,0:T(8,128)S(1)} %bitcast.26, f32[512,128]{1,0:T(8,128)S(1)} %bitcast.25, f32[2,18,8,256]{3,2,1,0:T(8,128)S(1)} %get-tuple-element.34.source, f32[2,22,8,256]{3,2,1,0:T(8,128)S(1)} %get-tuple-element.27.r0, ...), custom_call_target="tpu_custom_call" | custom-call | tf_op jit(solution)/shard_map/pallas_call | solution.py:406
  89.5 15.7 %all_to_all.21 = f32[16,1,128]{2,1,0:T(1,128)S(1)} all-to-all(f32[16,1,128]{2,1,0:T(1,128)S(1)} %get-tuple-element.39), channel_id=1, replica_groups={{0,8,16,24,32,40,48,56,64,72,80,88,96,104,112,120},{128,136,144,152,160..., dimensions={0} | all-to-all | bytes 16384 | tf_op jit(solution)/shard_map/all_to_all | solution.py:417
  105.3 13.6 %all_to_all.22 = f32[32,1,128]{2,1,0:T(1,128)S(1)} all-to-all(f32[32,1,128]{2,1,0:T(1,128)S(1)} %broadcast_in_dim.21), channel_id=1, replica_groups={{0,1,2,3,4,5,6,7,128,129,130,131,132,133,134,135,256,257,258,259,260,26..., dimensions={0} | all-to-all | bytes 32768 | tf_op jit(solution)/shard_map/all_to_all | solution.py:417
  118.9 0.8 shard_map.64
  (14 shorter events, 0.3 us)
Async XLA Ops:
  0.6 1.0 copy-start
  1.7 6.2 %collective-permute-start = (f32[2,2,7,8,128]{4,3,2,1,0:T(8,128)S(1)}, f32[2,2,7,8,128]{4,3,2,1,0:T(8,128)S(1)}, u32[]{:S(2)}, u32[]{:S(2)}) collective-permute-start(f32[2,2,7,8,128]{4,3,2,1,0:T(8,128)S(1)} %get-tuple-element.23), channel_id=1, source_target_pairs={{0,8},{8,16},{16,24},{24,32},{32,40},{40,48},{48,56},{56,64},{64,7... | collective-permute-start | bytes 344072 | tf_op jit(solution)/shard_map/ppermute | solution.py:422
  6.1 5.7 %collective-permute-start.1 = (f32[2,2,7,8,128]{4,3,2,1,0:T(8,128)S(1)}, f32[2,2,7,8,128]{4,3,2,1,0:T(8,128)S(1)}, u32[]{:S(2)}, u32[]{:S(2)}) collective-permute-start(f32[2,2,7,8,128]{4,3,2,1,0:T(8,128)S(1)} %get-tuple-element.25), channel_id=1, source_target_pairs={{8,0},{16,8},{24,16},{32,24},{40,32},{48,40},{56,48},{64,56},{72,6... | collective-permute-start | bytes 344072 | tf_op jit(solution)/shard_map/ppermute | solution.py:427
  11.9 6.2 %collective-permute-start.3 = (f32[2,22,8,128]{3,2,1,0:T(8,128)S(1)}, f32[2,22,8,128]{3,2,1,0:T(8,128)S(1)}, u32[]{:S(2)}, u32[]{:S(2)}) collective-permute-start(f32[2,22,8,128]{3,2,1,0:T(8,128)S(1)} %pad_maximum_fusion.a), channel_id=1, source_target_pairs={{0,7},{1,0},{2,1},{3,2},{4,3},{5,4},{6,5},{7,6},{8,15},{9,8},{10,9... | collective-permute-start | bytes 540680 | tf_op jit(solution)/shard_map/ppermute | solution.py:432
  16.6 2.5 %collective-permute-start.2 = (f32[2,22,8,128]{3,2,1,0:T(8,128)S(1)}, f32[2,22,8,128]{3,2,1,0:T(8,128)S(1)}, u32[]{:S(2)}, u32[]{:S(2)}) collective-permute-start(f32[2,22,8,128]{3,2,1,0:T(8,128)S(1)} %pad_maximum_fusion.1.b), channel_id=1, source_target_pairs={{0,1},{1,2},{2,3},{3,4},{4,5},{5,6},{6,7},{7,0},{8,9},{9,10},{10,1... | collective-permute-start | bytes 540680 | tf_op jit(solution)/shard_map/ppermute | solution.py:432
  20.5 34.2 %all-to-all-start = ((f32[64,8,128]{2,1,0:T(8,128)}), f32[64,8,128]{2,1,0:T(8,128)S(1)}, u32[]{:S(2)}, u32[]{:S(2)}) async-start(f32[64,8,128]{2,1,0:T(8,128)} %get-tuple-element.26), calls=%async_computation | async-start | bytes 524288 | tf_op jit(solution)/shard_map/all_to_all | solution.py:417
  37.8 6.0 %collective-permute-start.4 = (f32[2,2,8,256]{3,2,1,0:T(8,128)S(1)}, f32[2,2,8,256]{3,2,1,0:T(8,128)S(1)}, u32[]{:S(2)}, u32[]{:S(2)}) collective-permute-start(f32[2,2,8,256]{3,2,1,0:T(8,128)S(1)} %get-tuple-element.31), channel_id=1, source_target_pairs={{0,8},{8,16},{16,24},{24,32},{32,40},{40,48},{48,56},{56,64},{64,7... | collective-permute-start | bytes 98312 | tf_op jit(solution)/shard_map/ppermute | solution.py:422
  40.8 7.4 %collective-permute-start.5 = (f32[2,2,8,256]{3,2,1,0:T(8,128)S(1)}, f32[2,2,8,256]{3,2,1,0:T(8,128)S(1)}, u32[]{:S(2)}, u32[]{:S(2)}) collective-permute-start(f32[2,2,8,256]{3,2,1,0:T(8,128)S(1)} %get-tuple-element.32), channel_id=1, source_target_pairs={{8,0},{16,8},{24,16},{32,24},{40,32},{48,40},{56,48},{64,56},{72,6... | collective-permute-start | bytes 98312 | tf_op jit(solution)/shard_map/ppermute | solution.py:427
  56.8 7.4 %collective-permute-start.7 = (f32[8,128]{1,0:T(8,128)S(1)}, f32[8,128]{1,0:T(8,128)S(1)}, u32[]{:S(2)}, u32[]{:S(2)}) collective-permute-start(f32[8,128]{1,0:T(8,128)S(1)} %get-tuple-element.33.own), channel_id=1, source_target_pairs={{0,1},{1,2},{2,3},{3,4},{4,5},{5,6},{6,7},{7,0},{8,9},{9,10},{10,1... | collective-permute-start | bytes 12296 | tf_op jit(solution)/shard_map/ppermute | solution.py:432
  63.5 3.0 %collective-permute-start.6 = (f32[8,128]{1,0:T(8,128)S(1)}, f32[8,128]{1,0:T(8,128)S(1)}, u32[]{:S(2)}, u32[]{:S(2)}) collective-permute-start(f32[8,128]{1,0:T(8,128)S(1)} %get-tuple-element.33.own), channel_id=1, source_target_pairs={{0,7},{1,0},{2,1},{3,2},{4,3},{5,4},{6,5},{7,6},{8,15},{9,8},{10,9... | collective-permute-start | bytes 12296 | tf_op jit(solution)/shard_map/ppermute | solution.py:432
